TPU v7x, 32 devices: a whole 2x2x4 slice. The times are simulated.
32 devices in a mesh: row: 4 (over y, x), col: 8 (over z, core).
Axes of the slice: x: 2, y: 2, z: 4, core: 2. Of those that a mesh axis runs over, the one named last changes fastest.
Arguments:
- contacts: bfloat16 [256, 256, 256], P('row', 'col'), may hold values from -6 to 6
- w_first: bfloat16 [3, 3, 256, 256], replicated, may hold values from -0.1875 to 0.1875
- w_second: bfloat16 [3, 3, 256, 256], replicated, may hold values from -0.1875 to 0.1875
- w_third: bfloat16 [3, 3, 256, 256], replicated, may hold values from -0.1875 to 0.1875
Outputs:
- features: bfloat16 [256, 256, 256], P('row', 'col')
All inputs are finite; a program needn't handle non-finite values.
Results may differ from a plain program's by a relative error of at most 0.0064.
Values may be sent and summed in bfloat16 or wider, within the bound.
No kernel may reach another device: no remote copies, remote signals or barrier semaphores. Data moves between devices by JAX's collectives and lax.ppermute only.
A program may use at most 64 MiB of HBM per device.

v0:
```python
import jax
import jax.numpy as jnp
from jax import lax
from jax.sharding import PartitionSpec as P


def extended(array, sides, width):
    for axis, dim in sides:
        size, length = (lax.axis_size(axis), array.shape[dim])
        up = [(i, (i + 1) % size) for i in range(size - 1)]
        down = [(j, i) for i, j in up]
        last = lax.slice_in_dim(array, length - width, length, axis=dim)
        leading = lax.slice_in_dim(array, 0, width, axis=dim)
        before = lax.ppermute(last, axis, up)
        after = lax.ppermute(leading, axis, down)
        array = jnp.concatenate([before, array, after], axis=dim)
    return array


def conv_layer(activation, weight, dilation):
    tile_rows, tile_cols, channels = activation.shape
    padded = extended(activation, (("row", 0), ("col", 1)), dilation)
    windows = []
    for vertical in range(3):
        for lateral in range(3):
            windows.append(
                padded[
                    vertical * dilation : vertical * dilation + tile_rows,
                    lateral * dilation : lateral * dilation + tile_cols,
                    :,
                ]
            )
    stacked = jnp.concatenate(windows, axis=2).reshape(tile_rows * tile_cols, 9 * channels)
    product = jnp.dot(
        stacked, weight.reshape(9 * channels, weight.shape[3]), preferred_element_type=jnp.float32
    )
    return (
        jnp.maximum(product, 0.0)
        .astype(jnp.bfloat16)
        .reshape(tile_rows, tile_cols, weight.shape[3])
    )


def transposed(activation):
    tile_rows, tile_cols, channels = activation.shape
    col_count = lax.axis_size("col")
    row_count = lax.axis_size("row")
    col_per_row = col_count // row_count
    flat_width = tile_cols * tile_cols // row_count
    pieces = activation.reshape(col_per_row, row_count, flat_width, channels)
    pieces = lax.all_to_all(pieces, "row", split_axis=1, concat_axis=0, tiled=True)
    pieces = pieces.reshape(col_count, flat_width, channels)
    pieces = lax.all_to_all(pieces, "col", split_axis=0, concat_axis=0, tiled=True)
    pieces = lax.all_to_all(pieces, "row", split_axis=0, concat_axis=1, tiled=True)
    pieces = pieces.reshape(col_per_row, tile_cols, tile_cols, channels)
    return jnp.transpose(pieces, (0, 2, 1, 3)).reshape(tile_rows, tile_cols, channels)


def symmetrize(activation):
    mirrored = transposed(activation)
    return ((activation.astype(jnp.float32) + mirrored.astype(jnp.float32)) * 0.5).astype(
        jnp.bfloat16
    )


def local(contacts, w_first, w_second, w_third):
    first = conv_layer(contacts, w_first, 1)
    second = conv_layer(symmetrize(first), w_second, 2)
    return conv_layer(symmetrize(second), w_third, 4)


def solution(mesh):
    return jax.shard_map(
        local,
        mesh=mesh,
        in_specs=(P("row", "col", None), P(), P(), P()),
        out_specs=P("row", "col", None),
        check_vma=False,
    )
```

profile of v0, /device:TPU:5, one launch (start us, length us, event | category | flops | bytes accessed | tf_op | source)
XLA Modules:
  0.0 199.0 jit_solution(9135480635380153104)
XLA Ops:
  0.0 0.8 fusion.26
  0.8 3.1 %collective-permute-start = (bf16[1,32,256]{2,1,0:T(8,128)(2,1)S(1)}, bf16[1,32,256]{2,1,0:T(8,128)(2,1)S(1)}, u32[]{:S(2)}, u32[]{:S(2)}) collective-permute-start(bf16[1,32,256]{2,1,0:T(8,128)(2,1)S(1)} %get-tuple-element.20), channel_id=1, source_target_pairs={{0,8},{8,16},{16,24},{1,9},{9,17},{17,25},{2,10},{10,18},{18,26},{... | collective-permute-start | bytes 49160 | tf_op jit(solution)/shard_map/ppermute | solution.py:14
  4.0 3.1 %collective-permute-start.1 = (bf16[1,32,256]{2,1,0:T(8,128)(2,1)S(1)}, bf16[1,32,256]{2,1,0:T(8,128)(2,1)S(1)}, u32[]{:S(2)}, u32[]{:S(2)}) collective-permute-start(bf16[1,32,256]{2,1,0:T(8,128)(2,1)S(1)} %get-tuple-element.19), channel_id=1, source_target_pairs={{8,0},{16,8},{24,16},{9,1},{17,9},{25,17},{10,2},{18,10},{26,18},{... | collective-permute-start | bytes 49160 | tf_op jit(solution)/shard_map/ppermute | solution.py:15
  7.1 1.4 constant_dynamic-update-slice_fusion.1
  8.6 5.2 %collective-permute-start.2 = (bf16[66,1,256]{2,1,0:T(2,128)(2,1)S(1)}, bf16[66,1,256]{2,1,0:T(2,128)(2,1)S(1)}, u32[]{:S(2)}, u32[]{:S(2)}) collective-permute-start(bf16[66,1,256]{2,1,0:T(2,128)(2,1)S(1)} %get-tuple-element.14), channel_id=1, source_target_pairs={{0,1},{1,2},{2,3},{3,4},{4,5},{5,6},{6,7},{8,9},{9,10},{10,11},{11... | collective-permute-start | bytes 101384 | tf_op jit(solution)/shard_map/ppermute | solution.py:14
  13.8 1.9 collective-permute-start.3
  16.2 3.2 %collective-permute-done.3 = bf16[66,1,256]{2,1,0:T(2,128)(2,1)S(1)} collective-permute-done((bf16[66,1,256]{2,1,0:T(2,128)(2,1)S(1)}, bf16[66,1,256]{2,1,0:T(2,128)(2,1)S(1)}, u32[]{:S(2)}, u32[]{:S(2)}) %collective-permute-start.3) | collective-permute-done | bytes 33824 | tf_op jit(solution)/shard_map/ppermute | solution.py:15
  22.4 2.6 %fusion = bf16[2048,256]{1,0:T(8,128)(2,1)S(1)} fusion(bf16[2048,2304]{1,0:T(8,128)(2,1)S(1)} %bitcast.58, bf16[2304,256]{1,0:T(8,128)(2,1)S(1)} %bitcast.47), kind=kOutput, calls=%fused_computation.3 | convolution fusion | flops 2416967680 | bytes 11665408 | tf_op jit(solution)/shard_map/dot_general | solution.py:34
  25.1 15.3 %all_to_all.64 = bf16[2,4,256,256]{3,2,0,1:T(8,128)(2,1)S(1)} all-to-all(bf16[2,4,256,256]{3,2,0,1:T(8,128)(2,1)S(1)} %copy.9), channel_id=1, replica_groups=mesh['row'=4,'col'=8] {'row'}, dimensions={1} | all-to-all | bytes 2097152 | tf_op jit(solution)/shard_map/all_to_all | solution.py:51
  40.4 30.7 %all_to_all.65 = bf16[8,256,256]{2,1,0:T(8,128)(2,1)S(1)} all-to-all(bf16[8,256,256]{2,1,0:T(8,128)(2,1)S(1)} %bitcast.52), channel_id=1, replica_groups=mesh['row'=4,'col'=8] {'col'}, dimensions={0} | all-to-all | bytes 2097152 | tf_op jit(solution)/shard_map/all_to_all | solution.py:53
  71.1 15.4 %all_to_all.66 = bf16[8,256,256]{2,1,0:T(8,128)(2,1)S(1)} all-to-all(bf16[8,256,256]{2,1,0:T(8,128)(2,1)S(1)} %all_to_all.65), channel_id=1, replica_groups=mesh['row'=4,'col'=8] {'row'}, dimensions={0} | all-to-all | bytes 2097152 | tf_op jit(solution)/shard_map/all_to_all | solution.py:54
  86.7 1.2 copy.11
  88.4 2.1 %collective-permute-start.4 = (bf16[2,32,256]{2,1,0:T(8,128)(2,1)S(1)}, bf16[2,32,256]{2,1,0:T(8,128)(2,1)S(1)}, u32[]{:S(2)}, u32[]{:S(2)}) collective-permute-start(bf16[2,32,256]{2,1,0:T(8,128)(2,1)S(1)} %get-tuple-element.17), channel_id=1, source_target_pairs={{0,8},{8,16},{16,24},{1,9},{9,17},{17,25},{2,10},{10,18},{18,26},{... | collective-permute-start | bytes 98312 | tf_op jit(solution)/shard_map/ppermute | solution.py:14
  90.5 4.1 %collective-permute-start.5 = (bf16[2,32,256]{2,1,0:T(8,128)(2,1)S(1)}, bf16[2,32,256]{2,1,0:T(8,128)(2,1)S(1)}, u32[]{:S(2)}, u32[]{:S(2)}) collective-permute-start(bf16[2,32,256]{2,1,0:T(8,128)(2,1)S(1)} %get-tuple-element.18), channel_id=1, source_target_pairs={{8,0},{16,8},{24,16},{9,1},{17,9},{25,17},{10,2},{18,10},{26,18},{... | collective-permute-start | bytes 98312 | tf_op jit(solution)/shard_map/ppermute | solution.py:15
  94.6 1.0 collective-permute-done.5
  95.7 5.0 %collective-permute-start.7 = (bf16[68,2,256]{2,1,0:T(2,128)(2,1)S(1)}, bf16[68,2,256]{2,1,0:T(2,128)(2,1)S(1)}, u32[]{:S(2)}, u32[]{:S(2)}) collective-permute-start(bf16[68,2,256]{2,1,0:T(2,128)(2,1)S(1)} %get-tuple-element.11), channel_id=1, source_target_pairs={{1,0},{2,1},{3,2},{4,3},{5,4},{6,5},{7,6},{9,8},{10,9},{11,10},{12... | collective-permute-start | bytes 208904 | tf_op jit(solution)/shard_map/ppermute | solution.py:15
  100.7 2.1 %collective-permute-start.6 = (bf16[68,2,256]{2,1,0:T(2,128)(2,1)S(1)}, bf16[68,2,256]{2,1,0:T(2,128)(2,1)S(1)}, u32[]{:S(2)}, u32[]{:S(2)}) collective-permute-start(bf16[68,2,256]{2,1,0:T(2,128)(2,1)S(1)} %get-tuple-element.12), channel_id=1, source_target_pairs={{0,1},{1,2},{2,3},{3,4},{4,5},{5,6},{6,7},{8,9},{9,10},{10,11},{11... | collective-permute-start | bytes 208904 | tf_op jit(solution)/shard_map/ppermute | solution.py:14
  102.8 1.2 collective-permute-done.6
  104.0 0.9 pad_maximum_fusion.1
  107.7 2.6 %fusion.1 = bf16[2048,256]{1,0:T(8,128)(2,1)S(1)} fusion(bf16[2048,2304]{1,0:T(8,128)(2,1)S(1)} %bitcast.59, bf16[2304,256]{1,0:T(8,128)(2,1)S(1)} %bitcast.61), kind=kOutput, calls=%fused_computation.4 | convolution fusion | flops 2416967680 | bytes 11665408 | tf_op jit(solution)/shard_map/dot_general | solution.py:34
  110.4 17.4 %all_to_all.67 = bf16[2,4,256,256]{3,2,0,1:T(8,128)(2,1)S(1)} all-to-all(bf16[2,4,256,256]{3,2,0,1:T(8,128)(2,1)S(1)} %copy.12), channel_id=1, replica_groups=mesh['row'=4,'col'=8] {'row'}, dimensions={1} | all-to-all | bytes 2097152 | tf_op jit(solution)/shard_map/all_to_all | solution.py:51
  127.8 29.8 %all_to_all.68 = bf16[8,256,256]{2,1,0:T(8,128)(2,1)S(1)} all-to-all(bf16[8,256,256]{2,1,0:T(8,128)(2,1)S(1)} %bitcast.53), channel_id=1, replica_groups=mesh['row'=4,'col'=8] {'col'}, dimensions={0} | all-to-all | bytes 2097152 | tf_op jit(solution)/shard_map/all_to_all | solution.py:53
  157.6 15.5 %all_to_all.69 = bf16[8,256,256]{2,1,0:T(8,128)(2,1)S(1)} all-to-all(bf16[8,256,256]{2,1,0:T(8,128)(2,1)S(1)} %all_to_all.68), channel_id=1, replica_groups=mesh['row'=4,'col'=8] {'row'}, dimensions={0} | all-to-all | bytes 2097152 | tf_op jit(solution)/shard_map/all_to_all | solution.py:54
  173.3 1.2 copy.14
  175.0 2.1 %collective-permute-start.8 = (bf16[4,32,256]{2,1,0:T(8,128)(2,1)S(1)}, bf16[4,32,256]{2,1,0:T(8,128)(2,1)S(1)}, u32[]{:S(2)}, u32[]{:S(2)}) collective-permute-start(bf16[4,32,256]{2,1,0:T(8,128)(2,1)S(1)} %get-tuple-element.15), channel_id=1, source_target_pairs={{0,8},{8,16},{16,24},{1,9},{9,17},{17,25},{2,10},{10,18},{18,26},{... | collective-permute-start | bytes 196616 | tf_op jit(solution)/shard_map/ppermute | solution.py:14
  177.1 4.1 %collective-permute-start.9 = (bf16[4,32,256]{2,1,0:T(8,128)(2,1)S(1)}, bf16[4,32,256]{2,1,0:T(8,128)(2,1)S(1)}, u32[]{:S(2)}, u32[]{:S(2)}) collective-permute-start(bf16[4,32,256]{2,1,0:T(8,128)(2,1)S(1)} %get-tuple-element.16), channel_id=1, source_target_pairs={{8,0},{16,8},{24,16},{9,1},{17,9},{25,17},{10,2},{18,10},{26,18},{... | collective-permute-start | bytes 196616 | tf_op jit(solution)/shard_map/ppermute | solution.py:15
  181.2 1.3 collective-permute-done.9
  182.6 5.0 %collective-permute-start.11 = (bf16[72,4,256]{2,1,0:T(4,128)(2,1)S(1)}, bf16[72,4,256]{2,1,0:T(4,128)(2,1)S(1)}, u32[]{:S(2)}, u32[]{:S(2)}) collective-permute-start(bf16[72,4,256]{2,1,0:T(4,128)(2,1)S(1)} %get-tuple-element.7), channel_id=1, source_target_pairs={{1,0},{2,1},{3,2},{4,3},{5,4},{6,5},{7,6},{9,8},{10,9},{11,10},{12... | collective-permute-start | bytes 442376 | tf_op jit(solution)/shard_map/ppermute | solution.py:15
  187.6 2.1 %collective-permute-start.10 = (bf16[72,4,256]{2,1,0:T(4,128)(2,1)S(1)}, bf16[72,4,256]{2,1,0:T(4,128)(2,1)S(1)}, u32[]{:S(2)}, u32[]{:S(2)}) collective-permute-start(bf16[72,4,256]{2,1,0:T(4,128)(2,1)S(1)} %get-tuple-element.8), channel_id=1, source_target_pairs={{0,1},{1,2},{2,3},{3,4},{4,5},{5,6},{6,7},{8,9},{9,10},{10,11},{11... | collective-permute-start | bytes 442376 | tf_op jit(solution)/shard_map/ppermute | solution.py:14
  189.8 1.8 collective-permute-done.10
  191.7 1.0 pad_maximum_fusion
  195.4 3.6 %fusion.2 = bf16[2048,256]{1,0:T(8,128)(2,1)} fusion(bf16[2048,2304]{1,0:T(8,128)(2,1)S(1)} %bitcast.60, bf16[2304,256]{1,0:T(8,128)(2,1)S(1)} %bitcast.62), kind=kOutput, calls=%fused_computation.5 | convolution fusion | flops 2416967680 | bytes 11665408 | tf_op jit(solution)/shard_map/dot_general | solution.py:34
  (55 shorter events, 10.7 us)
Async XLA Ops:
  0.0 22.4 %copy-start = (bf16[3,3,256,256]{3,2,1,0:T(8,128)(2,1)S(1)}, bf16[3,3,256,256]{3,2,1,0:T(8,128)(2,1)}, u32[]{:S(2)}) copy-start(bf16[3,3,256,256]{3,2,1,0:T(8,128)(2,1)} %param.5) | copy-start | bytes 3538948
  0.8 6.2 %collective-permute-start = (bf16[1,32,256]{2,1,0:T(8,128)(2,1)S(1)}, bf16[1,32,256]{2,1,0:T(8,128)(2,1)S(1)}, u32[]{:S(2)}, u32[]{:S(2)}) collective-permute-start(bf16[1,32,256]{2,1,0:T(8,128)(2,1)S(1)} %get-tuple-element.20), channel_id=1, source_target_pairs={{0,8},{8,16},{16,24},{1,9},{9,17},{17,25},{2,10},{10,18},{18,26},{... | collective-permute-start | bytes 49160 | tf_op jit(solution)/shard_map/ppermute | solution.py:14
  4.0 4.5 %collective-permute-start.1 = (bf16[1,32,256]{2,1,0:T(8,128)(2,1)S(1)}, bf16[1,32,256]{2,1,0:T(8,128)(2,1)S(1)}, u32[]{:S(2)}, u32[]{:S(2)}) collective-permute-start(bf16[1,32,256]{2,1,0:T(8,128)(2,1)S(1)} %get-tuple-element.19), channel_id=1, source_target_pairs={{8,0},{16,8},{24,16},{9,1},{17,9},{25,17},{10,2},{18,10},{26,18},{... | collective-permute-start | bytes 49160 | tf_op jit(solution)/shard_map/ppermute | solution.py:15
  7.0 9.0 %copy-start.1 = (bf16[64,32,256]{2,1,0:T(8,128)(2,1)S(1)}, bf16[64,32,256]{2,1,0:T(8,128)(2,1)}, u32[]{:S(2)}) copy-start(bf16[64,32,256]{2,1,0:T(8,128)(2,1)} %param.4) | copy-start | bytes 3145732
  8.6 7.1 %collective-permute-start.2 = (bf16[66,1,256]{2,1,0:T(2,128)(2,1)S(1)}, bf16[66,1,256]{2,1,0:T(2,128)(2,1)S(1)}, u32[]{:S(2)}, u32[]{:S(2)}) collective-permute-start(bf16[66,1,256]{2,1,0:T(2,128)(2,1)S(1)} %get-tuple-element.14), channel_id=1, source_target_pairs={{0,1},{1,2},{2,3},{3,4},{4,5},{5,6},{6,7},{8,9},{9,10},{10,11},{11... | collective-permute-start | bytes 101384 | tf_op jit(solution)/shard_map/ppermute | solution.py:14
  13.8 5.6 %collective-permute-start.3 = (bf16[66,1,256]{2,1,0:T(2,128)(2,1)S(1)}, bf16[66,1,256]{2,1,0:T(2,128)(2,1)S(1)}, u32[]{:S(2)}, u32[]{:S(2)}) collective-permute-start(bf16[66,1,256]{2,1,0:T(2,128)(2,1)S(1)} %get-tuple-element.13), channel_id=1, source_target_pairs={{1,0},{2,1},{3,2},{4,3},{5,4},{6,5},{7,6},{9,8},{10,9},{11,10},{12... | collective-permute-start | bytes 101384 | tf_op jit(solution)/shard_map/ppermute | solution.py:15
  88.4 6.2 %collective-permute-start.4 = (bf16[2,32,256]{2,1,0:T(8,128)(2,1)S(1)}, bf16[2,32,256]{2,1,0:T(8,128)(2,1)S(1)}, u32[]{:S(2)}, u32[]{:S(2)}) collective-permute-start(bf16[2,32,256]{2,1,0:T(8,128)(2,1)S(1)} %get-tuple-element.17), channel_id=1, source_target_pairs={{0,8},{8,16},{16,24},{1,9},{9,17},{17,25},{2,10},{10,18},{18,26},{... | collective-permute-start | bytes 98312 | tf_op jit(solution)/shard_map/ppermute | solution.py:14
  90.5 5.1 %collective-permute-start.5 = (bf16[2,32,256]{2,1,0:T(8,128)(2,1)S(1)}, bf16[2,32,256]{2,1,0:T(8,128)(2,1)S(1)}, u32[]{:S(2)}, u32[]{:S(2)}) collective-permute-start(bf16[2,32,256]{2,1,0:T(8,128)(2,1)S(1)} %get-tuple-element.18), channel_id=1, source_target_pairs={{8,0},{16,8},{24,16},{9,1},{17,9},{25,17},{10,2},{18,10},{26,18},{... | collective-permute-start | bytes 98312 | tf_op jit(solution)/shard_map/ppermute | solution.py:15
  95.7 7.1 %collective-permute-start.7 = (bf16[68,2,256]{2,1,0:T(2,128)(2,1)S(1)}, bf16[68,2,256]{2,1,0:T(2,128)(2,1)S(1)}, u32[]{:S(2)}, u32[]{:S(2)}) collective-permute-start(bf16[68,2,256]{2,1,0:T(2,128)(2,1)S(1)} %get-tuple-element.11), channel_id=1, source_target_pairs={{1,0},{2,1},{3,2},{4,3},{5,4},{6,5},{7,6},{9,8},{10,9},{11,10},{12... | collective-permute-start | bytes 208904 | tf_op jit(solution)/shard_map/ppermute | solution.py:15
  100.7 3.3 %collective-permute-start.6 = (bf16[68,2,256]{2,1,0:T(2,128)(2,1)S(1)}, bf16[68,2,256]{2,1,0:T(2,128)(2,1)S(1)}, u32[]{:S(2)}, u32[]{:S(2)}) collective-permute-start(bf16[68,2,256]{2,1,0:T(2,128)(2,1)S(1)} %get-tuple-element.12), channel_id=1, source_target_pairs={{0,1},{1,2},{2,3},{3,4},{4,5},{5,6},{6,7},{8,9},{9,10},{10,11},{11... | collective-permute-start | bytes 208904 | tf_op jit(solution)/shard_map/ppermute | solution.py:14
  106.4 1.3 copy-start.2
  175.0 6.2 %collective-permute-start.8 = (bf16[4,32,256]{2,1,0:T(8,128)(2,1)S(1)}, bf16[4,32,256]{2,1,0:T(8,128)(2,1)S(1)}, u32[]{:S(2)}, u32[]{:S(2)}) collective-permute-start(bf16[4,32,256]{2,1,0:T(8,128)(2,1)S(1)} %get-tuple-element.15), channel_id=1, source_target_pairs={{0,8},{8,16},{16,24},{1,9},{9,17},{17,25},{2,10},{10,18},{18,26},{... | collective-permute-start | bytes 196616 | tf_op jit(solution)/shard_map/ppermute | solution.py:14
  177.1 5.4 %collective-permute-start.9 = (bf16[4,32,256]{2,1,0:T(8,128)(2,1)S(1)}, bf16[4,32,256]{2,1,0:T(8,128)(2,1)S(1)}, u32[]{:S(2)}, u32[]{:S(2)}) collective-permute-start(bf16[4,32,256]{2,1,0:T(8,128)(2,1)S(1)} %get-tuple-element.16), channel_id=1, source_target_pairs={{8,0},{16,8},{24,16},{9,1},{17,9},{25,17},{10,2},{18,10},{26,18},{... | collective-permute-start | bytes 196616 | tf_op jit(solution)/shard_map/ppermute | solution.py:15
  182.6 7.2 %collective-permute-start.11 = (bf16[72,4,256]{2,1,0:T(4,128)(2,1)S(1)}, bf16[72,4,256]{2,1,0:T(4,128)(2,1)S(1)}, u32[]{:S(2)}, u32[]{:S(2)}) collective-permute-start(bf16[72,4,256]{2,1,0:T(4,128)(2,1)S(1)} %get-tuple-element.7), channel_id=1, source_target_pairs={{1,0},{2,1},{3,2},{4,3},{5,4},{6,5},{7,6},{9,8},{10,9},{11,10},{12... | collective-permute-start | bytes 442376 | tf_op jit(solution)/shard_map/ppermute | solution.py:15
  187.6 4.0 %collective-permute-start.10 = (bf16[72,4,256]{2,1,0:T(4,128)(2,1)S(1)}, bf16[72,4,256]{2,1,0:T(4,128)(2,1)S(1)}, u32[]{:S(2)}, u32[]{:S(2)}) collective-permute-start(bf16[72,4,256]{2,1,0:T(4,128)(2,1)S(1)} %get-tuple-element.8), channel_id=1, source_target_pairs={{0,1},{1,2},{2,3},{3,4},{4,5},{5,6},{6,7},{8,9},{9,10},{10,11},{11... | collective-permute-start | bytes 442376 | tf_op jit(solution)/shard_map/ppermute | solution.py:14
  194.1 1.3 copy-start.3
where the time goes:
time: 202 us; the launch traced here: 199 us
  blocking collectives  124 us (61%)
  starting transfers between devices  39.9 us (20%)
  local copies, waits for them, and re-layouts  10.5 us (5%)
  matrix products  8.84 us (4%)
  waiting for transfers between devices  8.5 us (4%)
  other arithmetic  6.7 us (3%)
    all_to_all x2, blocking collectives, transposed(): lax.all_to_all(pieces, 'col', split_axis=0, concat_axis=0, tiled=True)  60.5 us
    all_to_all x2, blocking collectives, transposed(): lax.all_to_all(pieces, 'row', split_axis=1, concat_axis=0, tiled=True)  32.7 us
    all_to_all x2, blocking collectives, transposed(): lax.all_to_all(pieces, 'row', split_axis=0, concat_axis=1, tiled=True)  30.9 us
    ppermute x6, starting transfers between devices, extended(): after = lax.ppermute(leading, axis, down)  23.1 us
    ppermute x6, starting transfers between devices, extended(): before = lax.ppermute(last, axis, up)  16.8 us
    dot_general x3, matrix products, conv_layer(): jnp.dot(stacked, weight.reshape(9 * channels, weight.shape[3]), preferred...  8.84 us
    unnamed x23, local copies, waits for them, and re-layouts  5.68 us
    ppermute x6, waiting for transfers between devices, extended(): after = lax.ppermute(leading, axis, down)  5.48 us
  transfers between devices with their start and end apart: 12, of which 5 were waited for; matrix products, arithmetic and copies ran while one was open for 1% of the time, Pallas kernels for 0%

commit v1 on v0

v1 whole, which is shorter than its diff:
```python
import math

import jax
import jax.numpy as jnp
import numpy as np
from jax import lax
from jax.sharding import PartitionSpec as P

AXES = ("row", "col")


def paired(length):
    near = [(i, i + 1) for i in range(0, length - 1, 2)]
    far = [(i, i + 1) for i in range(1, length - 1, 2)]
    return [pairs + [(j, i) for i, j in pairs] for pairs in (near, far)]


def extended(array, axis, dim, width):
    size, length = lax.axis_size(axis), array.shape[dim]
    odd = lax.axis_index(axis) % 2
    near, far = paired(size)
    low = jnp.where(odd == 1, 0, length - width)
    to_near = lax.dynamic_slice_in_dim(array, low, width, axis=dim)
    to_far = lax.dynamic_slice_in_dim(array, length - width - low, width, axis=dim)
    from_far = lax.ppermute(to_far, axis, far) if far else jnp.zeros_like(to_far)
    from_near = lax.ppermute(to_near, axis, near)
    before = jnp.where(odd == 1, from_near, from_far)
    after = jnp.where(odd == 1, from_far, from_near)
    return jnp.concatenate([before, array, after], axis=dim)


def patches(padded, dilation):
    rows, cols, channels = padded.shape
    rows, cols = rows - 2 * dilation, cols - 2 * dilation
    windows = [
        padded[p * dilation : p * dilation + rows, q * dilation : q * dilation + cols, :]
        for p in range(3)
        for q in range(3)
    ]
    return jnp.concatenate(windows, axis=2).reshape(rows * cols, 9 * channels)


def convolved(stacked, weight):
    product = jnp.dot(
        stacked, weight.reshape(stacked.shape[1], weight.shape[3]), preferred_element_type=jnp.float32
    )
    return jnp.maximum(product, 0.0)


def routes(row_count):
    low = math.isqrt(row_count)
    first, second = {}, {}
    for r in range(row_count):
        for z in range(row_count):
            a, b, c, d = r // low, r % low, z // low, z % low
            if r == z:
                continue
            via = (r, z) if b == d else ((z, z) if a == c else (c * low + b, z))
            if via != (r, z):
                first[(r, z)] = via
            second.setdefault(via, []).append((z, r))
    if any(len(ends) > 1 for ends in second.values()) or len(set(first.values())) < len(first):
        pairs = [(r, z) for r in range(row_count) for z in range(row_count) if r != z]
        return {}, {(r, z): (z, r) for r, z in pairs}
    return first, {via: ends[0] for via, ends in second.items()}


def transposed(activation, parts):
    tile_rows, tile_cols, channels = activation.shape
    row_count, col_count = lax.axis_size("row"), lax.axis_size("col")
    ratio = col_count // row_count
    first, second = routes(row_count)
    row, col = lax.axis_index("row"), lax.axis_index("col")
    own = col % ratio

    def device(chip, core):
        return chip[0] * col_count + chip[1] * ratio + core

    def pairs(legs, shift):
        return [
            (device(s, k), device(e, (k + shift) % ratio)) for s, e in legs.items() for k in range(ratio)
        ]

    relay = np.zeros((row_count, row_count), bool)
    for via in first.values():
        relay[via] = True
    is_relay = jnp.asarray(relay)[row, col // ratio]
    diagonal = row == col // ratio
    stay = {(i, i): (i, i) for i in range(row_count)}
    step = tile_cols // parts
    blocks = []
    for shift in range(ratio):
        half = lax.dynamic_slice_in_dim(activation, (own + shift) % ratio * tile_cols, tile_cols, 0)
        got = []
        for part in range(parts):
            piece = half[part * step : part * step + step]
            sent = piece
            if first:
                hop = lax.ppermute(piece, AXES, pairs(first, 0))
                sent = jnp.where(is_relay, hop, piece)
            got.append(lax.ppermute(sent, AXES, pairs(second, shift)))
        kept = lax.ppermute(half, AXES, pairs(stay, shift)) if shift else half
        block = jnp.where(diagonal, kept, jnp.concatenate(got, axis=0))
        blocks.append(jnp.transpose(block, (1, 0, 2)))
    ordered = blocks[0]
    mirrored = jnp.concatenate(blocks, axis=0)
    stacked = mirrored.reshape(ratio, tile_cols, tile_cols, channels)
    places = [lax.dynamic_index_in_dim(stacked, (own - j) % ratio, 0, False) for j in range(ratio)]
    return jnp.concatenate(places, axis=0)


def inside(rows, cols, margin):
    row, col = lax.axis_index("row"), lax.axis_index("col")
    tile_rows, tile_cols = rows - 2 * margin, cols - 2 * margin
    y = row * tile_rows - margin + lax.broadcasted_iota(jnp.int32, (rows, cols, 1), 0)
    x = col * tile_cols - margin + lax.broadcasted_iota(jnp.int32, (rows, cols, 1), 1)
    total = lax.axis_size("row") * tile_rows
    return (y >= 0) & (y < total) & (x >= 0) & (x < total)


def local(contacts, w_first, w_second, w_third):
    tile_rows, tile_cols, channels = contacts.shape
    padded = extended(extended(contacts, "col", 1, 1), "row", 0, 1)
    first = convolved(patches(padded, 1), w_first).astype(jnp.bfloat16)
    first = first.reshape(tile_rows, tile_cols, channels)
    mirrored = transposed(first, 2)
    sym = ((first.astype(jnp.float32) + mirrored.astype(jnp.float32)) * 0.5).astype(jnp.bfloat16)
    padded = extended(extended(sym, "col", 1, 6), "row", 0, 6)
    stacked = patches(padded, 2)
    second = convolved(stacked, w_second).astype(jnp.bfloat16).astype(jnp.float32)
    flipped = convolved(stacked, jnp.swapaxes(w_second, 0, 1)).astype(jnp.bfloat16).astype(jnp.float32)
    sym = ((second + flipped) * 0.5).astype(jnp.bfloat16)
    rows, cols = tile_rows + 8, tile_cols + 8
    sym = jnp.where(inside(rows, cols, 4), sym.reshape(rows, cols, channels), 0)
    features = convolved(patches(sym, 4), w_third).astype(jnp.bfloat16)
    return features.reshape(tile_rows, tile_cols, channels)


def solution(mesh):
    return jax.shard_map(
        local,
        mesh=mesh,
        in_specs=(P("row", "col", None), P(), P(), P()),
        out_specs=P("row", "col", None),
        check_vma=False,
    )
```

time: 202 us -> 113 us (0.56); the launches traced: 199 us -> 112 us
  blocking collectives: 124 us -> 0 us
  waiting for transfers between devices: 8.5 us -> 26.8 us
  other arithmetic: 6.7 us -> 14.1 us
  matrix products: 8.84 us -> 14.2 us
  local copies, waits for them, and re-layouts: 10.5 us -> 14.9 us
    all_to_all x6 -> x0, blocking collectives: 124 us -> none  [the longest x2 60.5 us: transposed(): lax.all_to_all(pieces, 'col', split_axis=0, concat_axis=0, tiled=True)]
    ppermute x12 -> x17, waiting for transfers between devices: 8.5 us -> 26.8 us  [the longest x4 14.4 us: extended(): lax.ppermute(to_far, axis, far)]
    dot_general x3 -> x4, matrix products: 8.84 us -> 14.2 us  [convolved(): jnp.dot(stacked, weight.reshape(stacked.shape[1], weight.shape[3]), prefe...]
    select_n x0 -> x9, other arithmetic: none -> 5.03 us  [the longest x4 4.25 us: transposed(): sent = jnp.where(is_relay, hop, piece)]
    unnamed x23 -> x35, local copies, waits for them, and re-layouts: 5.68 us -> 10.6 us
    concatenate x5, other arithmetic: 2.71 us -> 5.57 us  [the longest x4 5.49 us: extended(): return jnp.concatenate([before, array, after], axis=dim)]
    convert_element_type x4 -> x0, local copies, waits for them, and re-layouts: 2.81 us -> none  [symmetrize(): mirrored.astype(jnp.float32)]
    dynamic_slice x0 -> x6, local copies, waits for them, and re-layouts: none -> 2.28 us  [the longest x3 1.53 us: extended(): to_near = lax.dynamic_slice_in_dim(array, low, width, axis=dim)]
  transfers between devices with their start and end apart: 12 -> 17, of which waited for: 5 -> 9; matrix products, arithmetic and copies ran while one was open for 1% -> 8% of each run, Pallas kernels for 0% -> 0%
where the time goes in v1:
time: 113 us; the launch traced here: 112 us
  starting transfers between devices  41.8 us (37%)
  waiting for transfers between devices  26.8 us (24%)
  local copies, waits for them, and re-layouts  14.9 us (13%)
  matrix products  14.2 us (13%)
  other arithmetic  14.1 us (12%)
    ppermute x4, starting transfers between devices, extended(): lax.ppermute(to_far, axis, far)  16.5 us
    ppermute x4, waiting for transfers between devices, extended(): lax.ppermute(to_far, axis, far)  14.4 us
    ppermute x4, starting transfers between devices, transposed(): got.append(lax.ppermute(sent, AXES, pairs(second, shift)))  14.4 us
    dot_general x4, matrix products, convolved(): jnp.dot(stacked, weight.reshape(stacked.shape[1], weight.shape[3]), prefe...  14.2 us
    ppermute x4, waiting for transfers between devices, transposed(): got.append(lax.ppermute(sent, AXES, pairs(second, shift)))  12 us
    unnamed x35, local copies, waits for them, and re-layouts  10.6 us
    concatenate x4, other arithmetic, extended(): return jnp.concatenate([before, array, after], axis=dim)  5.49 us
    ppermute x4, starting transfers between devices, extended(): from_near = lax.ppermute(to_near, axis, near)  5.37 us
  transfers between devices with their start and end apart: 17, of which 9 were waited for; matrix products, arithmetic and copies ran while one was open for 8% of the time, Pallas kernels for 0%

profile of v1, /device:TPU:5, one launch (start us, length us, event | category | flops | bytes accessed | tf_op | source)
XLA Modules:
  0.0 112.5 jit_solution(16681873204810264491)
XLA Ops:
  0.0 1.3 %constant_dynamic-slice_fusion.14 = (bf16[64,1,256]{2,1,0:T(2,128)(2,1)S(1)}, bf16[64,1,256]{2,1,0:T(2,128)(2,1)S(1)}) fusion(bf16[64,32,256]{2,1,0:T(8,128)(2,1)} %param.5, s32[]{:T(128)S(6)} %select_n.174, s32[]{:T(128)S(6)} %select_n.175), kind=kLoop, calls=%fused_computation.83 | loop fusion | bytes 131080 | tf_op jit(solution)/shard_map/dynamic_slice | solution.py:23
  2.1 3.1 %collective-permute-start.1 = (bf16[64,1,256]{2,1,0:T(2,128)(2,1)S(1)}, bf16[64,1,256]{2,1,0:T(2,128)(2,1)S(1)}, u32[]{:S(2)}, u32[]{:S(2)}) collective-permute-start(bf16[64,1,256]{2,1,0:T(2,128)(2,1)S(1)} %get-tuple-element.22), channel_id=1, source_target_pairs={{1,2},{3,4},{5,6},{2,1},{4,3},{6,5},{9,10},{11,12},{13,14},{10,9},... | collective-permute-start | bytes 98312 | tf_op jit(solution)/shard_map/ppermute | solution.py:25
  5.2 2.4 %collective-permute-done.1 = bf16[64,1,256]{2,1,0:T(2,128)(2,1)S(1)} collective-permute-done((bf16[64,1,256]{2,1,0:T(2,128)(2,1)S(1)}, bf16[64,1,256]{2,1,0:T(2,128)(2,1)S(1)}, u32[]{:S(2)}, u32[]{:S(2)}) %collective-permute-start.1) | collective-permute-done | bytes 32800 | tf_op jit(solution)/shard_map/ppermute | solution.py:25
  7.8 2.0 %pad_maximum_fusion.3 = bf16[64,34,256]{2,1,0:T(8,128)(2,1)S(1)} fusion(bf16[64,1,256]{2,1,0:T(2,128)(2,1)S(1)} %get-tuple-element.28, bf16[64,32,256]{2,1,0:T(8,128)(2,1)} %param.5, bf16[64,1,256]{2,1,0:T(2,128)(2,1)S(1)} %get-tuple-element.27), kind=kLoop, calls=%fused_computation.28 | loop fusion | flops 3342336 | bytes 2228224 | tf_op jit(solution)/shard_map/concatenate | solution.py:29
  9.8 1.3 %collective-permute-start.2 = (bf16[1,34,256]{2,1,0:T(8,128)(2,1)S(1)}, bf16[1,34,256]{2,1,0:T(8,128)(2,1)S(1)}, u32[]{:S(2)}, u32[]{:S(2)}) collective-permute-start(bf16[1,34,256]{2,1,0:T(8,128)(2,1)S(1)} %get-tuple-element.8), channel_id=1, source_target_pairs={{0,8},{16,24},{8,0},{24,16},{1,9},{17,25},{9,1},{25,17},{2,10},{18... | collective-permute-start | bytes 52232 | tf_op jit(solution)/shard_map/ppermute | solution.py:26
  11.1 1.9 %collective-permute-start.3 = (bf16[1,34,256]{2,1,0:T(8,128)(2,1)S(1)}, bf16[1,34,256]{2,1,0:T(8,128)(2,1)S(1)}, u32[]{:S(2)}, u32[]{:S(2)}) collective-permute-start(bf16[1,34,256]{2,1,0:T(8,128)(2,1)S(1)} %get-tuple-element.7), channel_id=1, source_target_pairs={{8,16},{16,8},{9,17},{17,9},{10,18},{18,10},{11,19},{19,11},{12,20... | collective-permute-start | bytes 52232 | tf_op jit(solution)/shard_map/ppermute | solution.py:25
  13.1 3.5 %collective-permute-done.3 = bf16[1,34,256]{2,1,0:T(8,128)(2,1)S(1)} collective-permute-done((bf16[1,34,256]{2,1,0:T(8,128)(2,1)S(1)}, bf16[1,34,256]{2,1,0:T(8,128)(2,1)S(1)}, u32[]{:S(2)}, u32[]{:S(2)}) %collective-permute-start.3) | collective-permute-done | bytes 17440 | tf_op jit(solution)/shard_map/ppermute | solution.py:25
  16.5 1.7 %pad_maximum_fusion.2 = (bf16[65,34,256]{2,1,0:T(8,128)(2,1)S(1)}, bf16[65,34,256]{2,1,0:T(8,128)(2,1)S(1)}) fusion(bf16[1,34,256]{2,1,0:T(8,128)(2,1)S(1)} %get-tuple-element.29, bf16[64,1,256]{2,1,0:T(2,128)(2,1)S(1)} %get-tuple-element.28, bf16[64,32,256]{2,1,0:T(8,128)(2,1)S(1)} %copy-done.1, bf16[64,1,256]{2,1,0:T(2,128)(2,1)S(1)} %get-tuple-element.27, ...), kind=kLoop, calls=%fused_computation.27 | loop fusion | flops 9052160 | bytes 3411968 | tf_op jit(solution)/shard_map/concatenate | solution.py:29
  21.5 2.6 %fusion.7 = bf16[2048,256]{1,0:T(8,128)(2,1)S(1)} fusion(bf16[2048,2304]{1,0:T(8,128)(2,1)S(1)} %bitcast.40, bf16[2304,256]{1,0:T(8,128)(2,1)S(1)} %bitcast.30), kind=kOutput, calls=%fused_computation.11 | convolution fusion | flops 2416967680 | bytes 11665408 | tf_op jit(solution)/shard_map/dot_general | solution.py:44
  24.3 1.4 %collective-permute-start.4 = (bf16[16,32,256]{2,1,0:T(8,128)(2,1)S(1)}, bf16[16,32,256]{2,1,0:T(8,128)(2,1)}, u32[]{:S(2)}, u32[]{:S(2)}) collective-permute-start(bf16[16,32,256]{2,1,0:T(8,128)(2,1)S(1)} %get-tuple-element.17), channel_id=1, source_target_pairs={{2,10},{3,11},{6,22},{7,23},{8,0},{9,1},{12,28},{13,29},{18,2},{19... | collective-permute-start | bytes 786440 | tf_op jit(solution)/shard_map/ppermute | solution.py:99
  27.0 1.4 %broadcast_select_fusion.4 = bf16[16,32,256]{2,1,0:T(8,128)(2,1)} fusion(bf16[16,32,256]{2,1,0:T(8,128)(2,1)} %collective-permute-done.4, bf16[16,32,256]{2,1,0:T(8,128)(2,1)S(1)} %get-tuple-element.17, pred[]{:T(512)} %bitcast.3), kind=kLoop, calls=%fused_computation.58 | loop fusion | flops 131072 | bytes 786433 | tf_op jit(solution)/shard_map/jit(_where)/select_n | solution.py:100
  28.4 1.9 %collective-permute-start.5 = (bf16[16,32,256]{2,1,0:T(8,128)(2,1)}, bf16[16,32,256]{2,1,0:T(8,128)(2,1)}, u32[]{:S(2)}, u32[]{:S(2)}) collective-permute-start(bf16[16,32,256]{2,1,0:T(8,128)(2,1)} %broadcast_select_fusion.4), channel_id=1, source_target_pairs={{10,8},{11,9},{4,16},{5,17},{22,24},{23,25},{0,2},{1,3},{28,18},{2... | collective-permute-start | bytes 786440 | tf_op jit(solution)/shard_map/ppermute | solution.py:101
  31.0 5.2 %collective-permute-start.7 = (bf16[16,32,256]{2,1,0:T(8,128)(2,1)S(1)}, bf16[16,32,256]{2,1,0:T(8,128)(2,1)S(1)}, u32[]{:S(2)}, u32[]{:S(2)}) collective-permute-start(bf16[16,32,256]{2,1,0:T(8,128)(2,1)S(1)} %broadcast_select_fusion.3), channel_id=1, source_target_pairs={{10,8},{11,9},{4,16},{5,17},{22,24},{23,25},{0,2},{1,3},{28,18},{2... | collective-permute-start | bytes 786440 | tf_op jit(solution)/shard_map/ppermute | solution.py:101
  36.2 1.4 %collective-permute-start.9 = (bf16[16,32,256]{2,1,0:T(8,128)(2,1)S(1)}, bf16[16,32,256]{2,1,0:T(8,128)(2,1)}, u32[]{:S(2)}, u32[]{:S(2)}) collective-permute-start(bf16[16,32,256]{2,1,0:T(8,128)(2,1)S(1)} %get-tuple-element.19), channel_id=1, source_target_pairs={{2,10},{3,11},{6,22},{7,23},{8,0},{9,1},{12,28},{13,29},{18,2},{19... | collective-permute-start | bytes 786440 | tf_op jit(solution)/shard_map/ppermute | solution.py:99
  38.7 4.8 %collective-permute-done.7 = bf16[16,32,256]{2,1,0:T(8,128)(2,1)S(1)} collective-permute-done((bf16[16,32,256]{2,1,0:T(8,128)(2,1)S(1)}, bf16[16,32,256]{2,1,0:T(8,128)(2,1)S(1)}, u32[]{:S(2)}, u32[]{:S(2)}) %collective-permute-start.7) | collective-permute-done | bytes 262176 | tf_op jit(solution)/shard_map/ppermute | solution.py:101
  43.5 1.8 %fusion.11 = (bf16[32,32,256]{2,0,1:T(8,128)(2,1)S(1)}, bf16[32,32,256]{2,1,0:T(8,128)(2,1)}) fusion(bf16[16,32,256]{2,1,0:T(8,128)(2,1)S(1)} %collective-permute-done.7, bf16[16,32,256]{2,1,0:T(8,128)(2,1)} %collective-permute-done.5, bf16[64,32,256]{2,1,0:T(8,128)(2,1)S(1)} %bitcast.32, s32[]{:T(128)S(6)} %select_n.185, pred[]{:T(512)S(6)} %eq.31, ...), kind=kLoop, calls=%fused_computation.50 | loop fusion | flops 524288 | bytes 2621449 | tf_op jit(solution)/shard_map/transpose | solution.py:104
  45.4 1.5 %collective-permute-start.8 = (bf16[32,32,256]{2,1,0:T(8,128)(2,1)}, bf16[32,32,256]{2,1,0:T(8,128)(2,1)}, u32[]{:S(2)}, u32[]{:S(2)}) collective-permute-start(bf16[32,32,256]{2,1,0:T(8,128)(2,1)} %get-tuple-element.16), channel_id=1, source_target_pairs={{0,1},{1,0},{10,11},{11,10},{20,21},{21,20},{30,31},{31,30}} | collective-permute-start | bytes 1572872 | tf_op jit(solution)/shard_map/ppermute | solution.py:102
  47.5 4.6 %collective-permute-start.10 = (bf16[16,32,256]{2,1,0:T(8,128)(2,1)S(1)}, bf16[16,32,256]{2,1,0:T(8,128)(2,1)S(1)}, u32[]{:S(2)}, u32[]{:S(2)}) collective-permute-start(bf16[16,32,256]{2,1,0:T(8,128)(2,1)S(1)} %broadcast_select_fusion.2), channel_id=1, source_target_pairs={{10,9},{11,8},{4,17},{5,16},{22,25},{23,24},{0,3},{1,2},{28,19},{2... | collective-permute-start | bytes 786440 | tf_op jit(solution)/shard_map/ppermute | solution.py:101
  52.1 1.4 %broadcast_select_fusion.1 = bf16[16,32,256]{2,1,0:T(8,128)(2,1)} fusion(bf16[16,32,256]{2,1,0:T(8,128)(2,1)S(1)} %collective-permute-done.11, bf16[16,32,256]{2,1,0:T(8,128)(2,1)S(1)} %get-tuple-element.18, pred[]{:T(512)} %bitcast.3), kind=kLoop, calls=%fused_computation.55 | loop fusion | flops 131072 | bytes 786433 | tf_op jit(solution)/shard_map/jit(_where)/select_n | solution.py:100
  53.5 2.8 %collective-permute-start.12 = (bf16[16,32,256]{2,1,0:T(8,128)(2,1)}, bf16[16,32,256]{2,1,0:T(8,128)(2,1)S(1)}, u32[]{:S(2)}, u32[]{:S(2)}) collective-permute-start(bf16[16,32,256]{2,1,0:T(8,128)(2,1)} %broadcast_select_fusion.1), channel_id=1, source_target_pairs={{10,9},{11,8},{4,17},{5,16},{22,25},{23,24},{0,3},{1,2},{28,19},{2... | collective-permute-start | bytes 786440 | tf_op jit(solution)/shard_map/ppermute | solution.py:101
  56.4 2.4 %copy.10 = bf16[3,3,256,256]{3,2,0,1:T(8,128)(2,1)} copy(bf16[3,3,256,256]{3,2,1,0:T(8,128)(2,1)} %param.7) | data formatting | bytes 2359296 | tf_op args[2]
  59.3 6.1 %collective-permute-done.12 = bf16[16,32,256]{2,1,0:T(8,128)(2,1)S(1)} collective-permute-done((bf16[16,32,256]{2,1,0:T(8,128)(2,1)}, bf16[16,32,256]{2,1,0:T(8,128)(2,1)S(1)}, u32[]{:S(2)}, u32[]{:S(2)}) %collective-permute-start.12) | collective-permute-done | bytes 262176 | tf_op jit(solution)/shard_map/ppermute | solution.py:101
  67.1 9.4 %collective-permute-start.14 = (bf16[64,6,256]{2,1,0:T(8,128)(2,1)S(1)}, bf16[64,6,256]{2,1,0:T(8,128)(2,1)S(1)}, u32[]{:S(2)}, u32[]{:S(2)}) collective-permute-start(bf16[64,6,256]{2,1,0:T(8,128)(2,1)S(1)} %get-tuple-element.12), channel_id=1, source_target_pairs={{1,2},{3,4},{5,6},{2,1},{4,3},{6,5},{9,10},{11,12},{13,14},{10,9},... | collective-permute-start | bytes 589832 | tf_op jit(solution)/shard_map/ppermute | solution.py:25
  76.6 4.3 %collective-permute-done.14 = bf16[64,6,256]{2,1,0:T(8,128)(2,1)S(1)} collective-permute-done((bf16[64,6,256]{2,1,0:T(8,128)(2,1)S(1)}, bf16[64,6,256]{2,1,0:T(8,128)(2,1)S(1)}, u32[]{:S(2)}, u32[]{:S(2)}) %collective-permute-start.14) | collective-permute-done | bytes 196640 | tf_op jit(solution)/shard_map/ppermute | solution.py:25
  80.9 0.9 pad_maximum_fusion.1
  81.9 3.2 %collective-permute-start.15 = (bf16[6,44,256]{2,1,0:T(8,128)(2,1)S(1)}, bf16[6,44,256]{2,1,0:T(8,128)(2,1)S(1)}, u32[]{:S(2)}, u32[]{:S(2)}) collective-permute-start(bf16[6,44,256]{2,1,0:T(8,128)(2,1)S(1)} %get-tuple-element.5), channel_id=1, source_target_pairs={{0,8},{16,24},{8,0},{24,16},{1,9},{17,25},{9,1},{25,17},{2,10},{18... | collective-permute-start | bytes 405512 | tf_op jit(solution)/shard_map/ppermute | solution.py:26
  85.0 2.1 %collective-permute-start.16 = (bf16[6,44,256]{2,1,0:T(8,128)(2,1)S(1)}, bf16[6,44,256]{2,1,0:T(8,128)(2,1)S(1)}, u32[]{:S(2)}, u32[]{:S(2)}) collective-permute-start(bf16[6,44,256]{2,1,0:T(8,128)(2,1)S(1)} %get-tuple-element.6), channel_id=1, source_target_pairs={{8,16},{16,8},{9,17},{17,9},{10,18},{18,10},{11,19},{19,11},{12,20... | collective-permute-start | bytes 405512 | tf_op jit(solution)/shard_map/ppermute | solution.py:25
  87.6 4.2 %collective-permute-done.16 = bf16[6,44,256]{2,1,0:T(8,128)(2,1)S(1)} collective-permute-done((bf16[6,44,256]{2,1,0:T(8,128)(2,1)S(1)}, bf16[6,44,256]{2,1,0:T(8,128)(2,1)S(1)}, u32[]{:S(2)}, u32[]{:S(2)}) %collective-permute-start.16) | collective-permute-done | bytes 135200 | tf_op jit(solution)/shard_map/ppermute | solution.py:25
  91.8 0.9 pad_maximum_fusion
  97.5 3.9 %fusion.1 = f32[2880,256]{1,0:T(8,128)S(1)} fusion(bf16[2880,2304]{1,0:T(8,128)(2,1)S(1)} %bitcast.38, bf16[2304,256]{1,0:T(8,128)(2,1)S(1)} %bitcast.37), kind=kOutput, calls=%fused_computation.2 | convolution fusion | flops 3399598080 | bytes 17399808 | tf_op jit(solution)/shard_map/dot_general | solution.py:44
  101.4 4.1 %fusion.6 = bf16[2880,256]{1,0:T(8,128)(2,1)S(1)} fusion(f32[2880,256]{1,0:T(8,128)S(1)} %fusion.1, bf16[2880,2304]{1,0:T(8,128)(2,1)S(1)} %bitcast.39, bf16[2304,256]{1,0:T(8,128)(2,1)S(1)} %bitcast.36), kind=kOutput, calls=%fused_computation.8 | convolution fusion | flops 3401809920 | bytes 18874368 | tf_op jit(solution)/shard_map/dot_general | solution.py:44
  108.9 3.6 %fusion.8 = bf16[2048,256]{1,0:T(8,128)(2,1)} fusion(bf16[2048,2304]{1,0:T(8,128)(2,1)S(1)} %bitcast.41, bf16[2304,256]{1,0:T(8,128)(2,1)S(1)} %bitcast.42), kind=kOutput, calls=%fused_computation.12 | convolution fusion | flops 2416967680 | bytes 11665408 | tf_op jit(solution)/shard_map/dot_general | solution.py:44
  (74 shorter events, 18.9 us)
Async XLA Ops:
  0.0 21.5 %copy-start = (bf16[3,3,256,256]{3,2,1,0:T(8,128)(2,1)S(1)}, bf16[3,3,256,256]{3,2,1,0:T(8,128)(2,1)}, u32[]{:S(2)}) copy-start(bf16[3,3,256,256]{3,2,1,0:T(8,128)(2,1)} %param.6) | copy-start | bytes 3538948
  0.0 16.5 %copy-start.1 = (bf16[64,32,256]{2,1,0:T(8,128)(2,1)S(1)}, bf16[64,32,256]{2,1,0:T(8,128)(2,1)}, u32[]{:S(2)}) copy-start(bf16[64,32,256]{2,1,0:T(8,128)(2,1)} %param.5) | copy-start | bytes 3145732
  1.3 3.9 %collective-permute-start = (bf16[64,1,256]{2,1,0:T(2,128)(2,1)S(1)}, bf16[64,1,256]{2,1,0:T(2,128)(2,1)S(1)}, u32[]{:S(2)}, u32[]{:S(2)}) collective-permute-start(bf16[64,1,256]{2,1,0:T(2,128)(2,1)S(1)} %get-tuple-element.21), channel_id=1, source_target_pairs={{0,1},{2,3},{4,5},{6,7},{1,0},{3,2},{5,4},{7,6},{8,9},{10,11},{12,... | collective-permute-start | bytes 98312 | tf_op jit(solution)/shard_map/ppermute | solution.py:26
  2.1 5.6 %collective-permute-start.1 = (bf16[64,1,256]{2,1,0:T(2,128)(2,1)S(1)}, bf16[64,1,256]{2,1,0:T(2,128)(2,1)S(1)}, u32[]{:S(2)}, u32[]{:S(2)}) collective-permute-start(bf16[64,1,256]{2,1,0:T(2,128)(2,1)S(1)} %get-tuple-element.22), channel_id=1, source_target_pairs={{1,2},{3,4},{5,6},{2,1},{4,3},{6,5},{9,10},{11,12},{13,14},{10,9},... | collective-permute-start | bytes 98312 | tf_op jit(solution)/shard_map/ppermute | solution.py:25
  9.8 3.2 %collective-permute-start.2 = (bf16[1,34,256]{2,1,0:T(8,128)(2,1)S(1)}, bf16[1,34,256]{2,1,0:T(8,128)(2,1)S(1)}, u32[]{:S(2)}, u32[]{:S(2)}) collective-permute-start(bf16[1,34,256]{2,1,0:T(8,128)(2,1)S(1)} %get-tuple-element.8), channel_id=1, source_target_pairs={{0,8},{16,24},{8,0},{24,16},{1,9},{17,25},{9,1},{25,17},{2,10},{18... | collective-permute-start | bytes 52232 | tf_op jit(solution)/shard_map/ppermute | solution.py:26
  11.1 5.4 %collective-permute-start.3 = (bf16[1,34,256]{2,1,0:T(8,128)(2,1)S(1)}, bf16[1,34,256]{2,1,0:T(8,128)(2,1)S(1)}, u32[]{:S(2)}, u32[]{:S(2)}) collective-permute-start(bf16[1,34,256]{2,1,0:T(8,128)(2,1)S(1)} %get-tuple-element.7), channel_id=1, source_target_pairs={{8,16},{16,8},{9,17},{17,9},{10,18},{18,10},{11,19},{19,11},{12,20... | collective-permute-start | bytes 52232 | tf_op jit(solution)/shard_map/ppermute | solution.py:25
  21.5 4.8 %copy-start.4 = (pred[4,4]{1,0:T(4,128)(4,1)S(1)}, pred[4,4]{1,0:T(4,128)(4,1)}, u32[]{:S(2)}) copy-start(pred[4,4]{1,0:T(4,128)(4,1)} %constant.107.clone) | copy-start | bytes 52
  24.3 2.7 %collective-permute-start.4 = (bf16[16,32,256]{2,1,0:T(8,128)(2,1)S(1)}, bf16[16,32,256]{2,1,0:T(8,128)(2,1)}, u32[]{:S(2)}, u32[]{:S(2)}) collective-permute-start(bf16[16,32,256]{2,1,0:T(8,128)(2,1)S(1)} %get-tuple-element.17), channel_id=1, source_target_pairs={{2,10},{3,11},{6,22},{7,23},{8,0},{9,1},{12,28},{13,29},{18,2},{19... | collective-permute-start | bytes 786440 | tf_op jit(solution)/shard_map/ppermute | solution.py:99
  25.6 4.7 %collective-permute-start.6 = (bf16[16,32,256]{2,1,0:T(8,128)(2,1)S(1)}, bf16[16,32,256]{2,1,0:T(8,128)(2,1)S(1)}, u32[]{:S(2)}, u32[]{:S(2)}) collective-permute-start(bf16[16,32,256]{2,1,0:T(8,128)(2,1)S(1)} %get-tuple-element.20), channel_id=1, source_target_pairs={{2,10},{3,11},{6,22},{7,23},{8,0},{9,1},{12,28},{13,29},{18,2},{19... | collective-permute-start | bytes 786440 | tf_op jit(solution)/shard_map/ppermute | solution.py:99
  28.4 10.3 %collective-permute-start.5 = (bf16[16,32,256]{2,1,0:T(8,128)(2,1)}, bf16[16,32,256]{2,1,0:T(8,128)(2,1)}, u32[]{:S(2)}, u32[]{:S(2)}) collective-permute-start(bf16[16,32,256]{2,1,0:T(8,128)(2,1)} %broadcast_select_fusion.4), channel_id=1, source_target_pairs={{10,8},{11,9},{4,16},{5,17},{22,24},{23,25},{0,2},{1,3},{28,18},{2... | collective-permute-start | bytes 786440 | tf_op jit(solution)/shard_map/ppermute | solution.py:101
  31.0 12.5 %collective-permute-start.7 = (bf16[16,32,256]{2,1,0:T(8,128)(2,1)S(1)}, bf16[16,32,256]{2,1,0:T(8,128)(2,1)S(1)}, u32[]{:S(2)}, u32[]{:S(2)}) collective-permute-start(bf16[16,32,256]{2,1,0:T(8,128)(2,1)S(1)} %broadcast_select_fusion.3), channel_id=1, source_target_pairs={{10,8},{11,9},{4,16},{5,17},{22,24},{23,25},{0,2},{1,3},{28,18},{2... | collective-permute-start | bytes 786440 | tf_op jit(solution)/shard_map/ppermute | solution.py:101
  36.2 10.6 %collective-permute-start.9 = (bf16[16,32,256]{2,1,0:T(8,128)(2,1)S(1)}, bf16[16,32,256]{2,1,0:T(8,128)(2,1)}, u32[]{:S(2)}, u32[]{:S(2)}) collective-permute-start(bf16[16,32,256]{2,1,0:T(8,128)(2,1)S(1)} %get-tuple-element.19), channel_id=1, source_target_pairs={{2,10},{3,11},{6,22},{7,23},{8,0},{9,1},{12,28},{13,29},{18,2},{19... | collective-permute-start | bytes 786440 | tf_op jit(solution)/shard_map/ppermute | solution.py:99
  37.6 14.6 %collective-permute-start.11 = (bf16[16,32,256]{2,1,0:T(8,128)(2,1)S(1)}, bf16[16,32,256]{2,1,0:T(8,128)(2,1)S(1)}, u32[]{:S(2)}, u32[]{:S(2)}) collective-permute-start(bf16[16,32,256]{2,1,0:T(8,128)(2,1)S(1)} %get-tuple-element.18), channel_id=1, source_target_pairs={{2,10},{3,11},{6,22},{7,23},{8,0},{9,1},{12,28},{13,29},{18,2},{19... | collective-permute-start | bytes 786440 | tf_op jit(solution)/shard_map/ppermute | solution.py:99
  45.4 20.1 %collective-permute-start.8 = (bf16[32,32,256]{2,1,0:T(8,128)(2,1)}, bf16[32,32,256]{2,1,0:T(8,128)(2,1)}, u32[]{:S(2)}, u32[]{:S(2)}) collective-permute-start(bf16[32,32,256]{2,1,0:T(8,128)(2,1)} %get-tuple-element.16), channel_id=1, source_target_pairs={{0,1},{1,0},{10,11},{11,10},{20,21},{21,20},{30,31},{31,30}} | collective-permute-start | bytes 1572872 | tf_op jit(solution)/shard_map/ppermute | solution.py:102
  47.5 11.8 %collective-permute-start.10 = (bf16[16,32,256]{2,1,0:T(8,128)(2,1)S(1)}, bf16[16,32,256]{2,1,0:T(8,128)(2,1)S(1)}, u32[]{:S(2)}, u32[]{:S(2)}) collective-permute-start(bf16[16,32,256]{2,1,0:T(8,128)(2,1)S(1)} %broadcast_select_fusion.2), channel_id=1, source_target_pairs={{10,9},{11,8},{4,17},{5,16},{22,25},{23,24},{0,3},{1,2},{28,19},{2... | collective-permute-start | bytes 786440 | tf_op jit(solution)/shard_map/ppermute | solution.py:101
  53.5 11.9 %collective-permute-start.12 = (bf16[16,32,256]{2,1,0:T(8,128)(2,1)}, bf16[16,32,256]{2,1,0:T(8,128)(2,1)S(1)}, u32[]{:S(2)}, u32[]{:S(2)}) collective-permute-start(bf16[16,32,256]{2,1,0:T(8,128)(2,1)} %broadcast_select_fusion.1), channel_id=1, source_target_pairs={{10,9},{11,8},{4,17},{5,16},{22,25},{23,24},{0,3},{1,2},{28,19},{2... | collective-permute-start | bytes 786440 | tf_op jit(solution)/shard_map/ppermute | solution.py:101
  66.9 9.6 %collective-permute-start.13 = (bf16[64,6,256]{2,1,0:T(8,128)(2,1)S(1)}, bf16[64,6,256]{2,1,0:T(8,128)(2,1)S(1)}, u32[]{:S(2)}, u32[]{:S(2)}) collective-permute-start(bf16[64,6,256]{2,1,0:T(8,128)(2,1)S(1)} %get-tuple-element.11), channel_id=1, source_target_pairs={{0,1},{2,3},{4,5},{6,7},{1,0},{3,2},{5,4},{7,6},{8,9},{10,11},{12,... | collective-permute-start | bytes 589832 | tf_op jit(solution)/shard_map/ppermute | solution.py:26
  67.1 13.8 %collective-permute-start.14 = (bf16[64,6,256]{2,1,0:T(8,128)(2,1)S(1)}, bf16[64,6,256]{2,1,0:T(8,128)(2,1)S(1)}, u32[]{:S(2)}, u32[]{:S(2)}) collective-permute-start(bf16[64,6,256]{2,1,0:T(8,128)(2,1)S(1)} %get-tuple-element.12), channel_id=1, source_target_pairs={{1,2},{3,4},{5,6},{2,1},{4,3},{6,5},{9,10},{11,12},{13,14},{10,9},... | collective-permute-start | bytes 589832 | tf_op jit(solution)/shard_map/ppermute | solution.py:25
  81.9 5.7 %collective-permute-start.15 = (bf16[6,44,256]{2,1,0:T(8,128)(2,1)S(1)}, bf16[6,44,256]{2,1,0:T(8,128)(2,1)S(1)}, u32[]{:S(2)}, u32[]{:S(2)}) collective-permute-start(bf16[6,44,256]{2,1,0:T(8,128)(2,1)S(1)} %get-tuple-element.5), channel_id=1, source_target_pairs={{0,8},{16,24},{8,0},{24,16},{1,9},{17,25},{9,1},{25,17},{2,10},{18... | collective-permute-start | bytes 405512 | tf_op jit(solution)/shard_map/ppermute | solution.py:26
  85.0 6.8 %collective-permute-start.16 = (bf16[6,44,256]{2,1,0:T(8,128)(2,1)S(1)}, bf16[6,44,256]{2,1,0:T(8,128)(2,1)S(1)}, u32[]{:S(2)}, u32[]{:S(2)}) collective-permute-start(bf16[6,44,256]{2,1,0:T(8,128)(2,1)S(1)} %get-tuple-element.6), channel_id=1, source_target_pairs={{8,16},{16,8},{9,17},{17,9},{10,18},{18,10},{11,19},{19,11},{12,20... | collective-permute-start | bytes 405512 | tf_op jit(solution)/shard_map/ppermute | solution.py:25
  96.0 1.5 %copy-start.3 = (bf16[3,3,256,256]{3,2,0,1:T(8,128)(2,1)S(1)}, bf16[3,3,256,256]{3,2,0,1:T(8,128)(2,1)}, u32[]{:S(2)}) copy-start(bf16[3,3,256,256]{3,2,0,1:T(8,128)(2,1)} %copy.10) | copy-start | bytes 3538948
  97.5 3.9 %copy-start.2 = (bf16[3,3,256,256]{3,2,1,0:T(8,128)(2,1)S(1)}, bf16[3,3,256,256]{3,2,1,0:T(8,128)(2,1)}, u32[]{:S(2)}) copy-start(bf16[3,3,256,256]{3,2,1,0:T(8,128)(2,1)} %param.7) | copy-start | bytes 3538948
  107.6 1.3 %copy-start.5 = (bf16[3,3,256,256]{3,2,1,0:T(8,128)(2,1)S(1)}, bf16[3,3,256,256]{3,2,1,0:T(8,128)(2,1)}, u32[]{:S(2)}) copy-start(bf16[3,3,256,256]{3,2,1,0:T(8,128)(2,1)} %param.8) | copy-start | bytes 3538948

commit v2 on v0

v2 whole, which is shorter than its diff:
```python
import math

import jax
import jax.numpy as jnp
import numpy as np
from jax import lax
from jax.experimental import pallas as pl
from jax.experimental.pallas import tpu as pltpu
from jax.sharding import PartitionSpec as P

AXES = ("row", "col")
BF16, F32 = jnp.bfloat16, jnp.float32
STRIP = 8
PAD = 16


def routes(row_count):
    low = math.isqrt(row_count)
    first, second = {}, {}
    for r in range(row_count):
        for z in range(row_count):
            a, b, c, d = r // low, r % low, z // low, z % low
            if r == z:
                continue
            via = (r, z) if b == d else ((z, z) if a == c else (c * low + b, z))
            if via != (r, z):
                first[(r, z)] = via
            second.setdefault(via, []).append((z, r))
    if any(len(ends) > 1 for ends in second.values()) or len(set(first.values())) < len(first):
        return {}, {(r, z): (z, r) for r in range(row_count) for z in range(row_count) if r != z}
    return first, {via: ends[0] for via, ends in second.items()}


class Place:
    def __init__(self):
        self.rows, self.cols = lax.axis_size("row"), lax.axis_size("col")
        self.row, self.col = lax.axis_index("row"), lax.axis_index("col")
        self.core = self.col % 2
        self.up = self.row % 2
        self.diagonal = self.row == self.col // 2
        self.first, self.second = routes(self.rows)

    def chips(self, array, legs):
        pairs = [
            (s[0] * self.cols + s[1] * 2 + k, e[0] * self.cols + e[1] * 2 + k)
            for s, e in legs.items()
            for k in range(2)
        ]
        return lax.ppermute(array, AXES, pairs)

    def carried(self, piece):
        sent = piece
        if self.first:
            relay = np.zeros((self.rows, self.rows), bool)
            for via in self.first.values():
                relay[via] = True
            here = jnp.asarray(relay)[self.row, self.col // 2]
            sent = jnp.where(here, self.chips(piece, self.first), piece)
        return self.chips(sent, self.second)


def pairwise(array, axis, start):
    size = lax.axis_size(axis)
    pairs = [(i, i + 1) for i in range(start, size - 1, 2)]
    if not pairs:
        return jnp.zeros_like(array)
    return lax.ppermute(array, axis, pairs + [(j, i) for i, j in pairs])


def widen(wide, padded, start, width, step):
    channels = padded.shape[2]
    for q in range(3):
        at = start + q * step
        wide[:, :, q * channels : (q + 1) * channels] = padded[:, at : at + width, :]


def products(wide, weight, row, rows, step, flip=False):
    width, channels = wide.shape[1], wide.shape[2] // 3
    taps = [
        wide[pl.ds(row + p * step, rows), :, q * channels : (q + 1) * channels].reshape(
            rows * width, channels
        )
        for p in range(3)
        for q in range(3)
    ]
    if flip:
        taps = [taps[q * 3 + p] for p in range(3) for q in range(3)]
    flat = weight[...].reshape(9 * channels, weight.shape[3])
    return jnp.maximum(jnp.dot(jnp.concatenate(taps, axis=1), flat, preferred_element_type=F32), 0.0)


def own_kernel(tile, near, far, band_near, band_far, weight, out, padded, wide, *, rows_a_step):
    core, up = lax.axis_index("col") % 2, lax.axis_index("row") % 2
    tile_rows, tile_cols, channels = tile.shape
    left, right = PAD - STRIP, PAD + tile_cols
    inner = pl.ds(STRIP, tile_rows)
    padded[inner, PAD:right, :] = tile[...]
    padded[inner, left:PAD, :] = jnp.where(core == 0, far[...], near[...])
    padded[inner, right : right + STRIP, :] = jnp.where(core == 0, near[...], far[...])
    padded[0:STRIP, left : right + STRIP, :] = jnp.where(up == 0, band_far[...], band_near[...])
    padded[pl.ds(STRIP + tile_rows, STRIP), left : right + STRIP, :] = jnp.where(
        up == 0, band_near[...], band_far[...]
    )
    width = out.shape[1]
    widen(wide, padded, left - 1, width, 1)

    def body(i, _):
        row = i * rows_a_step
        value = products(wide, weight, row + 1, rows_a_step, 1)
        out[pl.ds(row, rows_a_step)] = value.astype(BF16).reshape(rows_a_step, width, -1)
        return 0

    lax.fori_loop(0, out.shape[0] // rows_a_step, body, 0)


def band_kernel(kept0, got0, kept1, got1, near, far, to_near, to_far):
    row, col = lax.axis_index("row"), lax.axis_index("col")
    core, up = col % 2, row % 2
    diagonal = row == col // 2
    cols = got0.shape[0] // (2 * STRIP)
    mid = to_near.shape[0] - 4 * STRIP
    base = 2 * STRIP * cols

    def ring(ref_kept, ref_got, at, size):
        return jnp.where(diagonal, ref_kept[at : at + size, :], ref_got[at : at + size, :])

    for side in range(2):
        lo = 0 if side == 0 else cols - STRIP

        def emit(at, value, side=side):
            @pl.when(up == 1 - side)
            def _():
                to_near[at] = value

            @pl.when(up == side)
            def _():
                to_far[at] = value

        mine = core == side
        for y in range(STRIP):
            at = y * cols + lo
            half = STRIP * cols
            a = jnp.where(mine, far[half + at : half + at + STRIP, :], far[at : at + STRIP, :])
            b = jnp.where(mine, near[half + at : half + at + STRIP, :], near[at : at + STRIP, :])
            emit(y, jnp.where(core == 0, a, b))
            emit(3 * STRIP + mid + y, jnp.where(core == 0, b, a))
            for part, to in ((0, STRIP), (1, 2 * STRIP + mid)):
                where = part * half + at
                emit(
                    to + y,
                    jnp.where(
                        mine, ring(kept0, got0, where, STRIP), ring(kept1, got1, where, STRIP)
                    ),
                )
        for y in range(mid):
            at = base + y * STRIP
            emit(
                2 * STRIP + y,
                jnp.where(
                    mine,
                    ring(kept1, got1, at, STRIP),
                    ring(kept1, got1, at + mid * STRIP, STRIP),
                ),
            )


def rest_kernel(
    first, kept0, got0, kept1, got1, kept2, got2, near, far, band_near, band_far,
    w_first, w_second, w_third, out,
    padded, wide, flipped, sym, wide2, sym2, wide3,
    *, steps,
):
    row, col = lax.axis_index("row"), lax.axis_index("col")
    core, up = col % 2, row % 2
    diagonal = row == col // 2
    tile_rows, tile_cols, channels = out.shape
    mid = tile_cols - 2 * STRIP
    base = 2 * STRIP * tile_cols
    halves = channels // 128

    def pick(ref_kept, ref_got, at, size):
        return jnp.where(diagonal, ref_kept[at : at + size, :], ref_got[at : at + size, :])

    for k in range(2):

        @pl.when(core == k)
        def _():
            mine, other = PAD + k * tile_cols, PAD + (1 - k) * tile_cols
            for y in range(STRIP):
                for part, to in ((0, STRIP), (1, 2 * STRIP + mid)):
                    at = (part * STRIP + y) * tile_cols
                    padded[to + y, mine : mine + tile_cols, :] = pick(kept0, got0, at, tile_cols)
                    padded[to + y, other : other + tile_cols, :] = pick(kept1, got1, at, tile_cols)
            inner = tile_cols - STRIP
            edge = tile_rows - STRIP
            for y in range(mid):
                to = 2 * STRIP + y
                at = PAD + edge * k
                padded[to, at : at + STRIP, :] = pick(kept1, got1, base + y * STRIP, STRIP)
                at = PAD + edge * (1 - k)
                padded[to, at : at + STRIP, :] = pick(kept1, got1, base + (mid + y) * STRIP, STRIP)
                at = PAD + STRIP + inner * k
                padded[to, at : at + inner, :] = pick(kept2, got2, y * inner, inner)
                at = PAD + STRIP + inner * (1 - k)
                padded[to, at : at + inner, :] = pick(kept2, got2, (mid + y) * inner, inner)
            above, below = (far, near) if k == 0 else (near, far)
            half = STRIP * tile_cols
            for ref, to in ((above, 0), (below, STRIP + tile_cols)):
                for y in range(STRIP):
                    at = y * tile_cols
                    padded[to + y, other : other + tile_cols, :] = ref[at : at + tile_cols, :]
                    at += half
                    padded[to + y, mine : mine + tile_cols, :] = ref[at : at + tile_cols, :]

    padded[:, PAD - STRIP : PAD, :] = jnp.where(up == 0, band_far[...], band_near[...])
    end = PAD + tile_rows
    padded[:, end : end + STRIP, :] = jnp.where(up == 0, band_near[...], band_far[...])

    length = wide.shape[1]
    widen(wide, padded, PAD - STRIP - 1, length, 1)

    def firsts(i, _):
        at = i * steps[0]
        value = products(wide, w_first, at + 1, steps[0], 1).astype(BF16).astype(F32)
        for j in range(halves):
            to = pl.ds(pl.multiple_of((at + 2) * length, 8), steps[0] * length)
            flipped[j, to, :] = value[:, j * 128 : (j + 1) * 128]
        return 0

    lax.fori_loop(0, (tile_cols + 12) // steps[0], firsts, 0)

    width = first.shape[1]
    total_rows, total_cols = tile_rows * lax.axis_size("row"), tile_cols * lax.axis_size("col")
    x = col * tile_cols - STRIP + lax.broadcasted_iota(jnp.int32, (width, 1), 0)
    valid = (x >= 0) & (x < total_cols)

    def averages(i, _):
        y = row * tile_rows - 6 + i
        turned = jnp.concatenate(
            [flipped[j, pl.ds(i + 2, width, stride=length), :] for j in range(halves)], axis=1
        )
        mean = (first[i].astype(F32) + turned) * 0.5
        ok = valid & (y >= 0) & (y < total_rows)
        sym[i, STRIP : STRIP + width, :] = jnp.where(ok, mean, 0.0).astype(BF16)
        return 0

    lax.fori_loop(0, first.shape[0], averages, 0)

    widen(wide2, sym, STRIP - 2, width, 2)

    def seconds(i, _):
        at = i * steps[1]
        a = products(wide2, w_second, at, steps[1], 2).astype(BF16).astype(F32)
        b = products(wide2, w_second, at, steps[1], 2, flip=True).astype(BF16).astype(F32)
        mean = ((a + b) * 0.5).reshape(steps[1], width, channels)
        y = row * tile_rows - 4 + at + lax.broadcasted_iota(jnp.int32, (steps[1], 1, 1), 0)
        ok = valid.reshape(1, width, 1) & (y >= 0) & (y < total_rows)
        sym2[pl.ds(at, steps[1])] = jnp.where(ok, mean, 0.0).astype(BF16)
        return 0

    lax.fori_loop(0, (tile_rows + 8) // steps[1], seconds, 0)
    widen(wide3, sym2, STRIP - 4, tile_cols, 4)

    def thirds(i, _):
        at = i * steps[2]
        value = products(wide3, w_third, at, steps[2], 4)
        out[pl.ds(at, steps[2])] = value.astype(BF16).reshape(steps[2], tile_cols, channels)
        return 0

    lax.fori_loop(0, tile_rows // steps[2], thirds, 0)


def whole(count):
    return [pl.BlockSpec(memory_space=pltpu.VMEM)] * count


def divisor(number, most):
    return max(d for d in range(1, most + 1) if number % d == 0)


def local(contacts, w_first, w_second, w_third):
    tile_rows, tile_cols, channels = contacts.shape
    place = Place()
    core, up = place.core, place.up
    params = pltpu.CompilerParams(vmem_limit_bytes=48 * 2**20)
    span, stretch = tile_cols + 2 * STRIP, tile_rows + 2 * STRIP

    def flat(array):
        return array.reshape(-1, channels)

    def cut(array, at, size, dim):
        return lax.dynamic_slice_in_dim(array, at, size, dim)

    mine = cut(contacts, core * tile_cols, tile_cols, 0)
    other = pairwise(cut(contacts, (1 - core) * tile_cols, tile_cols, 0), "col", 0)
    edge = tile_cols - STRIP
    ends = [(0, STRIP), (edge, tile_cols)]
    kept0 = flat(jnp.concatenate([mine[a:b] for a, b in ends]))
    mid_mine, mid_other = mine[STRIP:edge], other[STRIP:edge]
    kept1 = jnp.concatenate(
        [flat(other[a:b]) for a, b in ends]
        + [flat(cut(mid_mine, core * edge, STRIP, 1)), flat(cut(mid_other, (1 - core) * edge, STRIP, 1))]
    )
    kept2 = jnp.concatenate(
        [flat(cut(mid_mine, (1 - core) * STRIP, edge, 1)), flat(cut(mid_other, core * STRIP, edge, 1))]
    )
    got0, got1 = place.carried(kept0), place.carried(kept1)

    near = pairwise(cut(contacts, (1 - core) * edge, STRIP, 1), "col", 0)
    far = pairwise(cut(contacts, core * edge, STRIP, 1), "col", 1)
    left, right = jnp.where(core == 0, far, near), jnp.where(core == 0, near, far)

    def band(at):
        return jnp.concatenate([cut(part, at, STRIP, 0) for part in (left, contacts, right)], axis=1)

    last = tile_rows - STRIP
    band_near = pairwise(band((1 - up) * last), "row", 0)
    band_far = pairwise(band(up * last), "row", 1)
    first = pl.pallas_call(
        lambda *refs: own_kernel(*refs, rows_a_step=divisor(tile_rows + 12, 19)),
        out_shape=jax.ShapeDtypeStruct((tile_rows + 12, span, channels), BF16),
        in_specs=whole(6),
        out_specs=whole(1)[0],
        scratch_shapes=[
            pltpu.VMEM((stretch, tile_cols + 2 * PAD, channels), BF16),
            pltpu.VMEM((stretch, span, 3 * channels), BF16),
        ],
        compiler_params=params,
        name="own_first",
    )(contacts, near, far, band_near, band_far, w_first)

    got2 = place.carried(kept2)

    def ends_of(at):
        pieces = []
        for kept, got in ((kept0, got0), (kept1, got1)):
            size = STRIP * tile_cols
            pieces.append(
                jnp.where(place.diagonal, cut(kept, at * size, size, 0), cut(got, at * size, size, 0))
            )
        return jnp.concatenate(pieces)

    near = pairwise(ends_of(1 - core), "col", 0)
    far = pairwise(ends_of(core), "col", 1)
    strip = jax.ShapeDtypeStruct((span, STRIP, channels), BF16)
    to_near, to_far = pl.pallas_call(
        band_kernel,
        out_shape=(strip, strip),
        in_specs=whole(6),
        out_specs=tuple(whole(2)),
        compiler_params=params,
        name="bands",
    )(kept0, got0, kept1, got1, near, far)
    band_near, band_far = pairwise(to_near, "row", 0), pairwise(to_far, "row", 1)
    steps = (divisor(tile_cols + 12, 11), divisor(tile_rows + 8, 12), divisor(tile_rows, 16))
    return pl.pallas_call(
        lambda *refs: rest_kernel(*refs, steps=steps),
        out_shape=jax.ShapeDtypeStruct(contacts.shape, BF16),
        in_specs=whole(14),
        out_specs=whole(1)[0],
        scratch_shapes=[
            pltpu.VMEM((span, tile_rows + 2 * PAD, channels), BF16),
            pltpu.VMEM((span, stretch, 3 * channels), BF16),
            pltpu.VMEM((channels // 128, span * stretch, 128), F32),
            pltpu.VMEM((tile_rows + 12, tile_cols + 2 * PAD, channels), BF16),
            pltpu.VMEM((tile_rows + 12, span, 3 * channels), BF16),
            pltpu.VMEM((tile_rows + 8, span, channels), BF16),
            pltpu.VMEM((tile_rows + 8, tile_cols, 3 * channels), BF16),
        ],
        compiler_params=params,
        name="rest",
    )(
        first, kept0, got0, kept1, got1, kept2, got2, near, far, band_near, band_far,
        w_first, w_second, w_third,
    )


def solution(mesh):
    return jax.shard_map(
        local,
        mesh=mesh,
        in_specs=(P("row", "col", None), P(), P(), P()),
        out_specs=P("row", "col", None),
        check_vma=False,
    )
```

time: 202 us -> 97.9 us (0.48)
  the two profiles are of different devices: /device:TPU:5 before, /device:TPU:3 now
where the time goes in v2:
time: 97.9 us; the launch traced here: 97.5 us
  starting transfers between devices  36.6 us (37%)
  Pallas kernels  32 us (33%)
  waiting for transfers between devices  21 us (21%)
  local copies, waits for them, and re-layouts  4.01 us (4%)
  other arithmetic  3.38 us (3%)
    pallas_call x1, Pallas kernels, local(): pl.pallas_call(lambda *refs: rest_kernel(*refs, steps=steps), out_shape=j...  25.1 us
    ppermute x6, starting transfers between devices, chips(): return lax.ppermute(array, AXES, pairs)  22.5 us
    ppermute x9, starting transfers between devices, pairwise(): return lax.ppermute(array, axis, pairs + [(j, i) for i, j in pairs])  14.2 us
    ppermute x9, waiting for transfers between devices, pairwise(): return lax.ppermute(array, axis, pairs + [(j, i) for i, j in pairs])  12.8 us
    ppermute x6, waiting for transfers between devices, chips(): return lax.ppermute(array, AXES, pairs)  8.21 us
    pallas_call x1, Pallas kernels, local(): pl.pallas_call(lambda *refs: own_kernel(*refs, rows_a_step=divisor(tile_r...  6.31 us
    select_n x3, other arithmetic, carried(): sent = jnp.where(here, self.chips(piece, self.first), piece)  3.06 us
    dynamic_slice x5, local copies, waits for them, and re-layouts, cut(): return lax.dynamic_slice_in_dim(array, at, size, dim)  2.02 us
  transfers between devices with their start and end apart: 15, of which 3 were waited for; matrix products, arithmetic and copies ran while one was open for 5% of the time, Pallas kernels for 7%

profile of v2, /device:TPU:3, one launch (start us, length us, event | category | flops | bytes accessed | tf_op | source)
XLA Modules:
  0.0 97.5 jit_solution(7044505173116361034)
XLA Ops:
  0.0 1.2 %constant_dynamic-slice_fusion.4 = bf16[32,32,256]{2,1,0:T(8,128)(2,1)S(1)} fusion(bf16[64,32,256]{2,1,0:T(8,128)(2,1)} %refs_0_.1, s32[]{:T(128)S(6)} %select_n.143), kind=kLoop, calls=%fused_computation.22 | loop fusion | bytes 1048580 | tf_op jit(solution)/shard_map/dynamic_slice | solution.py:292
  1.2 0.7 collective-permute-start.6
  2.0 1.9 %collective-permute-start.4 = (bf16[512,256]{1,0:T(8,128)(2,1)S(1)}, bf16[512,256]{1,0:T(8,128)(2,1)}, u32[]{:S(2)}, u32[]{:S(2)}) collective-permute-start(bf16[512,256]{1,0:T(8,128)(2,1)S(1)} %bitcast.11), channel_id=1, source_target_pairs={{2,10},{3,11},{6,22},{7,23},{8,0},{9,1},{12,28},{13,29},{18,2},{19... | collective-permute-start | bytes 786440 | tf_op jit(solution)/shard_map/ppermute | solution.py:49
  3.9 0.8 constant_dynamic-slice_fusion.11
  4.7 2.6 %collective-permute-start.1 = (bf16[64,8,256]{2,1,0:T(8,128)(2,1)}, bf16[64,8,256]{2,1,0:T(8,128)(2,1)S(1)}, u32[]{:S(2)}, u32[]{:S(2)}) collective-permute-start(bf16[64,8,256]{2,1,0:T(8,128)(2,1)} %get-tuple-element.13), channel_id=1, source_target_pairs={{1,2},{3,4},{5,6},{2,1},{4,3},{6,5},{9,10},{11,12},{13,14},{10,9},... | collective-permute-start | bytes 786440 | tf_op jit(solution)/shard_map/ppermute | solution.py:67
  7.3 0.1 collective-permute-start
  7.5 0.6 dynamic_slice.84
  8.3 4.3 %collective-permute-start.7 = (bf16[768,256]{1,0:T(8,128)(2,1)S(1)}, bf16[768,256]{1,0:T(8,128)(2,1)S(1)}, u32[]{:S(2)}, u32[]{:S(2)}) collective-permute-start(bf16[768,256]{1,0:T(8,128)(2,1)S(1)} %pad_maximum_fusion.kept1.refs_3_), channel_id=1, source_target_pairs={{2,10},{3,11},{6,22},{7,23},{8,0},{9,1},{12,28},{13,29},{18,2},{19... | collective-permute-start | bytes 1179656 | tf_op jit(solution)/shard_map/ppermute | solution.py:49
  12.6 1.6 %broadcast_select_fusion.2 = bf16[512,256]{1,0:T(8,128)(2,1)S(1)} fusion(bf16[512,256]{1,0:T(8,128)(2,1)} %collective-permute-done.4, pred[]{:T(512)} %bitcast.1, bf16[16,32,256]{2,1,0:T(8,128)(2,1)S(1)} %pad_maximum_fusion.2), kind=kLoop, calls=%fused_computation.7 | loop fusion | flops 131072 | bytes 786433 | tf_op jit(solution)/shard_map/jit(_where)/select_n | solution.py:58
  14.2 4.0 %collective-permute-start.5 = (bf16[512,256]{1,0:T(8,128)(2,1)S(1)}, bf16[512,256]{1,0:T(8,128)(2,1)S(1)}, u32[]{:S(2)}, u32[]{:S(2)}) collective-permute-start(bf16[512,256]{1,0:T(8,128)(2,1)S(1)} %broadcast_select_fusion.2), channel_id=1, source_target_pairs={{10,8},{11,9},{4,16},{5,17},{22,24},{23,25},{0,2},{1,3},{28,18},{2... | collective-permute-start | bytes 786440 | tf_op jit(solution)/shard_map/ppermute | solution.py:49
  18.3 2.3 %collective-permute-done.7 = bf16[768,256]{1,0:T(8,128)(2,1)S(1)} collective-permute-done((bf16[768,256]{1,0:T(8,128)(2,1)S(1)}, bf16[768,256]{1,0:T(8,128)(2,1)S(1)}, u32[]{:S(2)}, u32[]{:S(2)}) %collective-permute-start.7) | collective-permute-done | bytes 393248 | tf_op jit(solution)/shard_map/ppermute | solution.py:49
  20.6 0.7 broadcast_select_fusion.1
  21.3 5.4 %collective-permute-start.8 = (bf16[768,256]{1,0:T(8,128)(2,1)S(1)}, bf16[768,256]{1,0:T(8,128)(2,1)S(1)}, u32[]{:S(2)}, u32[]{:S(2)}) collective-permute-start(bf16[768,256]{1,0:T(8,128)(2,1)S(1)} %broadcast_select_fusion.1), channel_id=1, source_target_pairs={{10,8},{11,9},{4,16},{5,17},{22,24},{23,25},{0,2},{1,3},{28,18},{2... | collective-permute-start | bytes 1179656 | tf_op jit(solution)/shard_map/ppermute | solution.py:49
  26.8 1.9 %collective-permute-start.9 = (bf16[768,256]{1,0:T(8,128)(2,1)S(1)}, bf16[768,256]{1,0:T(8,128)(2,1)S(1)}, u32[]{:S(2)}, u32[]{:S(2)}) collective-permute-start(bf16[768,256]{1,0:T(8,128)(2,1)S(1)} %pad_maximum_fusion.1.refs_5_), channel_id=1, source_target_pairs={{2,10},{3,11},{6,22},{7,23},{8,0},{9,1},{12,28},{13,29},{18,2},{19... | collective-permute-start | bytes 1179656 | tf_op jit(solution)/shard_map/ppermute | solution.py:49
  28.7 0.1 dynamic-slice_select_fusion.1
  28.8 5.9 %collective-permute-done.8.got1.refs_4_ = bf16[768,256]{1,0:T(8,128)(2,1)S(1)} collective-permute-done((bf16[768,256]{1,0:T(8,128)(2,1)S(1)}, bf16[768,256]{1,0:T(8,128)(2,1)S(1)}, u32[]{:S(2)}, u32[]{:S(2)}) %collective-permute-start.8) | collective-permute-done | bytes 393248 | tf_op jit(solution)/shard_map/ppermute | solution.py:49
  34.7 0.1 dynamic-slice_select_fusion
  34.8 2.0 %collective-permute-start.11 = (bf16[512,256]{1,0:T(8,128)(2,1)S(1)}, bf16[512,256]{1,0:T(8,128)(2,1)S(1)}, u32[]{:S(2)}, u32[]{:S(2)}) collective-permute-start(bf16[512,256]{1,0:T(8,128)(2,1)S(1)} %pad_maximum_fusion.3), channel_id=1, source_target_pairs={{0,1},{2,3},{4,5},{6,7},{1,0},{3,2},{5,4},{7,6},{8,9},{10,11},{12,... | collective-permute-start | bytes 786440 | tf_op jit(solution)/shard_map/ppermute | solution.py:67
  36.8 1.9 %collective-permute-start.12 = (bf16[512,256]{1,0:T(8,128)(2,1)S(1)}, bf16[512,256]{1,0:T(8,128)(2,1)S(1)}, u32[]{:S(2)}, u32[]{:S(2)}) collective-permute-start(bf16[512,256]{1,0:T(8,128)(2,1)S(1)} %pad_maximum_fusion.4), channel_id=1, source_target_pairs={{1,2},{3,4},{5,6},{2,1},{4,3},{6,5},{9,10},{11,12},{13,14},{10,9},... | collective-permute-start | bytes 786440 | tf_op jit(solution)/shard_map/ppermute | solution.py:67
  38.7 0.7 broadcast_select_fusion
  39.5 4.9 %collective-permute-start.10 = (bf16[768,256]{1,0:T(8,128)(2,1)S(1)}, bf16[768,256]{1,0:T(8,128)(2,1)S(1)}, u32[]{:S(2)}, u32[]{:S(2)}) collective-permute-start(bf16[768,256]{1,0:T(8,128)(2,1)S(1)} %broadcast_select_fusion), channel_id=1, source_target_pairs={{10,8},{11,9},{4,16},{5,17},{22,24},{23,25},{0,2},{1,3},{28,18},{2... | collective-permute-start | bytes 1179656 | tf_op jit(solution)/shard_map/ppermute | solution.py:49
  44.4 0.0 copy-start.2
  44.5 0.1 collective-permute-start.2
  44.6 4.6 %collective-permute-start.3 = (bf16[8,48,256]{2,1,0:T(8,128)(2,1)S(1)}, bf16[8,48,256]{2,1,0:T(8,128)(2,1)S(1)}, u32[]{:S(2)}, u32[]{:S(2)}) collective-permute-start(bf16[8,48,256]{2,1,0:T(8,128)(2,1)S(1)} %pad_maximum_fusion.6), channel_id=1, source_target_pairs={{8,16},{16,8},{9,17},{17,9},{10,18},{18,10},{11,19},{19,11},{12,20... | collective-permute-start | bytes 589832 | tf_op jit(solution)/shard_map/ppermute | solution.py:67
  49.2 0.6 bands.1
  49.8 0.1 collective-permute-start.13
  49.9 0.0 copy-start.3
  49.9 2.1 %collective-permute-start.14 = (bf16[48,8,256]{2,1,0:T(8,128)(2,1)S(1)}, bf16[48,8,256]{2,1,0:T(8,128)(2,1)S(1)}, u32[]{:S(2)}, u32[]{:S(2)}) collective-permute-start(bf16[48,8,256]{2,1,0:T(8,128)(2,1)S(1)} %get-tuple-element.8), channel_id=1, source_target_pairs={{8,16},{16,8},{9,17},{17,9},{10,18},{18,10},{11,19},{19,11},{12,20... | collective-permute-start | bytes 589832 | tf_op jit(solution)/shard_map/ppermute | solution.py:67
  52.0 12.7 %collective-permute-done.3.refs_4_ = bf16[8,48,256]{2,1,0:T(8,128)(2,1)S(1)} collective-permute-done((bf16[8,48,256]{2,1,0:T(8,128)(2,1)S(1)}, bf16[8,48,256]{2,1,0:T(8,128)(2,1)S(1)}, u32[]{:S(2)}, u32[]{:S(2)}) %collective-permute-start.3) | collective-permute-done | bytes 196640 | tf_op jit(solution)/shard_map/ppermute | solution.py:67
  64.8 6.3 %own_first.1.refs_0_ = bf16[76,48,256]{2,1,0:T(8,128)(2,1)S(1)} custom-call(bf16[64,32,256]{2,1,0:T(8,128)(2,1)S(1)} %copy-done, bf16[64,8,256]{2,1,0:T(8,128)(2,1)S(1)} %collective-permute-done.refs_1_, bf16[64,8,256]{2,1,0:T(8,128)(2,1)S(1)} %collective-permute-done.1.refs_2_, bf16[8,48,256]{2,1,0:T(8,128)(2,1)S(1)} %collective-permute-done.2.refs_3_, ...), custom_call_target="tpu_custom_call" | custom-call | tf_op jit(solution)/shard_map/own_first/pallas_call | solution.py:319
  71.1 1.2 %copy-done.1 = bf16[76,48,256]{2,1,0:T(8,128)(2,1)} copy-done((bf16[76,48,256]{2,1,0:T(8,128)(2,1)}, bf16[76,48,256]{2,1,0:T(8,128)(2,1)S(1)}, u32[]{:S(2)}) %copy-start.1) | copy-done | bytes 1867800
  72.3 25.1 %rest.1 = bf16[64,32,256]{2,1,0:T(8,128)(2,1)} custom-call(bf16[76,48,256]{2,1,0:T(8,128)(2,1)} %copy-done.1, bf16[512,256]{1,0:T(8,128)(2,1)S(1)} %bitcast.14, bf16[512,256]{1,0:T(8,128)(2,1)S(1)} %collective-permute-done.5.got0.refs_2_, bf16[768,256]{1,0:T(8,128)(2,1)S(1)} %pad_maximum_fusion.kept1.refs_3_, ...), custom_call_target="tpu_custom_call" | custom-call | tf_op jit(solution)/shard_map/rest/pallas_call | solution.py:356
  (35 shorter events, 0.4 us)
Async XLA Ops:
  0.0 1.9 %copy-start = (bf16[64,32,256]{2,1,0:T(8,128)(2,1)S(1)}, bf16[64,32,256]{2,1,0:T(8,128)(2,1)}, u32[]{:S(2)}) copy-start(bf16[64,32,256]{2,1,0:T(8,128)(2,1)} %refs_0_.1) | copy-start | bytes 3145732
  1.2 7.0 %collective-permute-start.6 = (bf16[32,32,256]{2,1,0:T(8,128)(2,1)S(1)}, bf16[32,32,256]{2,1,0:T(8,128)(2,1)S(1)}, u32[]{:S(2)}, u32[]{:S(2)}) collective-permute-start(bf16[32,32,256]{2,1,0:T(8,128)(2,1)S(1)} %constant_dynamic-slice_fusion.4), channel_id=1, source_target_pairs={{0,1},{2,3},{4,5},{6,7},{1,0},{3,2},{5,4},{7,6},{8,9},{10,11},{12,... | collective-permute-start | bytes 1572872 | tf_op jit(solution)/shard_map/ppermute | solution.py:67
  1.9 5.5 %copy-start.4 = (pred[4,4]{1,0:T(4,128)(4,1)S(1)}, pred[4,4]{1,0:T(4,128)(4,1)}, u32[]{:S(2)}) copy-start(pred[4,4]{1,0:T(4,128)(4,1)} %constant.64.clone) | copy-start | bytes 52
  2.0 10.6 %collective-permute-start.4 = (bf16[512,256]{1,0:T(8,128)(2,1)S(1)}, bf16[512,256]{1,0:T(8,128)(2,1)}, u32[]{:S(2)}, u32[]{:S(2)}) collective-permute-start(bf16[512,256]{1,0:T(8,128)(2,1)S(1)} %bitcast.11), channel_id=1, source_target_pairs={{2,10},{3,11},{6,22},{7,23},{8,0},{9,1},{12,28},{13,29},{18,2},{19... | collective-permute-start | bytes 786440 | tf_op jit(solution)/shard_map/ppermute | solution.py:49
  4.7 13.5 %collective-permute-start.1 = (bf16[64,8,256]{2,1,0:T(8,128)(2,1)}, bf16[64,8,256]{2,1,0:T(8,128)(2,1)S(1)}, u32[]{:S(2)}, u32[]{:S(2)}) collective-permute-start(bf16[64,8,256]{2,1,0:T(8,128)(2,1)} %get-tuple-element.13), channel_id=1, source_target_pairs={{1,2},{3,4},{5,6},{2,1},{4,3},{6,5},{9,10},{11,12},{13,14},{10,9},... | collective-permute-start | bytes 786440 | tf_op jit(solution)/shard_map/ppermute | solution.py:67
  7.3 10.9 %collective-permute-start = (bf16[64,8,256]{2,1,0:T(8,128)(2,1)S(1)}, bf16[64,8,256]{2,1,0:T(8,128)(2,1)S(1)}, u32[]{:S(2)}, u32[]{:S(2)}) collective-permute-start(bf16[64,8,256]{2,1,0:T(8,128)(2,1)S(1)} %get-tuple-element.14), channel_id=1, source_target_pairs={{0,1},{2,3},{4,5},{6,7},{1,0},{3,2},{5,4},{7,6},{8,9},{10,11},{12,... | collective-permute-start | bytes 786440 | tf_op jit(solution)/shard_map/ppermute | solution.py:67
  8.3 12.3 %collective-permute-start.7 = (bf16[768,256]{1,0:T(8,128)(2,1)S(1)}, bf16[768,256]{1,0:T(8,128)(2,1)S(1)}, u32[]{:S(2)}, u32[]{:S(2)}) collective-permute-start(bf16[768,256]{1,0:T(8,128)(2,1)S(1)} %pad_maximum_fusion.kept1.refs_3_), channel_id=1, source_target_pairs={{2,10},{3,11},{6,22},{7,23},{8,0},{9,1},{12,28},{13,29},{18,2},{19... | collective-permute-start | bytes 1179656 | tf_op jit(solution)/shard_map/ppermute | solution.py:49
  14.2 14.5 %collective-permute-start.5 = (bf16[512,256]{1,0:T(8,128)(2,1)S(1)}, bf16[512,256]{1,0:T(8,128)(2,1)S(1)}, u32[]{:S(2)}, u32[]{:S(2)}) collective-permute-start(bf16[512,256]{1,0:T(8,128)(2,1)S(1)} %broadcast_select_fusion.2), channel_id=1, source_target_pairs={{10,8},{11,9},{4,16},{5,17},{22,24},{23,25},{0,2},{1,3},{28,18},{2... | collective-permute-start | bytes 786440 | tf_op jit(solution)/shard_map/ppermute | solution.py:49
  21.3 13.4 %collective-permute-start.8 = (bf16[768,256]{1,0:T(8,128)(2,1)S(1)}, bf16[768,256]{1,0:T(8,128)(2,1)S(1)}, u32[]{:S(2)}, u32[]{:S(2)}) collective-permute-start(bf16[768,256]{1,0:T(8,128)(2,1)S(1)} %broadcast_select_fusion.1), channel_id=1, source_target_pairs={{10,8},{11,9},{4,16},{5,17},{22,24},{23,25},{0,2},{1,3},{28,18},{2... | collective-permute-start | bytes 1179656 | tf_op jit(solution)/shard_map/ppermute | solution.py:49
  26.8 11.9 %collective-permute-start.9 = (bf16[768,256]{1,0:T(8,128)(2,1)S(1)}, bf16[768,256]{1,0:T(8,128)(2,1)S(1)}, u32[]{:S(2)}, u32[]{:S(2)}) collective-permute-start(bf16[768,256]{1,0:T(8,128)(2,1)S(1)} %pad_maximum_fusion.1.refs_5_), channel_id=1, source_target_pairs={{2,10},{3,11},{6,22},{7,23},{8,0},{9,1},{12,28},{13,29},{18,2},{19... | collective-permute-start | bytes 1179656 | tf_op jit(solution)/shard_map/ppermute | solution.py:49
  34.8 14.4 %collective-permute-start.11 = (bf16[512,256]{1,0:T(8,128)(2,1)S(1)}, bf16[512,256]{1,0:T(8,128)(2,1)S(1)}, u32[]{:S(2)}, u32[]{:S(2)}) collective-permute-start(bf16[512,256]{1,0:T(8,128)(2,1)S(1)} %pad_maximum_fusion.3), channel_id=1, source_target_pairs={{0,1},{2,3},{4,5},{6,7},{1,0},{3,2},{5,4},{7,6},{8,9},{10,11},{12,... | collective-permute-start | bytes 786440 | tf_op jit(solution)/shard_map/ppermute | solution.py:67
  36.8 12.4 %collective-permute-start.12 = (bf16[512,256]{1,0:T(8,128)(2,1)S(1)}, bf16[512,256]{1,0:T(8,128)(2,1)S(1)}, u32[]{:S(2)}, u32[]{:S(2)}) collective-permute-start(bf16[512,256]{1,0:T(8,128)(2,1)S(1)} %pad_maximum_fusion.4), channel_id=1, source_target_pairs={{1,2},{3,4},{5,6},{2,1},{4,3},{6,5},{9,10},{11,12},{13,14},{10,9},... | collective-permute-start | bytes 786440 | tf_op jit(solution)/shard_map/ppermute | solution.py:67
  39.5 32.9 %collective-permute-start.10 = (bf16[768,256]{1,0:T(8,128)(2,1)S(1)}, bf16[768,256]{1,0:T(8,128)(2,1)S(1)}, u32[]{:S(2)}, u32[]{:S(2)}) collective-permute-start(bf16[768,256]{1,0:T(8,128)(2,1)S(1)} %broadcast_select_fusion), channel_id=1, source_target_pairs={{10,8},{11,9},{4,16},{5,17},{22,24},{23,25},{0,2},{1,3},{28,18},{2... | collective-permute-start | bytes 1179656 | tf_op jit(solution)/shard_map/ppermute | solution.py:49
  44.4 20.3 %copy-start.2 = (bf16[3,3,256,256]{3,2,1,0:T(8,128)(2,1)S(1)}, bf16[3,3,256,256]{3,2,1,0:T(8,128)(2,1)}, u32[]{:S(2)}) copy-start(bf16[3,3,256,256]{3,2,1,0:T(8,128)(2,1)} %refs_11_.1) | copy-start | bytes 3538948
  44.5 7.6 %collective-permute-start.2 = (bf16[8,48,256]{2,1,0:T(8,128)(2,1)S(1)}, bf16[8,48,256]{2,1,0:T(8,128)(2,1)S(1)}, u32[]{:S(2)}, u32[]{:S(2)}) collective-permute-start(bf16[8,48,256]{2,1,0:T(8,128)(2,1)S(1)} %pad_maximum_fusion.5), channel_id=1, source_target_pairs={{0,8},{16,24},{8,0},{24,16},{1,9},{17,25},{9,1},{25,17},{2,10},{18... | collective-permute-start | bytes 589832 | tf_op jit(solution)/shard_map/ppermute | solution.py:67
  44.6 20.2 %collective-permute-start.3 = (bf16[8,48,256]{2,1,0:T(8,128)(2,1)S(1)}, bf16[8,48,256]{2,1,0:T(8,128)(2,1)S(1)}, u32[]{:S(2)}, u32[]{:S(2)}) collective-permute-start(bf16[8,48,256]{2,1,0:T(8,128)(2,1)S(1)} %pad_maximum_fusion.6), channel_id=1, source_target_pairs={{8,16},{16,8},{9,17},{17,9},{10,18},{18,10},{11,19},{19,11},{12,20... | collective-permute-start | bytes 589832 | tf_op jit(solution)/shard_map/ppermute | solution.py:67
  49.8 22.5 %collective-permute-start.13 = (bf16[48,8,256]{2,1,0:T(8,128)(2,1)S(1)}, bf16[48,8,256]{2,1,0:T(8,128)(2,1)S(1)}, u32[]{:S(2)}, u32[]{:S(2)}) collective-permute-start(bf16[48,8,256]{2,1,0:T(8,128)(2,1)S(1)} %get-tuple-element.7), channel_id=1, source_target_pairs={{0,8},{16,24},{8,0},{24,16},{1,9},{17,25},{9,1},{25,17},{2,10},{18... | collective-permute-start | bytes 589832 | tf_op jit(solution)/shard_map/ppermute | solution.py:67
  49.9 22.4 %copy-start.3 = (bf16[3,3,256,256]{3,2,1,0:T(8,128)(2,1)S(1)}, bf16[3,3,256,256]{3,2,1,0:T(8,128)(2,1)}, u32[]{:S(2)}) copy-start(bf16[3,3,256,256]{3,2,1,0:T(8,128)(2,1)} %refs_12_.1) | copy-start | bytes 3538948
  49.9 22.4 %collective-permute-start.14 = (bf16[48,8,256]{2,1,0:T(8,128)(2,1)S(1)}, bf16[48,8,256]{2,1,0:T(8,128)(2,1)S(1)}, u32[]{:S(2)}, u32[]{:S(2)}) collective-permute-start(bf16[48,8,256]{2,1,0:T(8,128)(2,1)S(1)} %get-tuple-element.8), channel_id=1, source_target_pairs={{8,16},{16,8},{9,17},{17,9},{10,18},{18,10},{11,19},{19,11},{12,20... | collective-permute-start | bytes 589832 | tf_op jit(solution)/shard_map/ppermute | solution.py:67
  71.1 1.3 %copy-start.1 = (bf16[76,48,256]{2,1,0:T(8,128)(2,1)}, bf16[76,48,256]{2,1,0:T(8,128)(2,1)S(1)}, u32[]{:S(2)}) copy-start(bf16[76,48,256]{2,1,0:T(8,128)(2,1)S(1)} %own_first.1.refs_0_) | copy-start | bytes 5603332

commit v3 on v0

v3 whole, which is shorter than its diff:
```python
import math

import jax
import jax.numpy as jnp
import numpy as np
from jax import lax
from jax.experimental import pallas as pl
from jax.experimental.pallas import tpu as pltpu
from jax.sharding import PartitionSpec as P

AXES = ("row", "col")
BF16, F32 = jnp.bfloat16, jnp.float32
PAD = 16
STRIP = 8
HALO = 6
EDGE = 6


def routes(row_count):
    low = math.isqrt(row_count)
    first, second = {}, {}
    for r in range(row_count):
        for z in range(row_count):
            a, b, c, d = r // low, r % low, z // low, z % low
            if r == z:
                continue
            via = (r, z) if b == d else ((z, z) if a == c else (c * low + b, z))
            first[(r, z)] = via
            second.setdefault(via, []).append((z, r))
    if any(len(ends) > 1 for ends in second.values()) or len(set(first.values())) < len(first):
        return {}, {(r, z): (z, r) for r in range(row_count) for z in range(row_count) if r != z}
    return first, {via: ends[0] for via, ends in second.items()}


class Place:
    def __init__(self):
        self.rows, self.cols = lax.axis_size("row"), lax.axis_size("col")
        self.row, self.col = lax.axis_index("row"), lax.axis_index("col")
        self.core = self.col % 2
        self.up = self.row % 2
        self.diagonal = self.row == self.col // 2
        self.first, self.second = routes(self.rows)

    def chips(self, array, legs, shift=0):
        pairs = [
            (s[0] * self.cols + s[1] * 2 + k, e[0] * self.cols + e[1] * 2 + (k + shift) % 2)
            for s, e in legs.items()
            for k in range(2)
        ]
        return lax.ppermute(array, AXES, pairs)

    def hop(self, piece):
        return self.chips(piece, self.first) if self.first else piece

    def land(self, hopped, shift=0):
        return self.chips(hopped, self.second, shift)


def pairwise(array, axis, start, name):
    size = lax.axis_size(axis)
    pairs = [(i, i + 1) for i in range(start, size - 1, 2)]
    if not pairs:
        return jnp.zeros_like(array)
    with jax.named_scope(name):
        return lax.ppermute(array, axis, pairs + [(j, i) for i, j in pairs])


def widen(wide, padded, start, width, step):
    channels = padded.shape[2]
    for q in range(3):
        at = start + q * step
        wide[:, :, q * channels : (q + 1) * channels] = padded[:, at : at + width, :]


def products(wide, weight, row, rows, step, flip=False):
    width, channels = wide.shape[1], wide.shape[2] // 3
    taps = [
        wide[pl.ds(row + p * step, rows), :, q * channels : (q + 1) * channels].reshape(
            rows * width, channels
        )
        for p in range(3)
        for q in range(3)
    ]
    if flip:
        taps = [taps[q * 3 + p] for p in range(3) for q in range(3)]
    flat = weight[...].reshape(9 * channels, weight.shape[3])
    return jnp.maximum(jnp.dot(jnp.concatenate(taps, axis=1), flat, preferred_element_type=F32), 0.0)


def stage_kernel(source, out, done):
    copy = pltpu.make_async_copy(source, out, done)
    copy.start()
    copy.wait()


def first_kernel(half, tile, above, below, before, after, weight, out, padded, wide, *, step):
    tile_rows, tile_cols, channels = tile.shape
    rows = out.shape[0]
    end = PAD + tile_cols
    top = half[0] * rows
    padded[1 : 1 + tile_rows, PAD:end, :] = tile[...]
    padded[0, PAD:end, :] = above[...]
    padded[1 + tile_rows, PAD:end, :] = below[...]
    padded[:, PAD - 1 : PAD, :] = before[...].reshape(tile_rows + 2, 1, channels)
    padded[:, end : end + 1, :] = after[...].reshape(tile_rows + 2, 1, channels)
    widen(wide, padded.at[pl.ds(top, rows + 2)], PAD - 1, tile_cols, 1)
    for at in range(0, rows, step):
        value = products(wide, weight, at, step, 1)
        out[at : at + step] = value.astype(BF16).reshape(step, tile_cols, channels)


def mean_kernel(mine, other, swapped, got0, got1, got2, out, block):
    row, col = lax.axis_index("row"), lax.axis_index("col")
    core = col % 2
    diagonal = row == col // 2
    size = mine.shape[0]
    lead = got0.shape[0]
    rest = size - lead

    @pl.when(diagonal)
    def _():
        block[0] = mine[...]
        block[1] = swapped[...]

    @pl.when(jnp.logical_not(diagonal))
    def _():
        block[0, :lead] = got0[...]
        block[0, lead:] = got1[:rest]
        block[1, : lead - rest] = got1[rest:]
        block[1, lead - rest :] = got2[...]

    for i, (half, first) in enumerate(((core, mine), (1 - core, other))):
        turned = jnp.swapaxes(block[i], 0, 1).astype(F32)
        out[pl.ds(half * size, size)] = ((first[...].astype(F32) + turned) * 0.5).astype(BF16)


def second_rows(wide, weight, at, rows, valid):
    a = products(wide, weight, at, rows, 2).astype(BF16).astype(F32)
    b = products(wide, weight, at, rows, 2, flip=True).astype(BF16).astype(F32)
    mean = ((a + b) * 0.5).reshape(rows, wide.shape[1], -1)
    return jnp.where(valid, mean, 0.0).astype(BF16)


def columns_inside(width, tile_cols):
    col = lax.axis_index("col")
    x = col * tile_cols - (width - tile_cols) // 2 + lax.broadcasted_iota(jnp.int32, (1, width, 1), 1)
    return (x >= 0) & (x < tile_cols * lax.axis_size("col"))


def middle_kernel(
    sym, before, after, w_second, w_third, features, tops, bottoms, padded, wide2, sym2, wide3, out, done, *, steps
):
    tile_rows, tile_cols, channels = sym.shape
    end = PAD + tile_cols
    padded[:, PAD:end, :] = sym[...]
    padded[:, PAD - STRIP : PAD, :] = before[...]
    padded[:, end : end + STRIP, :] = after[...]
    width = wide2.shape[1]
    side = (width - tile_cols) // 2
    widen(wide2, padded, PAD - side - 2, width, 2)
    valid = columns_inside(width, tile_cols)
    rows2, rows3 = sym2.shape[0], out.shape[0]

    def seconds(i, _):
        at = i * steps[0]
        sym2[pl.ds(at, steps[0])] = second_rows(wide2, w_second, at, steps[0], valid)
        return 0

    lax.fori_loop(0, rows2 // steps[0], seconds, 0)
    tops[...] = sym2[0:STRIP]
    bottoms[...] = sym2[rows2 - STRIP : rows2]
    widen(wide3, sym2, side - 4, tile_cols, 4)

    def thirds(i, _):
        at = i * steps[1]
        value = products(wide3, w_third, at, steps[1], 4)
        out[pl.ds(at, steps[1])] = value.astype(BF16).reshape(steps[1], tile_cols, channels)
        return 0

    lax.fori_loop(0, rows3 // steps[1], thirds, 0)
    copy = pltpu.make_async_copy(out, features.at[pl.ds(EDGE, rows3)], done)
    copy.start()
    copy.wait()


def edges_kernel(
    _, sym, before, after, above, below, tops, bottoms, w_second, w_third, features,
    padded, wide2, sym2, wide3, out, done,
):
    row = lax.axis_index("row")
    tile_rows, tile_cols, channels = sym.shape
    end = PAD + tile_cols
    width = wide2.shape[1]
    side = (width - tile_cols) // 2
    valid = columns_inside(width, tile_cols)
    near = padded.shape[0] - HALO
    for i in range(2):
        rows = pl.ds(HALO, near) if i == 0 else pl.ds(0, near)
        outside = pl.ds(0, HALO) if i == 0 else pl.ds(near, HALO)
        source = pl.ds(0, near) if i == 0 else pl.ds(tile_rows - near, near)
        padded[rows, PAD:end, :] = sym[source]
        padded[rows, PAD - STRIP : PAD, :] = before[source]
        padded[rows, end : end + STRIP, :] = after[source]
        padded[outside, PAD - STRIP : end + STRIP, :] = (above if i == 0 else below)[...]
        widen(wide2, padded, PAD - side - 2, width, 2)
        y = lax.broadcasted_iota(jnp.int32, (HALO, 1, 1), 0)
        if i == 0:
            inside = row * tile_rows - 4 + y >= 0
        else:
            inside = (row + 1) * tile_rows - 2 + y < tile_rows * lax.axis_size("row")
        value = second_rows(wide2, w_second, 0, HALO, valid & inside)
        if i == 0:
            sym2[0:HALO], sym2[HALO:] = value, tops[...]
        else:
            sym2[0:STRIP], sym2[STRIP:] = bottoms[...], value
        widen(wide3, sym2, side - 4, tile_cols, 4)
        value = products(wide3, w_third, 0, EDGE, 4)
        out[i] = value.astype(BF16).reshape(EDGE, tile_cols, channels)
        target = features.at[pl.ds(0 if i == 0 else tile_rows - EDGE, EDGE)]
        pltpu.make_async_copy(out.at[i], target, done.at[i]).start()
    for i in range(2):
        target = features.at[pl.ds(0 if i == 0 else tile_rows - EDGE, EDGE)]
        pltpu.make_async_copy(out.at[i], target, done.at[i]).wait()


def whole(count):
    return [pl.BlockSpec(memory_space=pltpu.VMEM)] * count


def divisor(number, most):
    return max(d for d in range(1, most + 1) if number % d == 0)


def cut(array, at, size, dim):
    return lax.dynamic_slice_in_dim(array, at, size, dim)


def local(contacts, w_first, w_second, w_third):
    tile_rows, tile_cols, channels = contacts.shape
    place = Place()
    core, up = place.core, place.up
    params = pltpu.CompilerParams(vmem_limit_bytes=32 * 2**20)
    anywhere = pl.BlockSpec(memory_space=pl.ANY)

    def shape(*dims):
        return jax.ShapeDtypeStruct((*dims, channels), BF16)

    def scratch(*dims):
        return pltpu.VMEM(dims, BF16)

    def cost(pixels):
        macs = pixels * 9 * channels * channels
        return pl.CostEstimate(flops=2 * macs, bytes_accessed=9 * channels * channels * 2, transcendentals=0)

    tile = pl.pallas_call(
        stage_kernel,
        out_shape=shape(tile_rows, tile_cols),
        in_specs=[anywhere],
        out_specs=whole(1)[0],
        scratch_shapes=[pltpu.SemaphoreType.DMA],
        compiler_params=params,
        name="stage",
    )(contacts)

    ends = [tile[0], tile[tile_rows - 1]]
    band_near = pairwise(jnp.where(up == 0, ends[1], ends[0]), "row", 0, "own_band_near")
    band_far = pairwise(jnp.where(up == 0, ends[0], ends[1]), "row", 1, "own_band_far")
    above, below = jnp.where(up == 0, band_far, band_near), jnp.where(up == 0, band_near, band_far)
    ends = [
        jnp.concatenate([above[x : x + 1], tile[:, x], below[x : x + 1]]) for x in (0, tile_cols - 1)
    ]
    near = pairwise(jnp.where(core == 0, ends[1], ends[0]), "col", 0, "own_near")
    far = pairwise(jnp.where(core == 0, ends[0], ends[1]), "col", 1, "own_far")
    before, after = jnp.where(core == 0, far, near), jnp.where(core == 0, near, far)

    def first_of(half):
        return pl.pallas_call(
            lambda *refs: first_kernel(*refs, step=tile_cols // 2),
            out_shape=shape(tile_cols, tile_cols),
            in_specs=[pl.BlockSpec(memory_space=pltpu.SMEM)] + whole(6),
            out_specs=whole(1)[0],
            scratch_shapes=[
                scratch(tile_rows + 2, tile_cols + 2 * PAD, channels),
                scratch(tile_cols + 2, tile_cols, 3 * channels),
            ],
            compiler_params=params,
            cost_estimate=cost(tile_cols * tile_cols),
            name="first",
        )(half.reshape(1), tile, above, below, before, after, w_first)

    mine, other = first_of(core), first_of(1 - core)
    lead = tile_cols * 11 // 16
    with jax.named_scope("hop0"):
        hop0 = place.hop(mine[:lead])
    swapped = pairwise(other, "col", 0, "swap")
    with jax.named_scope("hop1"):
        hop1 = place.hop(jnp.concatenate([mine[lead:], swapped[: 2 * lead - tile_cols]]))
    with jax.named_scope("hop2"):
        hop2 = place.hop(swapped[2 * lead - tile_cols :])
    with jax.named_scope("land0"):
        got0 = place.land(hop0)
    with jax.named_scope("land1"):
        got1 = place.land(hop1)
    with jax.named_scope("land2"):
        got2 = place.land(hop2)
    sym = pl.pallas_call(
        mean_kernel,
        out_shape=shape(tile_rows, tile_cols),
        in_specs=whole(6),
        out_specs=whole(1)[0],
        scratch_shapes=[scratch(2, tile_cols, tile_cols, channels)],
        compiler_params=params,
        name="mean",
    )(mine, other, swapped, got0, got1, got2)

    last = tile_cols - STRIP
    near = pairwise(cut(sym, (1 - core) * last, STRIP, 1), "col", 0, "sym_near")
    far = pairwise(cut(sym, core * last, STRIP, 1), "col", 1, "sym_far")
    before, after = jnp.where(core == 0, far, near), jnp.where(core == 0, near, far)

    def band(at):
        return jnp.concatenate([cut(part, at, HALO, 0) for part in (before, sym, after)], axis=1)

    last = tile_rows - HALO
    band_near = pairwise(band((1 - up) * last), "row", 0, "sym_band_near")
    band_far = pairwise(band(up * last), "row", 1, "sym_band_far")
    width = tile_cols + 2 * STRIP
    rows2, rows3 = tile_rows - 4, tile_rows - 2 * EDGE
    features, tops, bottoms = pl.pallas_call(
        lambda *refs: middle_kernel(*refs, steps=(divisor(rows2, 20), divisor(rows3, 26))),
        out_shape=(shape(tile_rows, tile_cols), shape(STRIP, width), shape(STRIP, width)),
        in_specs=whole(5),
        out_specs=(anywhere, *whole(2)),
        scratch_shapes=[
            scratch(tile_rows, tile_cols + 2 * PAD, channels),
            scratch(tile_rows, width, 3 * channels),
            scratch(rows2, width, channels),
            scratch(rows2, tile_cols, 3 * channels),
            scratch(rows3, tile_cols, channels),
            pltpu.SemaphoreType.DMA,
        ],
        compiler_params=params,
        cost_estimate=cost(2 * rows2 * width + rows3 * tile_cols),
        name="middle",
    )(sym, before, after, w_second, w_third)
    above, below = jnp.where(up == 0, band_far, band_near), jnp.where(up == 0, band_near, band_far)
    return pl.pallas_call(
        edges_kernel,
        out_shape=shape(tile_rows, tile_cols),
        in_specs=[anywhere] + whole(9),
        out_specs=anywhere,
        scratch_shapes=[
            scratch(HALO + 4, tile_cols + 2 * PAD, channels),
            scratch(HALO + 4, width, 3 * channels),
            scratch(HALO + STRIP, width, channels),
            scratch(HALO + STRIP, tile_cols, 3 * channels),
            scratch(2, EDGE, tile_cols, channels),
            pltpu.SemaphoreType.DMA((2,)),
        ],
        input_output_aliases={0: 0},
        compiler_params=params,
        cost_estimate=cost(2 * 2 * HALO * width + 2 * EDGE * tile_cols),
        name="edges",
    )(features, sym, before, after, above, below, tops, bottoms, w_second, w_third)


def solution(mesh):
    return jax.shard_map(
        local,
        mesh=mesh,
        in_specs=(P("row", "col", None), P(), P(), P()),
        out_specs=P("row", "col", None),
        check_vma=False,
    )
```

time: 202 us -> 91.3 us (0.45); the launches traced: 199 us -> 90.4 us
  blocking collectives: 124 us -> 0 us
  waiting for transfers between devices: 8.5 us -> 28.6 us
  Pallas kernels: 0 us -> 18.4 us
  matrix products: 8.84 us -> 0 us
  other arithmetic: 6.7 us -> 1.21 us
  local copies, waits for them, and re-layouts: 10.5 us -> 5.31 us
  starting transfers between devices: 39.9 us -> 36.5 us
    all_to_all x6 -> x0, blocking collectives: 124 us -> none  [the longest x2 60.5 us: transposed(): lax.all_to_all(pieces, 'col', split_axis=0, concat_axis=0, tiled=True)]
    ppermute x12 -> x15, waiting for transfers between devices: 8.5 us -> 28.6 us  [the longest x6 18.9 us: chips(): return lax.ppermute(array, AXES, pairs)]
    pallas_call x0 -> x6, Pallas kernels: none -> 18.4 us  [the longest x1 11.4 us: local(): pl.pallas_call(lambda *refs: middle_kernel(*refs, steps=(divisor(rows2, 2...]
    dot_general x3 -> x0, matrix products: 8.84 us -> none  [conv_layer(): jnp.dot(stacked, weight.reshape(9 * channels, weight.shape[3]), preferred...]
    ppermute x12 -> x15, starting transfers between devices: 39.9 us -> 36.5 us  [the longest x9 24.7 us: pairwise(): return lax.ppermute(array, axis, pairs + [(j, i) for i, j in pairs])]
    unnamed x11 -> x0, other arithmetic: 3.08 us -> none
    convert_element_type x4 -> x0, local copies, waits for them, and re-layouts: 2.81 us -> none  [symmetrize(): mirrored.astype(jnp.float32)]
    concatenate x5 -> x3, other arithmetic: 2.71 us -> 0.06 us  [the longest x1 0.03 us: local(): jnp.concatenate([mine[lead:], swapped[:2 * lead - tile_cols]])]
  transfers between devices with their start and end apart: 12 -> 15, of which waited for: 5 -> 5; matrix products, arithmetic and copies ran while one was open for 1% -> 0% of each run, Pallas kernels for 0% -> 14%
where the time goes in v3:
time: 91.3 us; the launch traced here: 90.4 us
  starting transfers between devices  36.5 us (40%)
  waiting for transfers between devices  28.6 us (31%)
  Pallas kernels  18.4 us (20%)
  local copies, waits for them, and re-layouts  5.31 us (6%)
  other arithmetic  1.21 us (1%)
    ppermute x9, starting transfers between devices, pairwise(): return lax.ppermute(array, axis, pairs + [(j, i) for i, j in pairs])  24.7 us
    ppermute x6, waiting for transfers between devices, chips(): return lax.ppermute(array, AXES, pairs)  18.9 us
    ppermute x6, starting transfers between devices, chips(): return lax.ppermute(array, AXES, pairs)  11.7 us
    pallas_call x1, Pallas kernels, local(): pl.pallas_call(lambda *refs: middle_kernel(*refs, steps=(divisor(rows2, 2...  11.4 us
    ppermute x9, waiting for transfers between devices, pairwise(): return lax.ppermute(array, axis, pairs + [(j, i) for i, j in pairs])  9.76 us
    unnamed x14, local copies, waits for them, and re-layouts  4.2 us
    pallas_call x2, Pallas kernels, first_of(): pl.pallas_call(lambda *refs: first_kernel(*refs, step=tile_cols // 2), ou...  3.26 us
    pallas_call x1, Pallas kernels, local(): pl.pallas_call(edges_kernel, out_shape=shape(tile_rows, tile_cols), in_sp...  3.07 us
  transfers between devices with their start and end apart: 15, of which 5 were waited for; matrix products, arithmetic and copies ran while one was open for 0% of the time, Pallas kernels for 14%

profile of v3, /device:TPU:5, one launch (start us, length us, event | category | flops | bytes accessed | tf_op | source)
XLA Modules:
  0.0 90.4 jit_solution(4485721064087299981)
XLA Ops:
  0.0 1.2 %copy-done.2 = bf16[64,32,256]{2,1,0:T(8,128)(2,1)S(1)} copy-done((bf16[64,32,256]{2,1,0:T(8,128)(2,1)S(1)}, bf16[64,32,256]{2,1,0:T(8,128)(2,1)}, u32[]{:S(2)}) %copy-start.2) | copy-done | bytes 1048600
  1.2 0.1 stage.1.refs_1_
  1.3 1.3 %collective-permute-start.1 = (bf16[32,256]{1,0:T(8,128)(2,1)S(1)}, bf16[32,256]{1,0:T(8,128)(2,1)S(1)}, u32[]{:S(2)}, u32[]{:S(2)}) collective-permute-start(bf16[32,256]{1,0:T(8,128)(2,1)S(1)} %get-tuple-element.17), channel_id=1, source_target_pairs={{0,8},{16,24},{8,0},{24,16},{1,9},{17,25},{9,1},{25,17},{2,10},{18... | collective-permute-start | bytes 49160 | tf_op jit(solution)/shard_map/own_band_near/ppermute | solution.py:65
  2.6 1.9 %collective-permute-start = (bf16[32,256]{1,0:T(8,128)(2,1)S(1)}, bf16[32,256]{1,0:T(8,128)(2,1)S(1)}, u32[]{:S(2)}, u32[]{:S(2)}) collective-permute-start(bf16[32,256]{1,0:T(8,128)(2,1)S(1)} %get-tuple-element.18), channel_id=1, source_target_pairs={{8,16},{16,8},{9,17},{17,9},{10,18},{18,10},{11,19},{19,11},{12,20... | collective-permute-start | bytes 49160 | tf_op jit(solution)/shard_map/own_band_far/ppermute | solution.py:65
  4.5 0.1 fusion
  4.7 3.3 %collective-permute-done = bf16[32,256]{1,0:T(8,128)(2,1)S(1)} collective-permute-done((bf16[32,256]{1,0:T(8,128)(2,1)S(1)}, bf16[32,256]{1,0:T(8,128)(2,1)S(1)}, u32[]{:S(2)}, u32[]{:S(2)}) %collective-permute-start) | collective-permute-done | bytes 16416 | tf_op jit(solution)/shard_map/own_band_far/ppermute | solution.py:65
  8.0 2.2 %collective-permute-start.3 = (bf16[66,256]{1,0:T(8,128)(2,1)S(1)}, bf16[66,256]{1,0:T(8,128)(2,1)S(1)}, u32[]{:S(2)}, u32[]{:S(2)}) collective-permute-start(bf16[66,256]{1,0:T(8,128)(2,1)S(1)} %get-tuple-element.29), channel_id=1, source_target_pairs={{0,1},{2,3},{4,5},{6,7},{1,0},{3,2},{5,4},{7,6},{8,9},{10,11},{12,... | collective-permute-start | bytes 101384 | tf_op jit(solution)/shard_map/own_near/ppermute | solution.py:65
  10.2 3.1 %collective-permute-start.2 = (bf16[66,256]{1,0:T(8,128)(2,1)S(1)}, bf16[66,256]{1,0:T(8,128)(2,1)S(1)}, u32[]{:S(2)}, u32[]{:S(2)}) collective-permute-start(bf16[66,256]{1,0:T(8,128)(2,1)S(1)} %get-tuple-element.30), channel_id=1, source_target_pairs={{1,2},{3,4},{5,6},{2,1},{4,3},{6,5},{9,10},{11,12},{13,14},{10,9},... | collective-permute-start | bytes 101384 | tf_op jit(solution)/shard_map/own_far/ppermute | solution.py:65
  13.3 2.1 %collective-permute-done.2 = bf16[66,256]{1,0:T(8,128)(2,1)S(1)} collective-permute-done((bf16[66,256]{1,0:T(8,128)(2,1)S(1)}, bf16[66,256]{1,0:T(8,128)(2,1)S(1)}, u32[]{:S(2)}, u32[]{:S(2)}) %collective-permute-start.2) | collective-permute-done | bytes 33824 | tf_op jit(solution)/shard_map/own_far/ppermute | solution.py:65
  15.5 1.3 %copy-done.5 = bf16[3,3,256,256]{3,2,1,0:T(8,128)(2,1)S(1)} copy-done((bf16[3,3,256,256]{3,2,1,0:T(8,128)(2,1)S(1)}, bf16[3,3,256,256]{3,2,1,0:T(8,128)(2,1)}, u32[]{:S(2)}) %copy-start.5) | copy-done | bytes 1179672
  16.8 1.6 %first.3.other = bf16[32,32,256]{2,1,0:T(8,128)(2,1)S(1)} custom-call(s32[1]{0:T(128)} %bitcast.5.refs_0_, bf16[64,32,256]{2,1,0:T(8,128)(2,1)S(1)} %stage.1.refs_1_, bf16[32,256]{1,0:T(8,128)(2,1)S(1)} %get-tuple-element.32.refs_2_, bf16[32,256]{1,0:T(8,128)(2,1)S(1)} %get-tuple-element.31.refs_3_, bf16[66,256]{1,0:T(8,128)(2,1)S(1)} %get-tuple-element.28.refs_4_, ...), custom_call_target="tpu_custom_call" | custom-call | flops 1207959552 | bytes 1179648 | tf_op jit(solution)/shard_map/first/pallas_call | solution.py:277
  18.5 1.6 %first.2.mine = bf16[32,32,256]{2,1,0:T(8,128)(2,1)S(1)} custom-call(s32[1]{0:T(128)} %bitcast.refs_0_, bf16[64,32,256]{2,1,0:T(8,128)(2,1)S(1)} %stage.1.refs_1_, bf16[32,256]{1,0:T(8,128)(2,1)S(1)} %get-tuple-element.32.refs_2_, bf16[32,256]{1,0:T(8,128)(2,1)S(1)} %get-tuple-element.31.refs_3_, bf16[66,256]{1,0:T(8,128)(2,1)S(1)} %get-tuple-element.28.refs_4_, ...), custom_call_target="tpu_custom_call" | custom-call | flops 1207959552 | bytes 1179648 | tf_op jit(solution)/shard_map/first/pallas_call | solution.py:277
  20.2 0.7 collective-permute-start.5
  20.9 0.7 collective-permute-start.7
  21.7 1.4 %collective-permute-start.9 = (bf16[20,32,256]{2,1,0:T(8,128)(2,1)S(1)}, bf16[20,32,256]{2,1,0:T(8,128)(2,1)}, u32[]{:S(2)}, u32[]{:S(2)}) collective-permute-start(bf16[20,32,256]{2,1,0:T(8,128)(2,1)S(1)} %slice.59), channel_id=1, source_target_pairs={{2,10},{3,11},{4,4},{5,5},{6,22},{7,23},{8,0},{9,1},{12,28},{13,29... | collective-permute-start | bytes 983048 | tf_op jit(solution)/shard_map/hop2/ppermute | solution.py:50
  23.1 1.9 %collective-permute-start.6 = (bf16[22,32,256]{2,1,0:T(8,128)(2,1)S(1)}, bf16[22,32,256]{2,1,0:T(8,128)(2,1)S(1)}, u32[]{:S(2)}, u32[]{:S(2)}) collective-permute-start(bf16[22,32,256]{2,1,0:T(8,128)(2,1)S(1)} %collective-permute-done.5), channel_id=1, source_target_pairs={{10,8},{11,9},{4,16},{5,17},{22,24},{23,25},{0,2},{1,3},{28,18},{2... | collective-permute-start | bytes 1081352 | tf_op jit(solution)/shard_map/land0/ppermute | solution.py:50
  25.0 5.2 %collective-permute-start.8 = (bf16[22,32,256]{2,1,0:T(8,128)(2,1)S(1)}, bf16[22,32,256]{2,1,0:T(8,128)(2,1)S(1)}, u32[]{:S(2)}, u32[]{:S(2)}) collective-permute-start(bf16[22,32,256]{2,1,0:T(8,128)(2,1)S(1)} %collective-permute-done.7), channel_id=1, source_target_pairs={{10,8},{11,9},{4,16},{5,17},{22,24},{23,25},{0,2},{1,3},{28,18},{2... | collective-permute-start | bytes 1081352 | tf_op jit(solution)/shard_map/land1/ppermute | solution.py:50
  30.2 1.9 %collective-permute-start.10 = (bf16[20,32,256]{2,1,0:T(8,128)(2,1)}, bf16[20,32,256]{2,1,0:T(8,128)(2,1)S(1)}, u32[]{:S(2)}, u32[]{:S(2)}) collective-permute-start(bf16[20,32,256]{2,1,0:T(8,128)(2,1)} %collective-permute-done.9), channel_id=1, source_target_pairs={{10,8},{11,9},{4,16},{5,17},{22,24},{23,25},{0,2},{1,3},{28,18},{2... | collective-permute-start | bytes 983048 | tf_op jit(solution)/shard_map/land2/ppermute | solution.py:50
  32.1 4.1 %collective-permute-done.6.got0 = bf16[22,32,256]{2,1,0:T(8,128)(2,1)S(1)} collective-permute-done((bf16[22,32,256]{2,1,0:T(8,128)(2,1)S(1)}, bf16[22,32,256]{2,1,0:T(8,128)(2,1)S(1)}, u32[]{:S(2)}, u32[]{:S(2)}) %collective-permute-start.6) | collective-permute-done | bytes 360480 | tf_op jit(solution)/shard_map/land0/ppermute | solution.py:50
  36.2 14.7 %collective-permute-done.10.got2 = bf16[20,32,256]{2,1,0:T(8,128)(2,1)S(1)} collective-permute-done((bf16[20,32,256]{2,1,0:T(8,128)(2,1)}, bf16[20,32,256]{2,1,0:T(8,128)(2,1)S(1)}, u32[]{:S(2)}, u32[]{:S(2)}) %collective-permute-start.10) | collective-permute-done | bytes 327712 | tf_op jit(solution)/shard_map/land2/ppermute | solution.py:50
  51.0 0.7 copy-done.3
  51.7 1.0 %copy-done.4 = bf16[20,32,256]{2,1,0:T(8,128)(2,1)S(1)} copy-done((bf16[20,32,256]{2,1,0:T(8,128)(2,1)S(1)}, bf16[20,32,256]{2,1,0:T(8,128)(2,1)}, u32[]{:S(2)}) %copy-start.4) | copy-done | bytes 327704
  52.7 0.6 mean.1.refs_0_.sym
  53.3 0.9 constant_dynamic-slice_fusion.6
  54.2 1.3 %collective-permute-start.12 = (bf16[64,8,256]{2,1,0:T(8,128)(2,1)}, bf16[64,8,256]{2,1,0:T(8,128)(2,1)}, u32[]{:S(2)}, u32[]{:S(2)}) collective-permute-start(bf16[64,8,256]{2,1,0:T(8,128)(2,1)} %get-tuple-element.13), channel_id=1, source_target_pairs={{0,1},{2,3},{4,5},{6,7},{1,0},{3,2},{5,4},{7,6},{8,9},{10,11},{12,... | collective-permute-start | bytes 786440 | tf_op jit(solution)/shard_map/sym_near/ppermute | solution.py:65
  55.5 8.8 %collective-permute-start.11 = (bf16[64,8,256]{2,1,0:T(8,128)(2,1)}, bf16[64,8,256]{2,1,0:T(8,128)(2,1)}, u32[]{:S(2)}, u32[]{:S(2)}) collective-permute-start(bf16[64,8,256]{2,1,0:T(8,128)(2,1)} %get-tuple-element.14), channel_id=1, source_target_pairs={{1,2},{3,4},{5,6},{2,1},{4,3},{6,5},{9,10},{11,12},{13,14},{10,9},... | collective-permute-start | bytes 786440 | tf_op jit(solution)/shard_map/sym_far/ppermute | solution.py:65
  64.3 4.3 %collective-permute-done.11 = bf16[64,8,256]{2,1,0:T(8,128)(2,1)} collective-permute-done((bf16[64,8,256]{2,1,0:T(8,128)(2,1)}, bf16[64,8,256]{2,1,0:T(8,128)(2,1)}, u32[]{:S(2)}, u32[]{:S(2)}) %collective-permute-start.11) | collective-permute-done | bytes 262176 | tf_op jit(solution)/shard_map/sym_far/ppermute | solution.py:65
  68.6 1.1 %broadcast_select_fusion = (bf16[64,8,256]{2,1,0:T(8,128)(2,1)S(1)}, bf16[64,8,256]{2,1,0:T(8,128)(2,1)S(1)}) fusion(bf16[64,8,256]{2,1,0:T(8,128)(2,1)} %collective-permute-done.12, bf16[64,8,256]{2,1,0:T(8,128)(2,1)} %collective-permute-done.11, pred[]{:T(512)S(6)} %eq.8), kind=kLoop, calls=%fused_computation.1 | loop fusion | flops 262144 | bytes 1048577 | tf_op jit(solution)/shard_map/jit(_where)/select_n | solution.py:319
  69.8 5.4 %collective-permute-start.13 = (bf16[6,48,256]{2,1,0:T(8,128)(2,1)S(1)}, bf16[6,48,256]{2,1,0:T(8,128)(2,1)S(1)}, u32[]{:S(2)}, u32[]{:S(2)}) collective-permute-start(bf16[6,48,256]{2,1,0:T(8,128)(2,1)S(1)} %pad_maximum_fusion.1), channel_id=1, source_target_pairs={{8,16},{16,8},{9,17},{17,9},{10,18},{18,10},{11,19},{19,11},{12,20... | collective-permute-start | bytes 442376 | tf_op jit(solution)/shard_map/sym_band_far/ppermute | solution.py:65
  75.2 0.7 collective-permute-start.14
  75.9 11.4 %middle.1 = (bf16[64,32,256]{2,1,0:T(8,128)(2,1)}, bf16[8,48,256]{2,1,0:T(8,128)(2,1)S(1)}, bf16[8,48,256]{2,1,0:T(8,128)(2,1)S(1)}) custom-call(bf16[64,32,256]{2,1,0:T(8,128)(2,1)S(1)} %mean.1.refs_0_.sym, bf16[64,8,256]{2,1,0:T(8,128)(2,1)S(1)} %get-tuple-element.20.refs_1_.before, bf16[64,8,256]{2,1,0:T(8,128)(2,1)S(1)} %get-tuple-element.19.refs_2_.after, ...), custom_call_target="tpu_custom_call" | custom-call | flops 8757706752 | bytes 1179648 | tf_op jit(solution)/shard_map/middle/pallas_call | solution.py:329
  87.3 3.1 %edges.1 = bf16[64,32,256]{2,1,0:T(8,128)(2,1)} custom-call(bf16[64,32,256]{2,1,0:T(8,128)(2,1)} %get-tuple-element.8._, bf16[64,32,256]{2,1,0:T(8,128)(2,1)S(1)} %mean.1.refs_0_.sym, bf16[64,8,256]{2,1,0:T(8,128)(2,1)S(1)} %get-tuple-element.20.refs_1_.before, ...), custom_call_target="tpu_custom_call", output_to_operand_aliasing={{}: (0, {})} | custom-call | flops 1811939328 | bytes 1179648 | tf_op jit(solution)/shard_map/edges/pallas_call | solution.py:347
  (38 shorter events, 0.4 us)
Async XLA Ops:
  0.0 1.2 %copy-start.2 = (bf16[64,32,256]{2,1,0:T(8,128)(2,1)S(1)}, bf16[64,32,256]{2,1,0:T(8,128)(2,1)}, u32[]{:S(2)}) copy-start(bf16[64,32,256]{2,1,0:T(8,128)(2,1)} %source.1) | copy-start | bytes 3145732
  1.3 3.3 %collective-permute-start.1 = (bf16[32,256]{1,0:T(8,128)(2,1)S(1)}, bf16[32,256]{1,0:T(8,128)(2,1)S(1)}, u32[]{:S(2)}, u32[]{:S(2)}) collective-permute-start(bf16[32,256]{1,0:T(8,128)(2,1)S(1)} %get-tuple-element.17), channel_id=1, source_target_pairs={{0,8},{16,24},{8,0},{24,16},{1,9},{17,25},{9,1},{25,17},{2,10},{18... | collective-permute-start | bytes 49160 | tf_op jit(solution)/shard_map/own_band_near/ppermute | solution.py:65
  2.6 5.4 %collective-permute-start = (bf16[32,256]{1,0:T(8,128)(2,1)S(1)}, bf16[32,256]{1,0:T(8,128)(2,1)S(1)}, u32[]{:S(2)}, u32[]{:S(2)}) collective-permute-start(bf16[32,256]{1,0:T(8,128)(2,1)S(1)} %get-tuple-element.18), channel_id=1, source_target_pairs={{8,16},{16,8},{9,17},{17,9},{10,18},{18,10},{11,19},{19,11},{12,20... | collective-permute-start | bytes 49160 | tf_op jit(solution)/shard_map/own_band_far/ppermute | solution.py:65
  8.0 5.3 %collective-permute-start.3 = (bf16[66,256]{1,0:T(8,128)(2,1)S(1)}, bf16[66,256]{1,0:T(8,128)(2,1)S(1)}, u32[]{:S(2)}, u32[]{:S(2)}) collective-permute-start(bf16[66,256]{1,0:T(8,128)(2,1)S(1)} %get-tuple-element.29), channel_id=1, source_target_pairs={{0,1},{2,3},{4,5},{6,7},{1,0},{3,2},{5,4},{7,6},{8,9},{10,11},{12,... | collective-permute-start | bytes 101384 | tf_op jit(solution)/shard_map/own_near/ppermute | solution.py:65
  10.2 5.3 %collective-permute-start.2 = (bf16[66,256]{1,0:T(8,128)(2,1)S(1)}, bf16[66,256]{1,0:T(8,128)(2,1)S(1)}, u32[]{:S(2)}, u32[]{:S(2)}) collective-permute-start(bf16[66,256]{1,0:T(8,128)(2,1)S(1)} %get-tuple-element.30), channel_id=1, source_target_pairs={{1,2},{3,4},{5,6},{2,1},{4,3},{6,5},{9,10},{11,12},{13,14},{10,9},... | collective-permute-start | bytes 101384 | tf_op jit(solution)/shard_map/own_far/ppermute | solution.py:65
  15.5 1.3 %copy-start.5 = (bf16[3,3,256,256]{3,2,1,0:T(8,128)(2,1)S(1)}, bf16[3,3,256,256]{3,2,1,0:T(8,128)(2,1)}, u32[]{:S(2)}) copy-start(bf16[3,3,256,256]{3,2,1,0:T(8,128)(2,1)} %refs_6_.3) | copy-start | bytes 3538948
  16.8 1.7 %copy-start.6 = (bf16[3,3,256,256]{3,2,1,0:T(8,128)(2,1)S(1)}, bf16[3,3,256,256]{3,2,1,0:T(8,128)(2,1)}, u32[]{:S(2)}) copy-start(bf16[3,3,256,256]{3,2,1,0:T(8,128)(2,1)} %refs_6_.3) | copy-start | bytes 3538948
  18.4 2.5 %collective-permute-start.4 = (bf16[32,32,256]{2,1,0:T(8,128)(2,1)S(1)}, bf16[32,32,256]{2,1,0:T(8,128)(2,1)S(1)}, u32[]{:S(2)}, u32[]{:S(2)}) collective-permute-start(bf16[32,32,256]{2,1,0:T(8,128)(2,1)S(1)} %first.3.other), channel_id=1, source_target_pairs={{0,1},{2,3},{4,5},{6,7},{1,0},{3,2},{5,4},{7,6},{8,9},{10,11},{12,... | collective-permute-start | bytes 1572872 | tf_op jit(solution)/shard_map/swap/ppermute | solution.py:65
  20.2 2.9 %collective-permute-start.5 = (bf16[22,32,256]{2,1,0:T(8,128)(2,1)S(1)}, bf16[22,32,256]{2,1,0:T(8,128)(2,1)S(1)}, u32[]{:S(2)}, u32[]{:S(2)}) collective-permute-start(bf16[22,32,256]{2,1,0:T(8,128)(2,1)S(1)} %slice.56), channel_id=1, source_target_pairs={{2,10},{3,11},{4,4},{5,5},{6,22},{7,23},{8,0},{9,1},{12,28},{13,29... | collective-permute-start | bytes 1081352 | tf_op jit(solution)/shard_map/hop0/ppermute | solution.py:50
  20.9 4.0 %collective-permute-start.7 = (bf16[22,32,256]{2,1,0:T(8,128)(2,1)S(1)}, bf16[22,32,256]{2,1,0:T(8,128)(2,1)S(1)}, u32[]{:S(2)}, u32[]{:S(2)}) collective-permute-start(bf16[22,32,256]{2,1,0:T(8,128)(2,1)S(1)} %pad_maximum_fusion), channel_id=1, source_target_pairs={{2,10},{3,11},{4,4},{5,5},{6,22},{7,23},{8,0},{9,1},{12,28},{13,29... | collective-permute-start | bytes 1081352 | tf_op jit(solution)/shard_map/hop1/ppermute | solution.py:50
  21.7 8.5 %collective-permute-start.9 = (bf16[20,32,256]{2,1,0:T(8,128)(2,1)S(1)}, bf16[20,32,256]{2,1,0:T(8,128)(2,1)}, u32[]{:S(2)}, u32[]{:S(2)}) collective-permute-start(bf16[20,32,256]{2,1,0:T(8,128)(2,1)S(1)} %slice.59), channel_id=1, source_target_pairs={{2,10},{3,11},{4,4},{5,5},{6,22},{7,23},{8,0},{9,1},{12,28},{13,29... | collective-permute-start | bytes 983048 | tf_op jit(solution)/shard_map/hop2/ppermute | solution.py:50
  23.1 13.2 %collective-permute-start.6 = (bf16[22,32,256]{2,1,0:T(8,128)(2,1)S(1)}, bf16[22,32,256]{2,1,0:T(8,128)(2,1)S(1)}, u32[]{:S(2)}, u32[]{:S(2)}) collective-permute-start(bf16[22,32,256]{2,1,0:T(8,128)(2,1)S(1)} %collective-permute-done.5), channel_id=1, source_target_pairs={{10,8},{11,9},{4,16},{5,17},{22,24},{23,25},{0,2},{1,3},{28,18},{2... | collective-permute-start | bytes 1081352 | tf_op jit(solution)/shard_map/land0/ppermute | solution.py:50
  25.0 26.7 %collective-permute-start.8 = (bf16[22,32,256]{2,1,0:T(8,128)(2,1)S(1)}, bf16[22,32,256]{2,1,0:T(8,128)(2,1)S(1)}, u32[]{:S(2)}, u32[]{:S(2)}) collective-permute-start(bf16[22,32,256]{2,1,0:T(8,128)(2,1)S(1)} %collective-permute-done.7), channel_id=1, source_target_pairs={{10,8},{11,9},{4,16},{5,17},{22,24},{23,25},{0,2},{1,3},{28,18},{2... | collective-permute-start | bytes 1081352 | tf_op jit(solution)/shard_map/land1/ppermute | solution.py:50
  30.2 20.8 %collective-permute-start.10 = (bf16[20,32,256]{2,1,0:T(8,128)(2,1)}, bf16[20,32,256]{2,1,0:T(8,128)(2,1)S(1)}, u32[]{:S(2)}, u32[]{:S(2)}) collective-permute-start(bf16[20,32,256]{2,1,0:T(8,128)(2,1)} %collective-permute-done.9), channel_id=1, source_target_pairs={{10,8},{11,9},{4,16},{5,17},{22,24},{23,25},{0,2},{1,3},{28,18},{2... | collective-permute-start | bytes 983048 | tf_op jit(solution)/shard_map/land2/ppermute | solution.py:50
  51.0 0.7 copy-start.3
  51.7 1.0 %copy-start.4 = (bf16[20,32,256]{2,1,0:T(8,128)(2,1)S(1)}, bf16[20,32,256]{2,1,0:T(8,128)(2,1)}, u32[]{:S(2)}) copy-start(bf16[20,32,256]{2,1,0:T(8,128)(2,1)} %copy-done.3) | copy-start | bytes 983044
  53.3 22.6 %copy-start.1 = (bf16[3,3,256,256]{3,2,1,0:T(8,128)(2,1)S(1)}, bf16[3,3,256,256]{3,2,1,0:T(8,128)(2,1)}, u32[]{:S(2)}) copy-start(bf16[3,3,256,256]{3,2,1,0:T(8,128)(2,1)} %w_third.1) | copy-start | bytes 3538948
  54.2 21.7 %copy-start = (bf16[3,3,256,256]{3,2,1,0:T(8,128)(2,1)S(1)}, bf16[3,3,256,256]{3,2,1,0:T(8,128)(2,1)}, u32[]{:S(2)}) copy-start(bf16[3,3,256,256]{3,2,1,0:T(8,128)(2,1)} %w_second.1) | copy-start | bytes 3538948
  54.2 10.1 %collective-permute-start.12 = (bf16[64,8,256]{2,1,0:T(8,128)(2,1)}, bf16[64,8,256]{2,1,0:T(8,128)(2,1)}, u32[]{:S(2)}, u32[]{:S(2)}) collective-permute-start(bf16[64,8,256]{2,1,0:T(8,128)(2,1)} %get-tuple-element.13), channel_id=1, source_target_pairs={{0,1},{2,3},{4,5},{6,7},{1,0},{3,2},{5,4},{7,6},{8,9},{10,11},{12,... | collective-permute-start | bytes 786440 | tf_op jit(solution)/shard_map/sym_near/ppermute | solution.py:65
  55.5 13.1 %collective-permute-start.11 = (bf16[64,8,256]{2,1,0:T(8,128)(2,1)}, bf16[64,8,256]{2,1,0:T(8,128)(2,1)}, u32[]{:S(2)}, u32[]{:S(2)}) collective-permute-start(bf16[64,8,256]{2,1,0:T(8,128)(2,1)} %get-tuple-element.14), channel_id=1, source_target_pairs={{1,2},{3,4},{5,6},{2,1},{4,3},{6,5},{9,10},{11,12},{13,14},{10,9},... | collective-permute-start | bytes 786440 | tf_op jit(solution)/shard_map/sym_far/ppermute | solution.py:65
  69.8 17.5 %collective-permute-start.13 = (bf16[6,48,256]{2,1,0:T(8,128)(2,1)S(1)}, bf16[6,48,256]{2,1,0:T(8,128)(2,1)S(1)}, u32[]{:S(2)}, u32[]{:S(2)}) collective-permute-start(bf16[6,48,256]{2,1,0:T(8,128)(2,1)S(1)} %pad_maximum_fusion.1), channel_id=1, source_target_pairs={{8,16},{16,8},{9,17},{17,9},{10,18},{18,10},{11,19},{19,11},{12,20... | collective-permute-start | bytes 442376 | tf_op jit(solution)/shard_map/sym_band_far/ppermute | solution.py:65
  75.2 12.1 %collective-permute-start.14 = (bf16[6,48,256]{2,1,0:T(8,128)(2,1)S(1)}, bf16[6,48,256]{2,1,0:T(8,128)(2,1)S(1)}, u32[]{:S(2)}, u32[]{:S(2)}) collective-permute-start(bf16[6,48,256]{2,1,0:T(8,128)(2,1)S(1)} %pad_maximum_fusion.2), channel_id=1, source_target_pairs={{0,8},{16,24},{8,0},{24,16},{1,9},{17,25},{9,1},{25,17},{2,10},{18... | collective-permute-start | bytes 442376 | tf_op jit(solution)/shard_map/sym_band_near/ppermute | solution.py:65

commit v4 on v3

v4 whole, which is shorter than its diff:
```python
import math

import jax
import jax.numpy as jnp
import numpy as np
from jax import lax
from jax.experimental import pallas as pl
from jax.experimental.pallas import tpu as pltpu
from jax.sharding import PartitionSpec as P

AXES = ("row", "col")
BF16, F32 = jnp.bfloat16, jnp.float32
PAD = 16
STRIP = 8
HALO = 6
EDGE = 6


def routes(row_count):
    low = math.isqrt(row_count)
    first, second = {}, {}
    for r in range(row_count):
        for z in range(row_count):
            a, b, c, d = r // low, r % low, z // low, z % low
            if r == z:
                continue
            via = (r, z) if b == d else ((z, z) if a == c else (c * low + b, z))
            first[(r, z)] = via
            second.setdefault(via, []).append((z, r))
    if any(len(ends) > 1 for ends in second.values()) or len(set(first.values())) < len(first):
        return {}, {(r, z): (z, r) for r in range(row_count) for z in range(row_count) if r != z}
    return first, {via: ends[0] for via, ends in second.items()}


class Place:
    def __init__(self):
        self.rows, self.cols = lax.axis_size("row"), lax.axis_size("col")
        self.row, self.col = lax.axis_index("row"), lax.axis_index("col")
        self.core = self.col % 2
        self.up = self.row % 2
        self.diagonal = self.row == self.col // 2
        self.first, self.second = routes(self.rows)

    def chips(self, array, legs, shift=0):
        pairs = [
            (s[0] * self.cols + s[1] * 2 + k, e[0] * self.cols + e[1] * 2 + (k + shift) % 2)
            for s, e in legs.items()
            for k in range(2)
        ]
        return lax.ppermute(array, AXES, pairs)

    def hop(self, piece):
        return self.chips(piece, self.first) if self.first else piece

    def land(self, hopped, shift=0):
        return self.chips(hopped, self.second, shift)


def pairwise(array, axis, start, name):
    size = lax.axis_size(axis)
    pairs = [(i, i + 1) for i in range(start, size - 1, 2)]
    if not pairs:
        return jnp.zeros_like(array)
    with jax.named_scope(name):
        return lax.ppermute(array, axis, pairs + [(j, i) for i, j in pairs])


def widen(wide, padded, start, width, step):
    channels = padded.shape[2]
    for q in range(3):
        at = start + q * step
        wide[:, :, q * channels : (q + 1) * channels] = padded[:, at : at + width, :]


def products(wide, weight, row, rows, step, flip=False):
    width, channels = wide.shape[1], wide.shape[2] // 3
    taps = [
        wide[pl.ds(row + p * step, rows), :, q * channels : (q + 1) * channels].reshape(
            rows * width, channels
        )
        for p in range(3)
        for q in range(3)
    ]
    if flip:
        taps = [taps[q * 3 + p] for p in range(3) for q in range(3)]
    flat = weight[...].reshape(9 * channels, weight.shape[3])
    return jnp.maximum(jnp.dot(jnp.concatenate(taps, axis=1), flat, preferred_element_type=F32), 0.0)


def stage_kernel(source, out, done):
    copy = pltpu.make_async_copy(source, out, done)
    copy.start()
    copy.wait()


def sides(near, far):
    core = lax.axis_index("col") % 2
    return jnp.where(core == 0, far, near), jnp.where(core == 0, near, far)


def put_tile(padded, tile, near, far):
    rows, cols, channels = tile.shape
    padded[1 : 1 + rows, PAD : PAD + cols, :] = tile[...]
    before, after = sides(near[...], far[...])
    padded[1 : 1 + rows, PAD - 1 : PAD, :] = before.reshape(rows, 1, channels)
    padded[1 : 1 + rows, PAD + cols : PAD + cols + 1, :] = after.reshape(rows, 1, channels)


def inner_first_kernel(tile, near, far, weight, out, padded, wide):
    rows, cols, channels = out.shape
    put_tile(padded, tile, near, far)
    at = lax.axis_index("col") % 2 * cols + (cols - rows) // 2
    widen(wide, padded.at[pl.ds(at, rows + 2)], PAD - 1, cols, 1)
    out[...] = products(wide, weight, 0, rows, 1).astype(BF16).reshape(rows, cols, channels)


def outer_first_kernel(tile, near, far, band_near, band_far, weight, mine, other, padded, wide):
    core, up = lax.axis_index("col") % 2, lax.axis_index("row") % 2
    rows, cols, channels = tile.shape
    put_tile(padded, tile, near, far)
    ends = slice(PAD - 1, PAD + cols + 1)
    padded[0, ends, :] = jnp.where(up == 0, band_far[...], band_near[...])
    padded[rows + 1, ends, :] = jnp.where(up == 0, band_near[...], band_far[...])
    inset = mine.shape[0] // 2
    top = core * cols
    pieces = [
        (top, inset, mine.at[:inset]),
        (top + cols - inset, inset, mine.at[inset:]),
        ((1 - core) * cols, cols, other),
    ]
    to = 0
    for at, count, _ in pieces:
        widen(wide.at[to : to + count + 2], padded.at[pl.ds(at, count + 2)], PAD - 1, cols, 1)
        to += count + 2
    to = 0
    for _, count, out in pieces:
        value = products(wide, weight, to, count, 1)
        out[...] = value.astype(BF16).reshape(count, cols, channels)
        to += count + 2


def mean_kernel(inner, outer, other, swapped, got0, got1, got2, out, to_near, to_far, block):
    row, col = lax.axis_index("row"), lax.axis_index("col")
    core = col % 2
    diagonal = row == col // 2
    size = other.shape[0]
    inset = outer.shape[0] // 2
    over = size - got2.shape[0]

    def put(to, inner, outer):
        to[inset : size - inset] = inner[...]
        to[:inset] = outer[:inset]
        to[size - inset :] = outer[inset : 2 * inset]

    @pl.when(diagonal)
    def _():
        put(block.at[0], inner, outer)
        block[1] = swapped[...]

    @pl.when(jnp.logical_not(diagonal))
    def _():
        put(block.at[0], got0, got1)
        block[1, :over] = got1[2 * inset :]
        block[1, over:] = got2[...]

    def mean(first, turned):
        return ((first.astype(F32) + turned.astype(F32)) * 0.5).astype(BF16)

    turned = jnp.swapaxes(block[0], 0, 1)
    half = core * size
    out[pl.ds(half + inset, size - 2 * inset)] = mean(inner[...], turned[inset : size - inset])
    out[pl.ds(half, inset)] = mean(outer[:inset], turned[:inset])
    out[pl.ds(half + size - inset, inset)] = mean(outer[inset:], turned[size - inset :])
    out[pl.ds((1 - core) * size, size)] = mean(other[...], jnp.swapaxes(block[1], 0, 1))
    start, end = out[:, :STRIP, :], out[:, size - STRIP :, :]
    to_near[...] = jnp.where(core == 0, end, start)
    to_far[...] = jnp.where(core == 0, start, end)


def second_rows(wide, weight, at, rows, valid):
    a = products(wide, weight, at, rows, 2).astype(BF16).astype(F32)
    b = products(wide, weight, at, rows, 2, flip=True).astype(BF16).astype(F32)
    mean = ((a + b) * 0.5).reshape(rows, wide.shape[1], -1)
    return jnp.where(valid, mean, 0.0).astype(BF16)


def columns_inside(x, tile_cols):
    x = x + lax.axis_index("col") * tile_cols
    return (x >= 0) & (x < tile_cols * lax.axis_size("col"))


def inner_second_kernel(sym, weight, out, wide, *, step):
    cols, channels = sym.shape[1], sym.shape[2]
    wide[:, 2:, :channels] = sym[:, : cols - 2, :]
    wide[:, :, channels : 2 * channels] = sym[...]
    wide[:, : cols - 2, 2 * channels :] = sym[:, 2:, :]
    for at in range(0, out.shape[0], step):
        out[at : at + step] = second_rows(wide, weight, at, step, True)


def middle_kernel(
    sym, near, far, inner, w_second, w_third, features, tops, bottoms, padded, wide2, sym2, wide3, out, done,
    *, steps
):
    tile_rows, tile_cols, channels = sym.shape
    end = PAD + tile_cols
    padded[:, PAD:end, :] = sym[...]
    before, after = sides(near[...], far[...])
    padded[:, PAD - STRIP : PAD, :] = before
    padded[:, end : end + STRIP, :] = after
    half = wide2.shape[1] // 2
    for q in range(3):
        lanes = slice(q * channels, (q + 1) * channels)
        at = PAD - 6 + 2 * q
        wide2[:, :half, lanes] = padded[:, at : at + half, :]
        at += tile_cols
        wide2[:, half:, lanes] = padded[:, at : at + half, :]
    x = lax.broadcasted_iota(jnp.int32, (1, 2 * half, 1), 1)
    valid = columns_inside(jnp.where(x < half, x - 4, x - half + tile_cols - 4), tile_cols)
    rows2, rows3 = sym2.shape[0], out.shape[0]
    sym2[:, STRIP : STRIP + tile_cols, :] = inner[...]
    for at in range(0, rows2, steps[0]):
        value = second_rows(wide2, w_second, at, steps[0], valid)
        rows = slice(at, at + steps[0])
        sym2[rows, STRIP - 4 : STRIP - 4 + half, :] = value[:, :half, :]
        to = STRIP + tile_cols - 4
        sym2[rows, to : to + half, :] = value[:, half:, :]
    tops[...] = sym2[0:STRIP]
    bottoms[...] = sym2[rows2 - STRIP : rows2]
    widen(wide3, sym2, STRIP - 4, tile_cols, 4)
    copies = []
    for i, at in enumerate(range(0, rows3, steps[1])):
        value = products(wide3, w_third, at, steps[1], 4)
        rows = pl.ds(at, steps[1])
        out[rows] = value.astype(BF16).reshape(steps[1], tile_cols, channels)
        target = features.at[pl.ds(EDGE + at, steps[1])]
        copies.append(pltpu.make_async_copy(out.at[rows], target, done.at[i]))
        copies[-1].start()
    for copy in copies:
        copy.wait()


def edges_kernel(
    _, sym, near, far, band_near, band_far, tops, bottoms, w_second, w_third, features,
    padded, wide2, sym2, wide3, out, done,
):
    row = lax.axis_index("row")
    up = row % 2
    tile_rows, tile_cols, channels = sym.shape
    end = PAD + tile_cols
    width = wide2.shape[2]
    side = (width - tile_cols) // 2
    x = lax.broadcasted_iota(jnp.int32, (1, width, 1), 1) - side
    valid = columns_inside(x, tile_cols)
    rows = padded.shape[1] - HALO
    bands = (
        jnp.where(up == 0, band_far[...], band_near[...]),
        jnp.where(up == 0, band_near[...], band_far[...]),
    )
    targets = [features.at[pl.ds(0, EDGE)], features.at[pl.ds(tile_rows - EDGE, EDGE)]]
    copies = [pltpu.make_async_copy(out.at[i], targets[i], done.at[i]) for i in range(2)]
    y = lax.broadcasted_iota(jnp.int32, (HALO, 1, 1), 0)
    insides = [
        row * tile_rows - 4 + y >= 0,
        (row + 1) * tile_rows - 2 + y < tile_rows * lax.axis_size("row"),
    ]
    for i in range(2):
        own = slice(HALO, HALO + rows) if i == 0 else slice(0, rows)
        outside = slice(0, HALO) if i == 0 else slice(rows, rows + HALO)
        source = slice(0, rows) if i == 0 else slice(tile_rows - rows, tile_rows)
        padded[i, own, PAD:end, :] = sym[source]
        before, after = sides(near[source], far[source])
        padded[i, own, PAD - STRIP : PAD, :] = before
        padded[i, own, end : end + STRIP, :] = after
        padded[i, outside, PAD - STRIP : end + STRIP, :] = bands[i]
        widen(wide2.at[i], padded.at[i], PAD - side - 2, width, 2)
    values = [second_rows(wide2.at[i], w_second, 0, HALO, valid & insides[i]) for i in range(2)]
    sym2[0, 0:HALO], sym2[0, HALO:] = values[0], tops[...]
    sym2[1, 0:STRIP], sym2[1, STRIP:] = bottoms[...], values[1]
    for i in range(2):
        widen(wide3.at[i], sym2.at[i], side - 4, tile_cols, 4)
    for i in range(2):
        value = products(wide3.at[i], w_third, 0, EDGE, 4)
        out[i] = value.astype(BF16).reshape(EDGE, tile_cols, channels)
        copies[i].start()
    for copy in copies:
        copy.wait()


def whole(count):
    return [pl.BlockSpec(memory_space=pltpu.VMEM)] * count


def divisor(number, most):
    return max(d for d in range(1, most + 1) if number % d == 0)


def cut(array, at, size, dim):
    return lax.dynamic_slice_in_dim(array, at, size, dim)


def local(contacts, w_first, w_second, w_third):
    tile_rows, tile_cols, channels = contacts.shape
    place = Place()
    core, up = place.core, place.up
    anywhere = pl.BlockSpec(memory_space=pl.ANY)

    def shape(*dims):
        return jax.ShapeDtypeStruct((*dims, channels), BF16)

    def scratch(*dims):
        return pltpu.VMEM(dims, BF16)

    def call(name, kernel, outs, ins, scratches, pixels=0, in_specs=None, out_specs=None, alias=None):
        macs = pixels * 9 * channels * channels
        return pl.pallas_call(
            kernel,
            out_shape=outs,
            in_specs=in_specs or whole(len(ins)),
            out_specs=out_specs or tuple(whole(len(outs))),
            scratch_shapes=scratches,
            input_output_aliases=alias or {},
            compiler_params=pltpu.CompilerParams(vmem_limit_bytes=24 * 2**20),
            cost_estimate=pl.CostEstimate(
                flops=2 * macs, bytes_accessed=18 * channels * channels, transcendentals=0
            ),
            name=name,
        )(*ins)

    (tile,) = call(
        "stage",
        stage_kernel,
        (shape(tile_rows, tile_cols),),
        (contacts,),
        [pltpu.SemaphoreType.DMA],
        in_specs=[anywhere],
    )

    ends = [contacts[:, 0], contacts[:, tile_cols - 1]]
    near = pairwise(jnp.where(core == 0, ends[1], ends[0]), "col", 0, "own_near")
    far = pairwise(jnp.where(core == 0, ends[0], ends[1]), "col", 1, "own_far")
    inset = tile_cols // 8
    lead = tile_cols - 2 * inset
    padded = scratch(tile_rows + 2, tile_cols + 2 * PAD, channels)
    (inner,) = call(
        "inner_first",
        inner_first_kernel,
        (shape(lead, tile_cols),),
        (tile, near, far, w_first),
        [padded, scratch(lead + 2, tile_cols, 3 * channels)],
        lead * tile_cols,
    )
    with jax.named_scope("hop0"):
        hop0 = place.hop(inner)
    before, after = sides(near, far)
    before, after, inner = lax.optimization_barrier((before, after, inner))
    ends = [
        jnp.concatenate([before[y : y + 1], tile[y], after[y : y + 1]]) for y in (0, tile_rows - 1)
    ]
    band_near = pairwise(jnp.where(up == 0, ends[1], ends[0]), "row", 0, "own_band_near")
    band_far = pairwise(jnp.where(up == 0, ends[0], ends[1]), "row", 1, "own_band_far")
    outer, other = call(
        "outer_first",
        outer_first_kernel,
        (shape(2 * inset, tile_cols), shape(tile_cols, tile_cols)),
        (tile, near, far, band_near, band_far, w_first),
        [padded, scratch(2 * inset + tile_cols + 6, tile_cols, 3 * channels)],
        0,
    )
    swapped = pairwise(other, "col", 0, "swap")
    over = tile_cols // 2 - inset
    with jax.named_scope("hop1"):
        hop1 = place.hop(jnp.concatenate([outer, swapped[:over]]))
    with jax.named_scope("hop2"):
        hop2 = place.hop(swapped[over:])
    with jax.named_scope("land0"):
        got0 = place.land(hop0)
    with jax.named_scope("land1"):
        got1 = place.land(hop1)
    with jax.named_scope("land2"):
        got2 = place.land(hop2)
    sym, to_near, to_far = call(
        "mean",
        mean_kernel,
        (shape(tile_rows, tile_cols), shape(tile_rows, STRIP), shape(tile_rows, STRIP)),
        (inner, outer, other, swapped, got0, got1, got2),
        [scratch(2, tile_cols, tile_cols, channels)],
    )

    near = pairwise(to_near, "col", 0, "sym_near")
    far = pairwise(to_far, "col", 1, "sym_far")
    rows2, rows3 = tile_rows - 4, tile_rows - 2 * EDGE
    (inner,) = call(
        "inner_second",
        lambda *refs: inner_second_kernel(*refs, step=divisor(rows2, 20)),
        (shape(rows2, tile_cols),),
        (sym, w_second),
        [scratch(tile_rows, tile_cols, 3 * channels)],
        2 * rows2 * tile_cols,
    )
    before, after = sides(near, far)

    def band(at):
        return jnp.concatenate([cut(part, at, HALO, 0) for part in (before, sym, after)], axis=1)

    last = tile_rows - HALO
    band_near = pairwise(band((1 - up) * last), "row", 0, "sym_band_near")
    band_far = pairwise(band(up * last), "row", 1, "sym_band_far")
    width = tile_cols + 2 * STRIP
    step = divisor(rows3, 26)
    features, tops, bottoms = call(
        "middle",
        lambda *refs: middle_kernel(*refs, steps=(divisor(rows2, 30), step)),
        (shape(tile_rows, tile_cols), shape(STRIP, width), shape(STRIP, width)),
        (sym, near, far, inner, w_second, w_third),
        [
            scratch(tile_rows, tile_cols + 2 * PAD, channels),
            scratch(tile_rows, 16, 3 * channels),
            scratch(rows2, width, channels),
            scratch(rows2, tile_cols, 3 * channels),
            scratch(rows3, tile_cols, channels),
            pltpu.SemaphoreType.DMA((rows3 // step,)),
        ],
        2 * rows2 * 16 + rows3 * tile_cols,
        out_specs=(anywhere, *whole(2)),
    )
    return call(
        "edges",
        edges_kernel,
        (shape(tile_rows, tile_cols),),
        (features, sym, near, far, band_near, band_far, tops, bottoms, w_second, w_third),
        [
            scratch(2, HALO + 4, tile_cols + 2 * PAD, channels),
            scratch(2, HALO + 4, width, 3 * channels),
            scratch(2, HALO + STRIP, width, channels),
            scratch(2, HALO + STRIP, tile_cols, 3 * channels),
            scratch(2, EDGE, tile_cols, channels),
            pltpu.SemaphoreType.DMA((2,)),
        ],
        2 * 2 * HALO * width + 2 * EDGE * tile_cols,
        in_specs=[anywhere] + whole(9),
        out_specs=(anywhere,),
        alias={0: 0},
    )[0]


def solution(mesh):
    return jax.shard_map(
        local,
        mesh=mesh,
        in_specs=(P("row", "col", None), P(), P(), P()),
        out_specs=P("row", "col", None),
        check_vma=False,
    )
```

time: 91.3 us -> 81.7 us (0.89)
  waiting for transfers between devices: 28.6 us -> 20.9 us
  local copies, waits for them, and re-layouts: 5.31 us -> 2.84 us
  starting transfers between devices: 36.5 us -> 38.7 us
  Pallas kernels: 18.4 us -> 17 us
  other arithmetic: 1.21 us -> 0.14 us
    ppermute x9, waiting for transfers between devices: 9.76 us -> 4.59 us  [pairwise(): return lax.ppermute(array, axis, pairs + [(j, i) for i, j in pairs])]
    ppermute x6, starting transfers between devices: 11.7 us -> 15.3 us  [chips(): return lax.ppermute(array, AXES, pairs)]
    unnamed x14 -> x8, local copies, waits for them, and re-layouts: 4.2 us -> 1.61 us
    ppermute x6, waiting for transfers between devices: 18.9 us -> 16.3 us  [chips(): return lax.ppermute(array, AXES, pairs)]
    pallas_call x6 -> x7, Pallas kernels: 18.4 us -> 17 us  [call(): pl.pallas_call(kernel, out_shape=outs, in_specs=in_specs or whole(len(ins...]
    ppermute x9, starting transfers between devices: 24.7 us -> 23.4 us  [pairwise(): return lax.ppermute(array, axis, pairs + [(j, i) for i, j in pairs])]
    select_n x5 -> x3, other arithmetic: 1.12 us -> 0.08 us  [the longest x2 0.05 us: sides(): return (jnp.where(core == 0, far, near), jnp.where(core == 0, near, far))]
    slice x6 -> x4, local copies, waits for them, and re-layouts: 0.19 us -> 1.18 us  [the longest x1 1.14 us: local(): ends = [contacts[:, 0], contacts[:, tile_cols - 1]]]
  transfers between devices with their start and end apart: 15 -> 15, of which waited for: 5 -> 7; matrix products, arithmetic and copies ran while one was open for 0% -> 0% of each run, Pallas kernels for 14% -> 13%
where the time goes in v4:
time: 81.7 us; the launch traced here: 80.1 us
  starting transfers between devices  38.7 us (47%)
  waiting for transfers between devices  20.9 us (26%)
  Pallas kernels  17 us (21%)
  local copies, waits for them, and re-layouts  2.84 us (3%)
    ppermute x9, starting transfers between devices, pairwise(): return lax.ppermute(array, axis, pairs + [(j, i) for i, j in pairs])  23.4 us
    pallas_call x7, Pallas kernels, call(): pl.pallas_call(kernel, out_shape=outs, in_specs=in_specs or whole(len(ins...  17 us
    ppermute x6, waiting for transfers between devices, chips(): return lax.ppermute(array, AXES, pairs)  16.3 us
    ppermute x6, starting transfers between devices, chips(): return lax.ppermute(array, AXES, pairs)  15.3 us
    ppermute x9, waiting for transfers between devices, pairwise(): return lax.ppermute(array, axis, pairs + [(j, i) for i, j in pairs])  4.59 us
  transfers between devices with their start and end apart: 15, of which 7 were waited for; matrix products, arithmetic and copies ran while one was open for 0% of the time, Pallas kernels for 13%

profile of v4, /device:TPU:5, one launch (start us, length us, event | category | flops | bytes accessed | tf_op | source)
XLA Modules:
  0.0 80.1 jit_solution(3911291823901616074)
XLA Ops:
  0.0 1.1 %fusion = (bf16[64,1,256]{2,1,0:T(2,128)(2,1)S(1)}, bf16[64,1,256]{2,1,0:T(2,128)(2,1)S(1)}) fusion(bf16[64,32,256]{2,1,0:T(8,128)(2,1)} %source.1), kind=kLoop, calls=%fused_computation.21 | loop fusion | bytes 131072 | tf_op jit(solution)/shard_map/slice | solution.py:339
  1.2 0.7 collective-permute-start.1
  1.9 3.1 %collective-permute-start = (bf16[64,256]{1,0:T(8,128)(2,1)S(1)}, bf16[64,256]{1,0:T(8,128)(2,1)S(1)}, u32[]{:S(2)}, u32[]{:S(2)}) collective-permute-start(bf16[64,256]{1,0:T(8,128)(2,1)S(1)} %get-tuple-element.40), channel_id=1, source_target_pairs={{1,2},{3,4},{5,6},{2,1},{4,3},{6,5},{9,10},{11,12},{13,14},{10,9},... | collective-permute-start | bytes 98312 | tf_op jit(solution)/shard_map/own_far/ppermute | solution.py:65
  5.0 1.2 %copy-done = bf16[64,32,256]{2,1,0:T(8,128)(2,1)S(1)} copy-done((bf16[64,32,256]{2,1,0:T(8,128)(2,1)S(1)}, bf16[64,32,256]{2,1,0:T(8,128)(2,1)}, u32[]{:S(2)}) %copy-start) | copy-done | bytes 1048600
  6.2 0.1 stage.1.tile
  6.4 0.8 collective-permute-done.far
  7.1 0.4 copy-done.3
  7.5 1.4 %inner_first.1.inner = bf16[24,32,256]{2,1,0:T(8,128)(2,1)S(1)} custom-call(bf16[64,32,256]{2,1,0:T(8,128)(2,1)S(1)} %stage.1.tile, bf16[64,256]{1,0:T(8,128)(2,1)S(1)} %collective-permute-done.1.near, bf16[64,256]{1,0:T(8,128)(2,1)S(1)} %collective-permute-done.far, bf16[3,3,256,256]{3,2,1,0:T(8,128)(2,1)S(1)} %copy-done.3), custom_call_target="tpu_custom_call" | custom-call | flops 905969664 | bytes 1179648 | tf_op jit(solution)/shard_map/inner_first/pallas_call | solution.py:316
  8.9 3.1 %collective-permute-start.3 = (bf16[34,256]{1,0:T(8,128)(2,1)S(1)}, bf16[34,256]{1,0:T(8,128)(2,1)S(1)}, u32[]{:S(2)}, u32[]{:S(2)}) collective-permute-start(bf16[34,256]{1,0:T(8,128)(2,1)S(1)} %get-tuple-element.43), channel_id=1, source_target_pairs={{8,16},{16,8},{9,17},{17,9},{10,18},{18,10},{11,19},{19,11},{12,20... | collective-permute-start | bytes 52232 | tf_op jit(solution)/shard_map/own_band_far/ppermute | solution.py:65
  12.0 0.1 collective-permute-start.2
  12.1 2.3 %collective-permute-done.3.band_far = bf16[34,256]{1,0:T(8,128)(2,1)S(1)} collective-permute-done((bf16[34,256]{1,0:T(8,128)(2,1)S(1)}, bf16[34,256]{1,0:T(8,128)(2,1)S(1)}, u32[]{:S(2)}, u32[]{:S(2)}) %collective-permute-start.3) | collective-permute-done | bytes 17440 | tf_op jit(solution)/shard_map/own_band_far/ppermute | solution.py:65
  14.3 0.3 collective-permute-done.2.band_near
  14.7 2.0 %outer_first.1 = (bf16[8,32,256]{2,1,0:T(8,128)(2,1)S(1)}, bf16[32,32,256]{2,1,0:T(8,128)(2,1)S(1)}) custom-call(bf16[64,32,256]{2,1,0:T(8,128)(2,1)S(1)} %stage.1.tile, bf16[64,256]{1,0:T(8,128)(2,1)S(1)} %collective-permute-done.1.near, bf16[64,256]{1,0:T(8,128)(2,1)S(1)} %collective-permute-done.far, ...), custom_call_target="tpu_custom_call" | custom-call | bytes 1179648 | tf_op jit(solution)/shard_map/outer_first/pallas_call | solution.py:316
  16.7 0.1 collective-permute-start.4
  16.8 0.7 collective-permute-start.5
  17.5 1.2 %collective-permute-done.4.swapped = bf16[32,32,256]{2,1,0:T(8,128)(2,1)S(1)} collective-permute-done((bf16[32,32,256]{2,1,0:T(8,128)(2,1)S(1)}, bf16[32,32,256]{2,1,0:T(8,128)(2,1)S(1)}, u32[]{:S(2)}, u32[]{:S(2)}) %collective-permute-start.4) | collective-permute-done | bytes 524320 | tf_op jit(solution)/shard_map/swap/ppermute | solution.py:65
  18.7 1.4 %collective-permute-start.9 = (bf16[20,32,256]{2,1,0:T(8,128)(2,1)S(1)}, bf16[20,32,256]{2,1,0:T(8,128)(2,1)}, u32[]{:S(2)}, u32[]{:S(2)}) collective-permute-start(bf16[20,32,256]{2,1,0:T(8,128)(2,1)S(1)} %slice.43), channel_id=1, source_target_pairs={{2,10},{3,11},{4,4},{5,5},{6,22},{7,23},{8,0},{9,1},{12,28},{13,29... | collective-permute-start | bytes 983048 | tf_op jit(solution)/shard_map/hop2/ppermute | solution.py:50
  20.1 1.4 %collective-permute-start.7 = (bf16[20,32,256]{2,1,0:T(8,128)(2,1)S(1)}, bf16[20,32,256]{2,1,0:T(8,128)(2,1)}, u32[]{:S(2)}, u32[]{:S(2)}) collective-permute-start(bf16[20,32,256]{2,1,0:T(8,128)(2,1)S(1)} %pad_maximum_fusion), channel_id=1, source_target_pairs={{2,10},{3,11},{4,4},{5,5},{6,22},{7,23},{8,0},{9,1},{12,28},{13,29... | collective-permute-start | bytes 983048 | tf_op jit(solution)/shard_map/hop1/ppermute | solution.py:50
  21.5 4.8 %collective-permute-start.6 = (bf16[24,32,256]{2,1,0:T(8,128)(2,1)S(1)}, bf16[24,32,256]{2,1,0:T(8,128)(2,1)S(1)}, u32[]{:S(2)}, u32[]{:S(2)}) collective-permute-start(bf16[24,32,256]{2,1,0:T(8,128)(2,1)S(1)} %collective-permute-done.5), channel_id=1, source_target_pairs={{10,8},{11,9},{4,16},{5,17},{22,24},{23,25},{0,2},{1,3},{28,18},{2... | collective-permute-start | bytes 1179656 | tf_op jit(solution)/shard_map/land0/ppermute | solution.py:50
  26.3 2.2 %collective-permute-start.10 = (bf16[20,32,256]{2,1,0:T(8,128)(2,1)}, bf16[20,32,256]{2,1,0:T(8,128)(2,1)S(1)}, u32[]{:S(2)}, u32[]{:S(2)}) collective-permute-start(bf16[20,32,256]{2,1,0:T(8,128)(2,1)} %collective-permute-done.9), channel_id=1, source_target_pairs={{10,8},{11,9},{4,16},{5,17},{22,24},{23,25},{0,2},{1,3},{28,18},{2... | collective-permute-start | bytes 983048 | tf_op jit(solution)/shard_map/land2/ppermute | solution.py:50
  28.6 4.8 %collective-permute-start.8 = (bf16[20,32,256]{2,1,0:T(8,128)(2,1)}, bf16[20,32,256]{2,1,0:T(8,128)(2,1)S(1)}, u32[]{:S(2)}, u32[]{:S(2)}) collective-permute-start(bf16[20,32,256]{2,1,0:T(8,128)(2,1)} %collective-permute-done.7), channel_id=1, source_target_pairs={{10,8},{11,9},{4,16},{5,17},{22,24},{23,25},{0,2},{1,3},{28,18},{2... | collective-permute-start | bytes 983048 | tf_op jit(solution)/shard_map/land1/ppermute | solution.py:50
  33.5 2.3 %collective-permute-done.6.got0 = bf16[24,32,256]{2,1,0:T(8,128)(2,1)S(1)} collective-permute-done((bf16[24,32,256]{2,1,0:T(8,128)(2,1)S(1)}, bf16[24,32,256]{2,1,0:T(8,128)(2,1)S(1)}, u32[]{:S(2)}, u32[]{:S(2)}) %collective-permute-start.6) | collective-permute-done | bytes 393248 | tf_op jit(solution)/shard_map/land0/ppermute | solution.py:50
  35.8 7.0 %collective-permute-done.10.got2 = bf16[20,32,256]{2,1,0:T(8,128)(2,1)S(1)} collective-permute-done((bf16[20,32,256]{2,1,0:T(8,128)(2,1)}, bf16[20,32,256]{2,1,0:T(8,128)(2,1)S(1)}, u32[]{:S(2)}, u32[]{:S(2)}) %collective-permute-start.10) | collective-permute-done | bytes 327712 | tf_op jit(solution)/shard_map/land2/ppermute | solution.py:50
  42.8 7.0 %collective-permute-done.8.got1 = bf16[20,32,256]{2,1,0:T(8,128)(2,1)S(1)} collective-permute-done((bf16[20,32,256]{2,1,0:T(8,128)(2,1)}, bf16[20,32,256]{2,1,0:T(8,128)(2,1)S(1)}, u32[]{:S(2)}, u32[]{:S(2)}) %collective-permute-start.8) | collective-permute-done | bytes 327712 | tf_op jit(solution)/shard_map/land1/ppermute | solution.py:50
  49.8 0.9 %mean.1 = (bf16[64,32,256]{2,1,0:T(8,128)(2,1)S(1)}, bf16[64,8,256]{2,1,0:T(8,128)(2,1)S(1)}, bf16[64,8,256]{2,1,0:T(8,128)(2,1)S(1)}) custom-call(bf16[24,32,256]{2,1,0:T(8,128)(2,1)S(1)} %inner_first.1.inner, bf16[8,32,256]{2,1,0:T(8,128)(2,1)S(1)} %get-tuple-element.19.outer, bf16[32,32,256]{2,1,0:T(8,128)(2,1)S(1)} %get-tuple-element.20.other, ...), custom_call_target="tpu_custom_call" | custom-call | bytes 1179648 | tf_op jit(solution)/shard_map/mean/pallas_call | solution.py:316
  50.7 1.0 %collective-permute-start.11 = (bf16[64,8,256]{2,1,0:T(8,128)(2,1)S(1)}, bf16[64,8,256]{2,1,0:T(8,128)(2,1)S(1)}, u32[]{:S(2)}, u32[]{:S(2)}) collective-permute-start(bf16[64,8,256]{2,1,0:T(8,128)(2,1)S(1)} %get-tuple-element.22), channel_id=1, source_target_pairs={{0,1},{2,3},{4,5},{6,7},{1,0},{3,2},{5,4},{7,6},{8,9},{10,11},{12,... | collective-permute-start | bytes 786440 | tf_op jit(solution)/shard_map/sym_near/ppermute | solution.py:65
  51.7 10.0 %collective-permute-start.12 = (bf16[64,8,256]{2,1,0:T(8,128)(2,1)S(1)}, bf16[64,8,256]{2,1,0:T(8,128)(2,1)S(1)}, u32[]{:S(2)}, u32[]{:S(2)}) collective-permute-start(bf16[64,8,256]{2,1,0:T(8,128)(2,1)S(1)} %get-tuple-element.23), channel_id=1, source_target_pairs={{1,2},{3,4},{5,6},{2,1},{4,3},{6,5},{9,10},{11,12},{13,14},{10,9},... | collective-permute-start | bytes 786440 | tf_op jit(solution)/shard_map/sym_far/ppermute | solution.py:65
  61.7 4.6 %inner_second.1.refs_3_ = bf16[60,32,256]{2,1,0:T(8,128)(2,1)S(1)} custom-call(bf16[64,32,256]{2,1,0:T(8,128)(2,1)S(1)} %get-tuple-element.21.refs_0_.sym, bf16[3,3,256,256]{3,2,1,0:T(8,128)(2,1)S(1)} %copy-done.1), custom_call_target="tpu_custom_call" | custom-call | flops 4529848320 | bytes 1179648 | tf_op jit(solution)/shard_map/inner_second/pallas_call | solution.py:316
  66.5 3.2 %collective-permute-start.13 = (bf16[6,48,256]{2,1,0:T(8,128)(2,1)S(1)}, bf16[6,48,256]{2,1,0:T(8,128)(2,1)S(1)}, u32[]{:S(2)}, u32[]{:S(2)}) collective-permute-start(bf16[6,48,256]{2,1,0:T(8,128)(2,1)S(1)} %pad_maximum_fusion.1), channel_id=1, source_target_pairs={{0,8},{16,24},{8,0},{24,16},{1,9},{17,25},{9,1},{25,17},{2,10},{18... | collective-permute-start | bytes 442376 | tf_op jit(solution)/shard_map/sym_band_near/ppermute | solution.py:65
  69.7 2.1 %collective-permute-start.14 = (bf16[6,48,256]{2,1,0:T(8,128)(2,1)S(1)}, bf16[6,48,256]{2,1,0:T(8,128)(2,1)S(1)}, u32[]{:S(2)}, u32[]{:S(2)}) collective-permute-start(bf16[6,48,256]{2,1,0:T(8,128)(2,1)S(1)} %pad_maximum_fusion.2), channel_id=1, source_target_pairs={{8,16},{16,8},{9,17},{17,9},{10,18},{18,10},{11,19},{19,11},{12,20... | collective-permute-start | bytes 442376 | tf_op jit(solution)/shard_map/sym_band_far/ppermute | solution.py:65
  71.9 5.4 %middle.1 = (bf16[64,32,256]{2,1,0:T(8,128)(2,1)}, bf16[8,48,256]{2,1,0:T(8,128)(2,1)S(1)}, bf16[8,48,256]{2,1,0:T(8,128)(2,1)S(1)}) custom-call(bf16[64,32,256]{2,1,0:T(8,128)(2,1)S(1)} %get-tuple-element.21.refs_0_.sym, bf16[64,8,256]{2,1,0:T(8,128)(2,1)S(1)} %collective-permute-done.11.refs_1_.near, ...), custom_call_target="tpu_custom_call" | custom-call | flops 4227858432 | bytes 1179648 | tf_op jit(solution)/shard_map/middle/pallas_call | solution.py:316
  77.3 2.7 %edges.1 = bf16[64,32,256]{2,1,0:T(8,128)(2,1)} custom-call(bf16[64,32,256]{2,1,0:T(8,128)(2,1)} %get-tuple-element.24._, bf16[64,32,256]{2,1,0:T(8,128)(2,1)S(1)} %get-tuple-element.21.refs_0_.sym, bf16[64,8,256]{2,1,0:T(8,128)(2,1)S(1)} %collective-permute-done.11.refs_1_.near, ...), custom_call_target="tpu_custom_call", output_to_operand_aliasing={{}: (0, {})} | custom-call | flops 1811939328 | bytes 1179648 | tf_op jit(solution)/shard_map/edges/pallas_call | solution.py:316
  (28 shorter events, 0.3 us)
Async XLA Ops:
  1.2 5.2 %collective-permute-start.1 = (bf16[64,256]{1,0:T(8,128)(2,1)S(1)}, bf16[64,256]{1,0:T(8,128)(2,1)S(1)}, u32[]{:S(2)}, u32[]{:S(2)}) collective-permute-start(bf16[64,256]{1,0:T(8,128)(2,1)S(1)} %get-tuple-element.39), channel_id=1, source_target_pairs={{0,1},{2,3},{4,5},{6,7},{1,0},{3,2},{5,4},{7,6},{8,9},{10,11},{12,... | collective-permute-start | bytes 98312 | tf_op jit(solution)/shard_map/own_near/ppermute | solution.py:65
  1.9 5.2 %collective-permute-start = (bf16[64,256]{1,0:T(8,128)(2,1)S(1)}, bf16[64,256]{1,0:T(8,128)(2,1)S(1)}, u32[]{:S(2)}, u32[]{:S(2)}) collective-permute-start(bf16[64,256]{1,0:T(8,128)(2,1)S(1)} %get-tuple-element.40), channel_id=1, source_target_pairs={{1,2},{3,4},{5,6},{2,1},{4,3},{6,5},{9,10},{11,12},{13,14},{10,9},... | collective-permute-start | bytes 98312 | tf_op jit(solution)/shard_map/own_far/ppermute | solution.py:65
  5.0 1.2 %copy-start = (bf16[64,32,256]{2,1,0:T(8,128)(2,1)S(1)}, bf16[64,32,256]{2,1,0:T(8,128)(2,1)}, u32[]{:S(2)}) copy-start(bf16[64,32,256]{2,1,0:T(8,128)(2,1)} %source.1) | copy-start | bytes 3145732
  6.2 1.3 %copy-start.3 = (bf16[3,3,256,256]{3,2,1,0:T(8,128)(2,1)S(1)}, bf16[3,3,256,256]{3,2,1,0:T(8,128)(2,1)}, u32[]{:S(2)}) copy-start(bf16[3,3,256,256]{3,2,1,0:T(8,128)(2,1)} %weight.3) | copy-start | bytes 3538948
  8.9 5.4 %collective-permute-start.3 = (bf16[34,256]{1,0:T(8,128)(2,1)S(1)}, bf16[34,256]{1,0:T(8,128)(2,1)S(1)}, u32[]{:S(2)}, u32[]{:S(2)}) collective-permute-start(bf16[34,256]{1,0:T(8,128)(2,1)S(1)} %get-tuple-element.43), channel_id=1, source_target_pairs={{8,16},{16,8},{9,17},{17,9},{10,18},{18,10},{11,19},{19,11},{12,20... | collective-permute-start | bytes 52232 | tf_op jit(solution)/shard_map/own_band_far/ppermute | solution.py:65
  12.0 2.7 %collective-permute-start.2 = (bf16[34,256]{1,0:T(8,128)(2,1)S(1)}, bf16[34,256]{1,0:T(8,128)(2,1)S(1)}, u32[]{:S(2)}, u32[]{:S(2)}) collective-permute-start(bf16[34,256]{1,0:T(8,128)(2,1)S(1)} %get-tuple-element.44), channel_id=1, source_target_pairs={{0,8},{16,24},{8,0},{24,16},{1,9},{17,25},{9,1},{25,17},{2,10},{18... | collective-permute-start | bytes 52232 | tf_op jit(solution)/shard_map/own_band_near/ppermute | solution.py:65
  16.7 2.0 %collective-permute-start.4 = (bf16[32,32,256]{2,1,0:T(8,128)(2,1)S(1)}, bf16[32,32,256]{2,1,0:T(8,128)(2,1)S(1)}, u32[]{:S(2)}, u32[]{:S(2)}) collective-permute-start(bf16[32,32,256]{2,1,0:T(8,128)(2,1)S(1)} %get-tuple-element.20.other), channel_id=1, source_target_pairs={{0,1},{2,3},{4,5},{6,7},{1,0},{3,2},{5,4},{7,6},{8,9},{10,11},{12,... | collective-permute-start | bytes 1572872 | tf_op jit(solution)/shard_map/swap/ppermute | solution.py:65
  16.8 4.7 %collective-permute-start.5 = (bf16[24,32,256]{2,1,0:T(8,128)(2,1)S(1)}, bf16[24,32,256]{2,1,0:T(8,128)(2,1)S(1)}, u32[]{:S(2)}, u32[]{:S(2)}) collective-permute-start(bf16[24,32,256]{2,1,0:T(8,128)(2,1)S(1)} %inner_first.1.inner), channel_id=1, source_target_pairs={{2,10},{3,11},{4,4},{5,5},{6,22},{7,23},{8,0},{9,1},{12,28},{13,29... | collective-permute-start | bytes 1179656 | tf_op jit(solution)/shard_map/hop0/ppermute | solution.py:50
  18.7 7.7 %collective-permute-start.9 = (bf16[20,32,256]{2,1,0:T(8,128)(2,1)S(1)}, bf16[20,32,256]{2,1,0:T(8,128)(2,1)}, u32[]{:S(2)}, u32[]{:S(2)}) collective-permute-start(bf16[20,32,256]{2,1,0:T(8,128)(2,1)S(1)} %slice.43), channel_id=1, source_target_pairs={{2,10},{3,11},{4,4},{5,5},{6,22},{7,23},{8,0},{9,1},{12,28},{13,29... | collective-permute-start | bytes 983048 | tf_op jit(solution)/shard_map/hop2/ppermute | solution.py:50
  20.1 8.5 %collective-permute-start.7 = (bf16[20,32,256]{2,1,0:T(8,128)(2,1)S(1)}, bf16[20,32,256]{2,1,0:T(8,128)(2,1)}, u32[]{:S(2)}, u32[]{:S(2)}) collective-permute-start(bf16[20,32,256]{2,1,0:T(8,128)(2,1)S(1)} %pad_maximum_fusion), channel_id=1, source_target_pairs={{2,10},{3,11},{4,4},{5,5},{6,22},{7,23},{8,0},{9,1},{12,28},{13,29... | collective-permute-start | bytes 983048 | tf_op jit(solution)/shard_map/hop1/ppermute | solution.py:50
  21.5 14.3 %collective-permute-start.6 = (bf16[24,32,256]{2,1,0:T(8,128)(2,1)S(1)}, bf16[24,32,256]{2,1,0:T(8,128)(2,1)S(1)}, u32[]{:S(2)}, u32[]{:S(2)}) collective-permute-start(bf16[24,32,256]{2,1,0:T(8,128)(2,1)S(1)} %collective-permute-done.5), channel_id=1, source_target_pairs={{10,8},{11,9},{4,16},{5,17},{22,24},{23,25},{0,2},{1,3},{28,18},{2... | collective-permute-start | bytes 1179656 | tf_op jit(solution)/shard_map/land0/ppermute | solution.py:50
  26.3 16.4 %collective-permute-start.10 = (bf16[20,32,256]{2,1,0:T(8,128)(2,1)}, bf16[20,32,256]{2,1,0:T(8,128)(2,1)S(1)}, u32[]{:S(2)}, u32[]{:S(2)}) collective-permute-start(bf16[20,32,256]{2,1,0:T(8,128)(2,1)} %collective-permute-done.9), channel_id=1, source_target_pairs={{10,8},{11,9},{4,16},{5,17},{22,24},{23,25},{0,2},{1,3},{28,18},{2... | collective-permute-start | bytes 983048 | tf_op jit(solution)/shard_map/land2/ppermute | solution.py:50
  28.6 21.2 %collective-permute-start.8 = (bf16[20,32,256]{2,1,0:T(8,128)(2,1)}, bf16[20,32,256]{2,1,0:T(8,128)(2,1)S(1)}, u32[]{:S(2)}, u32[]{:S(2)}) collective-permute-start(bf16[20,32,256]{2,1,0:T(8,128)(2,1)} %collective-permute-done.7), channel_id=1, source_target_pairs={{10,8},{11,9},{4,16},{5,17},{22,24},{23,25},{0,2},{1,3},{28,18},{2... | collective-permute-start | bytes 983048 | tf_op jit(solution)/shard_map/land1/ppermute | solution.py:50
  33.5 28.2 %copy-start.1 = (bf16[3,3,256,256]{3,2,1,0:T(8,128)(2,1)S(1)}, bf16[3,3,256,256]{3,2,1,0:T(8,128)(2,1)}, u32[]{:S(2)}) copy-start(bf16[3,3,256,256]{3,2,1,0:T(8,128)(2,1)} %w_second.1) | copy-start | bytes 3538948
  50.7 15.7 %collective-permute-start.11 = (bf16[64,8,256]{2,1,0:T(8,128)(2,1)S(1)}, bf16[64,8,256]{2,1,0:T(8,128)(2,1)S(1)}, u32[]{:S(2)}, u32[]{:S(2)}) collective-permute-start(bf16[64,8,256]{2,1,0:T(8,128)(2,1)S(1)} %get-tuple-element.22), channel_id=1, source_target_pairs={{0,1},{2,3},{4,5},{6,7},{1,0},{3,2},{5,4},{7,6},{8,9},{10,11},{12,... | collective-permute-start | bytes 786440 | tf_op jit(solution)/shard_map/sym_near/ppermute | solution.py:65
  51.7 14.7 %collective-permute-start.12 = (bf16[64,8,256]{2,1,0:T(8,128)(2,1)S(1)}, bf16[64,8,256]{2,1,0:T(8,128)(2,1)S(1)}, u32[]{:S(2)}, u32[]{:S(2)}) collective-permute-start(bf16[64,8,256]{2,1,0:T(8,128)(2,1)S(1)} %get-tuple-element.23), channel_id=1, source_target_pairs={{1,2},{3,4},{5,6},{2,1},{4,3},{6,5},{9,10},{11,12},{13,14},{10,9},... | collective-permute-start | bytes 786440 | tf_op jit(solution)/shard_map/sym_far/ppermute | solution.py:65
  66.3 5.5 %copy-start.2 = (bf16[3,3,256,256]{3,2,1,0:T(8,128)(2,1)S(1)}, bf16[3,3,256,256]{3,2,1,0:T(8,128)(2,1)}, u32[]{:S(2)}) copy-start(bf16[3,3,256,256]{3,2,1,0:T(8,128)(2,1)} %w_third.1) | copy-start | bytes 3538948
  66.5 10.8 %collective-permute-start.13 = (bf16[6,48,256]{2,1,0:T(8,128)(2,1)S(1)}, bf16[6,48,256]{2,1,0:T(8,128)(2,1)S(1)}, u32[]{:S(2)}, u32[]{:S(2)}) collective-permute-start(bf16[6,48,256]{2,1,0:T(8,128)(2,1)S(1)} %pad_maximum_fusion.1), channel_id=1, source_target_pairs={{0,8},{16,24},{8,0},{24,16},{1,9},{17,25},{9,1},{25,17},{2,10},{18... | collective-permute-start | bytes 442376 | tf_op jit(solution)/shard_map/sym_band_near/ppermute | solution.py:65
  69.7 7.5 %collective-permute-start.14 = (bf16[6,48,256]{2,1,0:T(8,128)(2,1)S(1)}, bf16[6,48,256]{2,1,0:T(8,128)(2,1)S(1)}, u32[]{:S(2)}, u32[]{:S(2)}) collective-permute-start(bf16[6,48,256]{2,1,0:T(8,128)(2,1)S(1)} %pad_maximum_fusion.2), channel_id=1, source_target_pairs={{8,16},{16,8},{9,17},{17,9},{10,18},{18,10},{11,19},{19,11},{12,20... | collective-permute-start | bytes 442376 | tf_op jit(solution)/shard_map/sym_band_far/ppermute | solution.py:65

commit v5 on v4

--- a/solution.py
+++ b/solution.py
@@ -16,7 +16,7 @@
 EDGE = 6
 
 
-def routes(row_count):
+def routes(row_count, plan):
     low = math.isqrt(row_count)
     first, second = {}, {}
     for r in range(row_count):
@@ -24,7 +24,9 @@
             a, b, c, d = r // low, r % low, z // low, z % low
             if r == z:
                 continue
-            via = (r, z) if b == d else ((z, z) if a == c else (c * low + b, z))
+            straight, across = (b == d, a == c) if plan == 0 else (a == c, b == d)
+            turn = c * low + b if plan == 0 else a * low + d
+            via = (r if straight else z if across else turn, z)
             first[(r, z)] = via
             second.setdefault(via, []).append((z, r))
     if any(len(ends) > 1 for ends in second.values()) or len(set(first.values())) < len(first):
@@ -39,21 +41,26 @@
         self.core = self.col % 2
         self.up = self.row % 2
         self.diagonal = self.row == self.col // 2
-        self.first, self.second = routes(self.rows)
-
-    def chips(self, array, legs, shift=0):
+        self.legs = [routes(self.rows, plan) for plan in range(2)]
+
+    def chips(self, array, legs):
         pairs = [
-            (s[0] * self.cols + s[1] * 2 + k, e[0] * self.cols + e[1] * 2 + (k + shift) % 2)
+            (s[0] * self.cols + s[1] * 2 + k, e[0] * self.cols + e[1] * 2 + k)
             for s, e in legs.items()
             for k in range(2)
         ]
         return lax.ppermute(array, AXES, pairs)
 
-    def hop(self, piece):
-        return self.chips(piece, self.first) if self.first else piece
-
-    def land(self, hopped, shift=0):
-        return self.chips(hopped, self.second, shift)
+    def hop(self, piece, plan):
+        first = self.legs[plan][0]
+        return self.chips(piece, first) if first else piece
+
+    def direct(self, piece):
+        places = [(r, z) for r in range(self.rows) for z in range(self.rows) if r != z]
+        return self.chips(piece, {(r, z): (z, r) for r, z in places})
+
+    def land(self, hopped, plan):
+        return self.chips(hopped, self.legs[plan][1])
 
 
 def pairwise(array, axis, start, name):
@@ -87,12 +94,6 @@
     return jnp.maximum(jnp.dot(jnp.concatenate(taps, axis=1), flat, preferred_element_type=F32), 0.0)
 
 
-def stage_kernel(source, out, done):
-    copy = pltpu.make_async_copy(source, out, done)
-    copy.start()
-    copy.wait()
-
-
 def sides(near, far):
     core = lax.axis_index("col") % 2
     return jnp.where(core == 0, far, near), jnp.where(core == 0, near, far)
@@ -106,72 +107,79 @@
     padded[1 : 1 + rows, PAD + cols : PAD + cols + 1, :] = after.reshape(rows, 1, channels)
 
 
-def inner_first_kernel(tile, near, far, weight, out, padded, wide):
-    rows, cols, channels = out.shape
-    put_tile(padded, tile, near, far)
-    at = lax.axis_index("col") % 2 * cols + (cols - rows) // 2
-    widen(wide, padded.at[pl.ds(at, rows + 2)], PAD - 1, cols, 1)
-    out[...] = products(wide, weight, 0, rows, 1).astype(BF16).reshape(rows, cols, channels)
-
-
-def outer_first_kernel(tile, near, far, band_near, band_far, weight, mine, other, padded, wide):
+def first_kernel(tile, near, far, band_near, band_far, weight, out, mine, other, padded, wide, *, step):
     core, up = lax.axis_index("col") % 2, lax.axis_index("row") % 2
     rows, cols, channels = tile.shape
     put_tile(padded, tile, near, far)
     ends = slice(PAD - 1, PAD + cols + 1)
     padded[0, ends, :] = jnp.where(up == 0, band_far[...], band_near[...])
     padded[rows + 1, ends, :] = jnp.where(up == 0, band_near[...], band_far[...])
-    inset = mine.shape[0] // 2
-    top = core * cols
-    pieces = [
-        (top, inset, mine.at[:inset]),
-        (top + cols - inset, inset, mine.at[inset:]),
-        ((1 - core) * cols, cols, other),
-    ]
-    to = 0
-    for at, count, _ in pieces:
-        widen(wide.at[to : to + count + 2], padded.at[pl.ds(at, count + 2)], PAD - 1, cols, 1)
-        to += count + 2
-    to = 0
-    for _, count, out in pieces:
-        value = products(wide, weight, to, count, 1)
-        out[...] = value.astype(BF16).reshape(count, cols, channels)
-        to += count + 2
-
-
-def mean_kernel(inner, outer, other, swapped, got0, got1, got2, out, to_near, to_far, block):
+    widen(wide, padded, PAD - 1, cols, 1)
+    for at in range(0, rows, step):
+        value = products(wide, weight, at, step, 1)
+        out[at : at + step] = value.astype(BF16).reshape(step, cols, channels)
+    outer = jnp.where(core == 0, out[:, 0, :], out[:, cols - 1, :])
+    for half in range(2):
+        top = half * cols
+
+        def put(ring, top=top):
+            ring[:cols] = out[top]
+            ring[cols : 2 * cols] = out[top + cols - 1]
+            ring[2 * cols :] = outer[top : top + cols]
+
+        pl.when(core == half)(lambda put=put: put(mine))
+        pl.when(core != half)(lambda put=put: put(other))
+
+
+def turned_kernel(kept0, kept1, kept2, kept3, got0, got1, got2, got3, weight, out, padded, wide, *, step):
+    core = lax.axis_index("col") % 2
+    diagonal = lax.axis_index("row") == lax.axis_index("col") // 2
+    size, length, channels = out.shape
+    rows = kept0.shape[0]
+
+    def put(pieces):
+        for side in range(2):
+            left = PAD + side * size
+
+            def fill(first, second, left=left):
+                padded[1 : 1 + rows, left : left + size, :] = first[...]
+                padded[1 + rows : 1 + size, left : left + size, :] = second[...]
+
+            pl.when(core == side)(lambda fill=fill: fill(pieces[0], pieces[2]))
+            pl.when(core != side)(lambda fill=fill: fill(pieces[1], pieces[3]))
+
+    pl.when(diagonal)(lambda: put((kept0, kept1, kept2, kept3)))
+    pl.when(jnp.logical_not(diagonal))(lambda: put((got0, got1, got2, got3)))
+    widen(wide, padded, PAD - 1, length, 1)
+    for at in range(0, size, step):
+        value = products(wide, weight, at, step, 1)
+        out[at : at + step] = value.astype(BF16).reshape(step, length, channels)
+
+
+def mean_kernel(first, turned, kept, got, out, to_near, to_far, block, ring):
     row, col = lax.axis_index("row"), lax.axis_index("col")
     core = col % 2
     diagonal = row == col // 2
-    size = other.shape[0]
-    inset = outer.shape[0] // 2
-    over = size - got2.shape[0]
-
-    def put(to, inner, outer):
-        to[inset : size - inset] = inner[...]
-        to[:inset] = outer[:inset]
-        to[size - inset :] = outer[inset : 2 * inset]
-
-    @pl.when(diagonal)
-    def _():
-        put(block.at[0], inner, outer)
-        block[1] = swapped[...]
-
-    @pl.when(jnp.logical_not(diagonal))
-    def _():
-        put(block.at[0], got0, got1)
-        block[1, :over] = got1[2 * inset :]
-        block[1, over:] = got2[...]
-
-    def mean(first, turned):
-        return ((first.astype(F32) + turned.astype(F32)) * 0.5).astype(BF16)
-
-    turned = jnp.swapaxes(block[0], 0, 1)
-    half = core * size
-    out[pl.ds(half + inset, size - 2 * inset)] = mean(inner[...], turned[inset : size - inset])
-    out[pl.ds(half, inset)] = mean(outer[:inset], turned[:inset])
-    out[pl.ds(half + size - inset, inset)] = mean(outer[inset:], turned[size - inset :])
-    out[pl.ds((1 - core) * size, size)] = mean(other[...], jnp.swapaxes(block[1], 0, 1))
+    size, length, channels = turned.shape
+    count = 3 * size
+    ring[...] = jnp.where(diagonal, kept[...], got[...])
+    block[...] = turned[...]
+    for side in range(2):
+        left = side * size
+        edge = 0 if side == 0 else length - 1
+
+        def put(at, left=left, edge=edge):
+            block[0, left : left + size, :] = ring[at : at + size]
+            block[size - 1, left : left + size, :] = ring[at + size : at + 2 * size]
+            outer = ring[at + 2 * size : at + count]
+            block[:, edge : edge + 1, :] = outer.reshape(size, 1, channels)
+
+        pl.when(core == side)(lambda put=put: put(0))
+        pl.when(core != side)(lambda put=put: put(count))
+    for side in range(2):
+        rows = slice(side * size, (side + 1) * size)
+        other = jnp.swapaxes(block[:, rows, :], 0, 1).astype(F32)
+        out[rows] = ((first[rows].astype(F32) + other) * 0.5).astype(BF16)
     start, end = out[:, :STRIP, :], out[:, size - STRIP :, :]
     to_near[...] = jnp.where(core == 0, end, start)
     to_far[...] = jnp.where(core == 0, start, end)
@@ -327,64 +335,60 @@
             name=name,
         )(*ins)
 
-    (tile,) = call(
-        "stage",
-        stage_kernel,
-        (shape(tile_rows, tile_cols),),
-        (contacts,),
-        [pltpu.SemaphoreType.DMA],
-        in_specs=[anywhere],
-    )
-
-    ends = [contacts[:, 0], contacts[:, tile_cols - 1]]
+    tile = contacts
+    mine = cut(tile, core * tile_cols, tile_cols, 0)
+    swapped = pairwise(cut(tile, (1 - core) * tile_cols, tile_cols, 0), "col", 0, "swap")
+    most = tile_cols // 2
+    pieces = [mine[:most], swapped[:most], mine[most:], swapped[most:]]
+    hops, got = [], []
+
+    ends = [tile[:, 0], tile[:, tile_cols - 1]]
     near = pairwise(jnp.where(core == 0, ends[1], ends[0]), "col", 0, "own_near")
     far = pairwise(jnp.where(core == 0, ends[0], ends[1]), "col", 1, "own_far")
-    inset = tile_cols // 8
-    lead = tile_cols - 2 * inset
-    padded = scratch(tile_rows + 2, tile_cols + 2 * PAD, channels)
-    (inner,) = call(
-        "inner_first",
-        inner_first_kernel,
-        (shape(lead, tile_cols),),
-        (tile, near, far, w_first),
-        [padded, scratch(lead + 2, tile_cols, 3 * channels)],
-        lead * tile_cols,
-    )
-    with jax.named_scope("hop0"):
-        hop0 = place.hop(inner)
     before, after = sides(near, far)
-    before, after, inner = lax.optimization_barrier((before, after, inner))
     ends = [
         jnp.concatenate([before[y : y + 1], tile[y], after[y : y + 1]]) for y in (0, tile_rows - 1)
     ]
     band_near = pairwise(jnp.where(up == 0, ends[1], ends[0]), "row", 0, "own_band_near")
     band_far = pairwise(jnp.where(up == 0, ends[0], ends[1]), "row", 1, "own_band_far")
-    outer, other = call(
-        "outer_first",
-        outer_first_kernel,
-        (shape(2 * inset, tile_cols), shape(tile_cols, tile_cols)),
+    band_near, band_far, *pieces = lax.optimization_barrier((band_near, band_far, *pieces))
+    for i, piece in enumerate(pieces):
+        with jax.named_scope(f"hop{i}"):
+            hops.append(place.hop(piece, i % 2))
+    for i, hop in enumerate(hops):
+        with jax.named_scope(f"land{i}"):
+            got.append(place.land(hop, i % 2))
+    first, ring, other_ring = call(
+        "first",
+        lambda *refs: first_kernel(*refs, step=divisor(tile_rows, 16)),
+        (shape(tile_rows, tile_cols), *(shape(3 * tile_cols),) * 2),
         (tile, near, far, band_near, band_far, w_first),
-        [padded, scratch(2 * inset + tile_cols + 6, tile_cols, 3 * channels)],
-        0,
-    )
-    swapped = pairwise(other, "col", 0, "swap")
-    over = tile_cols // 2 - inset
-    with jax.named_scope("hop1"):
-        hop1 = place.hop(jnp.concatenate([outer, swapped[:over]]))
-    with jax.named_scope("hop2"):
-        hop2 = place.hop(swapped[over:])
-    with jax.named_scope("land0"):
-        got0 = place.land(hop0)
-    with jax.named_scope("land1"):
-        got1 = place.land(hop1)
-    with jax.named_scope("land2"):
-        got2 = place.land(hop2)
+        [
+            scratch(tile_rows + 2, tile_cols + 2 * PAD, channels),
+            scratch(tile_rows + 2, tile_cols, 3 * channels),
+        ],
+        tile_rows * tile_cols,
+    )
+    ring = jnp.concatenate([ring, pairwise(other_ring, "col", 0, "ring_swap")])
+    with jax.named_scope("ring"):
+        got_ring = place.direct(ring)
+    (turned,) = call(
+        "turned",
+        lambda *refs: turned_kernel(*refs, step=divisor(tile_cols, 8)),
+        (shape(tile_cols, tile_rows),),
+        (*pieces, *got, w_first),
+        [
+            scratch(tile_cols + 2, tile_rows + 2 * PAD, channels),
+            scratch(tile_cols + 2, tile_rows, 3 * channels),
+        ],
+        tile_rows * tile_cols,
+    )
     sym, to_near, to_far = call(
         "mean",
         mean_kernel,
         (shape(tile_rows, tile_cols), shape(tile_rows, STRIP), shape(tile_rows, STRIP)),
-        (inner, outer, other, swapped, got0, got1, got2),
-        [scratch(2, tile_cols, tile_cols, channels)],
+        (first, turned, ring, got_ring),
+        [scratch(tile_cols, tile_rows, channels), scratch(6 * tile_cols, channels)],
     )
 
     near = pairwise(to_near, "col", 0, "sym_near")

time: 81.7 us -> 79.4 us (0.972); the launches traced: 80.1 us -> 79 us
  waiting for transfers between devices: 20.9 us -> 8.86 us
  starting transfers between devices: 38.7 us -> 46.7 us
  Pallas kernels: 17 us -> 19.2 us
    ppermute x6 -> x9, waiting for transfers between devices: 16.3 us -> 6.13 us  [chips(): return lax.ppermute(array, AXES, pairs)]
    ppermute x6 -> x9, starting transfers between devices: 15.3 us -> 25.1 us  [chips(): return lax.ppermute(array, AXES, pairs)]
    pallas_call x7 -> x6, Pallas kernels: 17 us -> 19.2 us  [call(): pl.pallas_call(kernel, out_shape=outs, in_specs=in_specs or whole(len(ins...]
    ppermute x9 -> x10, waiting for transfers between devices: 4.59 us -> 2.73 us  [pairwise(): return lax.ppermute(array, axis, pairs + [(j, i) for i, j in pairs])]
    ppermute x9 -> x10, starting transfers between devices: 23.4 us -> 21.6 us  [pairwise(): return lax.ppermute(array, axis, pairs + [(j, i) for i, j in pairs])]
    unnamed x8 -> x9, local copies, waits for them, and re-layouts: 1.61 us -> 0.02 us
    slice x3, local copies, waits for them, and re-layouts: 1.17 us -> 2.33 us  [the longest x1 1.23 us: local(): ends = [tile[:, 0], tile[:, tile_cols - 1]]]
    dynamic_slice x3 -> x4, local copies, waits for them, and re-layouts: 0.05 us -> 1.13 us  [cut(): return lax.dynamic_slice_in_dim(array, at, size, dim)]
  transfers between devices with their start and end apart: 15 -> 19, of which waited for: 7 -> 4; matrix products, arithmetic and copies ran while one was open for 0% -> 3% of each run, Pallas kernels for 13% -> 20%
where the time goes in v5:
time: 79.4 us; the launch traced here: 79 us
  starting transfers between devices  46.7 us (59%)
  Pallas kernels  19.2 us (24%)
  waiting for transfers between devices  8.86 us (11%)
  local copies, waits for them, and re-layouts  3.5 us (4%)
    ppermute x9, starting transfers between devices, chips(): return lax.ppermute(array, AXES, pairs)  25.1 us
    ppermute x10, starting transfers between devices, pairwise(): return lax.ppermute(array, axis, pairs + [(j, i) for i, j in pairs])  21.6 us
    pallas_call x6, Pallas kernels, call(): pl.pallas_call(kernel, out_shape=outs, in_specs=in_specs or whole(len(ins...  19.2 us
    ppermute x9, waiting for transfers between devices, chips(): return lax.ppermute(array, AXES, pairs)  6.13 us
    ppermute x10, waiting for transfers between devices, pairwise(): return lax.ppermute(array, axis, pairs + [(j, i) for i, j in pairs])  2.73 us
  transfers between devices with their start and end apart: 19, of which 4 were waited for; matrix products, arithmetic and copies ran while one was open for 3% of the time, Pallas kernels for 20%

profile of v5, /device:TPU:5, one launch (start us, length us, event | category | flops | bytes accessed | tf_op | source)
XLA Modules:
  0.0 79.0 jit_solution(6954954120625277579)
XLA Ops:
  0.0 1.2 %fusion = (bf16[64,1,256]{2,1,0:T(2,128)(2,1)S(1)}, bf16[64,1,256]{2,1,0:T(2,128)(2,1)S(1)}) fusion(bf16[64,32,256]{2,1,0:T(8,128)(2,1)} %refs_0_.1), kind=kLoop, calls=%fused_computation.25 | loop fusion | bytes 131072 | tf_op jit(solution)/shard_map/slice | solution.py:345
  1.3 3.8 %collective-permute-start.1 = (bf16[64,256]{1,0:T(8,128)(2,1)S(1)}, bf16[64,256]{1,0:T(8,128)(2,1)S(1)}, u32[]{:S(2)}, u32[]{:S(2)}) collective-permute-start(bf16[64,256]{1,0:T(8,128)(2,1)S(1)} %get-tuple-element.51), channel_id=1, source_target_pairs={{1,2},{3,4},{5,6},{2,1},{4,3},{6,5},{9,10},{11,12},{13,14},{10,9},... | collective-permute-start | bytes 98312 | tf_op jit(solution)/shard_map/own_far/ppermute | solution.py:72
  5.0 0.1 collective-permute-start
  5.1 1.1 %constant_dynamic-slice_fusion.7 = bf16[32,32,256]{2,1,0:T(8,128)(2,1)S(1)} fusion(bf16[64,32,256]{2,1,0:T(8,128)(2,1)} %refs_0_.1, s32[]{:T(128)S(6)} %select_n.97), kind=kLoop, calls=%fused_computation.23 | loop fusion | bytes 1048580 | tf_op jit(solution)/shard_map/dynamic_slice | solution.py:307
  6.2 0.5 collective-permute-start.4
  6.9 3.2 %collective-permute-start.3 = (bf16[34,256]{1,0:T(8,128)(2,1)S(1)}, bf16[34,256]{1,0:T(8,128)(2,1)S(1)}, u32[]{:S(2)}, u32[]{:S(2)}) collective-permute-start(bf16[34,256]{1,0:T(8,128)(2,1)S(1)} %get-tuple-element.55), channel_id=1, source_target_pairs={{8,16},{16,8},{9,17},{17,9},{10,18},{18,10},{11,19},{19,11},{12,20... | collective-permute-start | bytes 52232 | tf_op jit(solution)/shard_map/own_band_far/ppermute | solution.py:72
  10.1 0.1 collective-permute-start.2
  10.2 1.1 %fusion.1 = (bf16[16,32,256]{2,1,0:T(8,128)(2,1)S(1)}, bf16[16,32,256]{2,1,0:T(8,128)(2,1)S(1)}) fusion(bf16[32,32,256]{2,1,0:T(8,128)(2,1)} %collective-permute-done.4), kind=kLoop, calls=%fused_computation.26 | loop fusion | bytes 1048576 | tf_op jit(solution)/shard_map/slice | solution.py:342
  11.3 1.2 %collective-permute-done.3.refs_4_ = bf16[34,256]{1,0:T(8,128)(2,1)S(1)} collective-permute-done((bf16[34,256]{1,0:T(8,128)(2,1)S(1)}, bf16[34,256]{1,0:T(8,128)(2,1)S(1)}, u32[]{:S(2)}, u32[]{:S(2)}) %collective-permute-start.3) | collective-permute-done | bytes 17440 | tf_op jit(solution)/shard_map/own_band_far/ppermute | solution.py:72
  12.5 0.6 collective-permute-done.2.refs_3_
  13.1 1.3 %collective-permute-start.5 = (bf16[16,32,256]{2,1,0:T(8,128)(2,1)S(1)}, bf16[16,32,256]{2,1,0:T(8,128)(2,1)}, u32[]{:S(2)}, u32[]{:S(2)}) collective-permute-start(bf16[16,32,256]{2,1,0:T(8,128)(2,1)S(1)} %get-tuple-element.23.refs_0_), channel_id=1, source_target_pairs={{2,10},{3,11},{4,4},{5,5},{6,22},{7,23},{8,0},{9,1},{12,28},{13,29... | collective-permute-start | bytes 786440 | tf_op jit(solution)/shard_map/hop0/ppermute | solution.py:52
  14.4 1.9 %collective-permute-start.7 = (bf16[16,32,256]{2,1,0:T(8,128)(2,1)S(1)}, bf16[16,32,256]{2,1,0:T(8,128)(2,1)}, u32[]{:S(2)}, u32[]{:S(2)}) collective-permute-start(bf16[16,32,256]{2,1,0:T(8,128)(2,1)S(1)} %get-tuple-element.24.refs_1_), channel_id=1, source_target_pairs={{2,2},{3,3},{4,20},{5,21},{6,14},{7,15},{8,8},{9,9},{12,4},{13,5},... | collective-permute-start | bytes 786440 | tf_op jit(solution)/shard_map/hop1/ppermute | solution.py:52
  16.4 1.3 %collective-permute-start.9 = (bf16[16,32,256]{2,1,0:T(8,128)(2,1)S(1)}, bf16[16,32,256]{2,1,0:T(8,128)(2,1)}, u32[]{:S(2)}, u32[]{:S(2)}) collective-permute-start(bf16[16,32,256]{2,1,0:T(8,128)(2,1)S(1)} %get-tuple-element.25.refs_2_), channel_id=1, source_target_pairs={{2,10},{3,11},{4,4},{5,5},{6,22},{7,23},{8,0},{9,1},{12,28},{13,29... | collective-permute-start | bytes 786440 | tf_op jit(solution)/shard_map/hop2/ppermute | solution.py:52
  17.7 1.9 %collective-permute-start.11 = (bf16[16,32,256]{2,1,0:T(8,128)(2,1)S(1)}, bf16[16,32,256]{2,1,0:T(8,128)(2,1)}, u32[]{:S(2)}, u32[]{:S(2)}) collective-permute-start(bf16[16,32,256]{2,1,0:T(8,128)(2,1)S(1)} %get-tuple-element.26.refs_3_), channel_id=1, source_target_pairs={{2,2},{3,3},{4,20},{5,21},{6,14},{7,15},{8,8},{9,9},{12,4},{13,5},... | collective-permute-start | bytes 786440 | tf_op jit(solution)/shard_map/hop3/ppermute | solution.py:52
  19.6 5.4 %collective-permute-start.6 = (bf16[16,32,256]{2,1,0:T(8,128)(2,1)}, bf16[16,32,256]{2,1,0:T(8,128)(2,1)S(1)}, u32[]{:S(2)}, u32[]{:S(2)}) collective-permute-start(bf16[16,32,256]{2,1,0:T(8,128)(2,1)} %collective-permute-done.5), channel_id=1, source_target_pairs={{10,8},{11,9},{4,16},{5,17},{22,24},{23,25},{0,2},{1,3},{28,18},{2... | collective-permute-start | bytes 786440 | tf_op jit(solution)/shard_map/land0/ppermute | solution.py:52
  25.0 2.4 %collective-permute-start.8 = (bf16[16,32,256]{2,1,0:T(8,128)(2,1)}, bf16[16,32,256]{2,1,0:T(8,128)(2,1)S(1)}, u32[]{:S(2)}, u32[]{:S(2)}) collective-permute-start(bf16[16,32,256]{2,1,0:T(8,128)(2,1)} %collective-permute-done.7), channel_id=1, source_target_pairs={{2,8},{3,9},{20,16},{21,17},{14,24},{15,25},{8,2},{9,3},{4,18},{5,... | collective-permute-start | bytes 786440 | tf_op jit(solution)/shard_map/land1/ppermute | solution.py:52
  27.5 3.5 %collective-permute-start.10 = (bf16[16,32,256]{2,1,0:T(8,128)(2,1)}, bf16[16,32,256]{2,1,0:T(8,128)(2,1)S(1)}, u32[]{:S(2)}, u32[]{:S(2)}) collective-permute-start(bf16[16,32,256]{2,1,0:T(8,128)(2,1)} %collective-permute-done.9), channel_id=1, source_target_pairs={{10,8},{11,9},{4,16},{5,17},{22,24},{23,25},{0,2},{1,3},{28,18},{2... | collective-permute-start | bytes 786440 | tf_op jit(solution)/shard_map/land2/ppermute | solution.py:52
  31.0 1.9 %collective-permute-start.12 = (bf16[16,32,256]{2,1,0:T(8,128)(2,1)}, bf16[16,32,256]{2,1,0:T(8,128)(2,1)S(1)}, u32[]{:S(2)}, u32[]{:S(2)}) collective-permute-start(bf16[16,32,256]{2,1,0:T(8,128)(2,1)} %collective-permute-done.11), channel_id=1, source_target_pairs={{2,8},{3,9},{20,16},{21,17},{14,24},{15,25},{8,2},{9,3},{4,18},{5,... | collective-permute-start | bytes 786440 | tf_op jit(solution)/shard_map/land3/ppermute | solution.py:52
  32.9 2.9 %first.1 = (bf16[64,32,256]{2,1,0:T(8,128)(2,1)S(1)}, bf16[96,256]{1,0:T(8,128)(2,1)S(1)}, bf16[96,256]{1,0:T(8,128)(2,1)S(1)}) custom-call(bf16[64,32,256]{2,1,0:T(8,128)(2,1)S(1)} %copy-done, bf16[64,256]{1,0:T(8,128)(2,1)S(1)} %collective-permute-done.refs_1_, bf16[64,256]{1,0:T(8,128)(2,1)S(1)} %collective-permute-done.1.refs_2_, ...), custom_call_target="tpu_custom_call" | custom-call | flops 2415919104 | bytes 1179648 | tf_op jit(solution)/shard_map/first/pallas_call | solution.py:324
  35.8 2.7 %collective-permute-start.13 = (bf16[96,256]{1,0:T(8,128)(2,1)S(1)}, bf16[96,256]{1,0:T(8,128)(2,1)S(1)}, u32[]{:S(2)}, u32[]{:S(2)}) collective-permute-start(bf16[96,256]{1,0:T(8,128)(2,1)S(1)} %get-tuple-element.28), channel_id=1, source_target_pairs={{0,1},{2,3},{4,5},{6,7},{1,0},{3,2},{5,4},{7,6},{8,9},{10,11},{12,... | collective-permute-start | bytes 147464 | tf_op jit(solution)/shard_map/ring_swap/ppermute | solution.py:72
  38.5 0.9 %collective-permute-done.13 = bf16[96,256]{1,0:T(8,128)(2,1)S(1)} collective-permute-done((bf16[96,256]{1,0:T(8,128)(2,1)S(1)}, bf16[96,256]{1,0:T(8,128)(2,1)S(1)}, u32[]{:S(2)}, u32[]{:S(2)}) %collective-permute-start.13) | collective-permute-done | bytes 49184 | tf_op jit(solution)/shard_map/ring_swap/ppermute | solution.py:72
  39.4 5.4 %collective-permute-start.14 = (bf16[192,256]{1,0:T(8,128)(2,1)S(1)}, bf16[192,256]{1,0:T(8,128)(2,1)S(1)}, u32[]{:S(2)}, u32[]{:S(2)}) collective-permute-start(bf16[192,256]{1,0:T(8,128)(2,1)S(1)} %constant_dynamic-update-slice_fusion.kept), channel_id=1, source_target_pairs={{2,8},{3,9},{4,16},{5,17},{6,24},{7,25},{8,2},{9,3},{12,18},{13,19... | collective-permute-start | bytes 294920 | tf_op jit(solution)/shard_map/ring/ppermute | solution.py:52
  44.9 6.1 %collective-permute-done.12.refs_7_ = bf16[16,32,256]{2,1,0:T(8,128)(2,1)S(1)} collective-permute-done((bf16[16,32,256]{2,1,0:T(8,128)(2,1)}, bf16[16,32,256]{2,1,0:T(8,128)(2,1)S(1)}, u32[]{:S(2)}, u32[]{:S(2)}) %collective-permute-start.12) | collective-permute-done | bytes 262176 | tf_op jit(solution)/shard_map/land3/ppermute | solution.py:52
  51.0 2.7 %turned.1 = bf16[32,64,256]{2,1,0:T(8,128)(2,1)S(1)} custom-call(bf16[16,32,256]{2,1,0:T(8,128)(2,1)S(1)} %get-tuple-element.23.refs_0_, bf16[16,32,256]{2,1,0:T(8,128)(2,1)S(1)} %get-tuple-element.24.refs_1_, bf16[16,32,256]{2,1,0:T(8,128)(2,1)S(1)} %get-tuple-element.25.refs_2_, bf16[16,32,256]{2,1,0:T(8,128)(2,1)S(1)} %get-tuple-element.26.refs_3_, ...), custom_call_target="tpu_custom_call" | custom-call | flops 2415919104 | bytes 1179648 | tf_op jit(solution)/shard_map/turned/pallas_call | solution.py:324
  53.7 0.9 %mean.1 = (bf16[64,32,256]{2,1,0:T(8,128)(2,1)S(1)}, bf16[64,8,256]{2,1,0:T(8,128)(2,1)S(1)}, bf16[64,8,256]{2,1,0:T(8,128)(2,1)S(1)}) custom-call(bf16[64,32,256]{2,1,0:T(8,128)(2,1)S(1)} %get-tuple-element.22.first, bf16[32,64,256]{2,1,0:T(8,128)(2,1)S(1)} %turned.1, bf16[192,256]{1,0:T(8,128)(2,1)S(1)} %constant_dynamic-update-slice_fusion.kept, ...), custom_call_target="tpu_custom_call" | custom-call | bytes 1179648 | tf_op jit(solution)/shard_map/mean/pallas_call | solution.py:324
  54.6 1.4 %collective-permute-start.15 = (bf16[64,8,256]{2,1,0:T(8,128)(2,1)S(1)}, bf16[64,8,256]{2,1,0:T(8,128)(2,1)S(1)}, u32[]{:S(2)}, u32[]{:S(2)}) collective-permute-start(bf16[64,8,256]{2,1,0:T(8,128)(2,1)S(1)} %get-tuple-element.30), channel_id=1, source_target_pairs={{0,1},{2,3},{4,5},{6,7},{1,0},{3,2},{5,4},{7,6},{8,9},{10,11},{12,... | collective-permute-start | bytes 786440 | tf_op jit(solution)/shard_map/sym_near/ppermute | solution.py:72
  56.0 4.4 %collective-permute-start.16 = (bf16[64,8,256]{2,1,0:T(8,128)(2,1)S(1)}, bf16[64,8,256]{2,1,0:T(8,128)(2,1)S(1)}, u32[]{:S(2)}, u32[]{:S(2)}) collective-permute-start(bf16[64,8,256]{2,1,0:T(8,128)(2,1)S(1)} %get-tuple-element.31), channel_id=1, source_target_pairs={{1,2},{3,4},{5,6},{2,1},{4,3},{6,5},{9,10},{11,12},{13,14},{10,9},... | collective-permute-start | bytes 786440 | tf_op jit(solution)/shard_map/sym_far/ppermute | solution.py:72
  60.4 4.6 %inner_second.1.refs_3_ = bf16[60,32,256]{2,1,0:T(8,128)(2,1)S(1)} custom-call(bf16[64,32,256]{2,1,0:T(8,128)(2,1)S(1)} %get-tuple-element.29.refs_0_.sym, bf16[3,3,256,256]{3,2,1,0:T(8,128)(2,1)S(1)} %copy-done.1), custom_call_target="tpu_custom_call" | custom-call | flops 4529848320 | bytes 1179648 | tf_op jit(solution)/shard_map/inner_second/pallas_call | solution.py:324
  65.2 0.1 collective-permute-start.17
  65.3 5.4 %collective-permute-start.18 = (bf16[6,48,256]{2,1,0:T(8,128)(2,1)S(1)}, bf16[6,48,256]{2,1,0:T(8,128)(2,1)S(1)}, u32[]{:S(2)}, u32[]{:S(2)}) collective-permute-start(bf16[6,48,256]{2,1,0:T(8,128)(2,1)S(1)} %pad_maximum_fusion.1), channel_id=1, source_target_pairs={{8,16},{16,8},{9,17},{17,9},{10,18},{18,10},{11,19},{19,11},{12,20... | collective-permute-start | bytes 442376 | tf_op jit(solution)/shard_map/sym_band_far/ppermute | solution.py:72
  70.7 5.4 %middle.1 = (bf16[64,32,256]{2,1,0:T(8,128)(2,1)}, bf16[8,48,256]{2,1,0:T(8,128)(2,1)S(1)}, bf16[8,48,256]{2,1,0:T(8,128)(2,1)S(1)}) custom-call(bf16[64,32,256]{2,1,0:T(8,128)(2,1)S(1)} %get-tuple-element.29.refs_0_.sym, bf16[64,8,256]{2,1,0:T(8,128)(2,1)S(1)} %collective-permute-done.15.refs_1_.near, ...), custom_call_target="tpu_custom_call" | custom-call | flops 4227858432 | bytes 1179648 | tf_op jit(solution)/shard_map/middle/pallas_call | solution.py:324
  76.1 2.7 %edges.1 = bf16[64,32,256]{2,1,0:T(8,128)(2,1)} custom-call(bf16[64,32,256]{2,1,0:T(8,128)(2,1)} %get-tuple-element.32._, bf16[64,32,256]{2,1,0:T(8,128)(2,1)S(1)} %get-tuple-element.29.refs_0_.sym, bf16[64,8,256]{2,1,0:T(8,128)(2,1)S(1)} %collective-permute-done.15.refs_1_.near, ...), custom_call_target="tpu_custom_call", output_to_operand_aliasing={{}: (0, {})} | custom-call | flops 1811939328 | bytes 1179648 | tf_op jit(solution)/shard_map/edges/pallas_call | solution.py:324
  (37 shorter events, 0.3 us)
Async XLA Ops:
  0.0 6.7 %copy-start = (bf16[64,32,256]{2,1,0:T(8,128)(2,1)S(1)}, bf16[64,32,256]{2,1,0:T(8,128)(2,1)}, u32[]{:S(2)}) copy-start(bf16[64,32,256]{2,1,0:T(8,128)(2,1)} %refs_0_.1) | copy-start | bytes 3145732
  1.3 5.6 %collective-permute-start.1 = (bf16[64,256]{1,0:T(8,128)(2,1)S(1)}, bf16[64,256]{1,0:T(8,128)(2,1)S(1)}, u32[]{:S(2)}, u32[]{:S(2)}) collective-permute-start(bf16[64,256]{1,0:T(8,128)(2,1)S(1)} %get-tuple-element.51), channel_id=1, source_target_pairs={{1,2},{3,4},{5,6},{2,1},{4,3},{6,5},{9,10},{11,12},{13,14},{10,9},... | collective-permute-start | bytes 98312 | tf_op jit(solution)/shard_map/own_far/ppermute | solution.py:72
  5.0 1.8 %collective-permute-start = (bf16[64,256]{1,0:T(8,128)(2,1)S(1)}, bf16[64,256]{1,0:T(8,128)(2,1)S(1)}, u32[]{:S(2)}, u32[]{:S(2)}) collective-permute-start(bf16[64,256]{1,0:T(8,128)(2,1)S(1)} %get-tuple-element.52), channel_id=1, source_target_pairs={{0,1},{2,3},{4,5},{6,7},{1,0},{3,2},{5,4},{7,6},{8,9},{10,11},{12,... | collective-permute-start | bytes 98312 | tf_op jit(solution)/shard_map/own_near/ppermute | solution.py:72
  6.2 4.0 %collective-permute-start.4 = (bf16[32,32,256]{2,1,0:T(8,128)(2,1)S(1)}, bf16[32,32,256]{2,1,0:T(8,128)(2,1)}, u32[]{:S(2)}, u32[]{:S(2)}) collective-permute-start(bf16[32,32,256]{2,1,0:T(8,128)(2,1)S(1)} %constant_dynamic-slice_fusion.7), channel_id=1, source_target_pairs={{0,1},{2,3},{4,5},{6,7},{1,0},{3,2},{5,4},{7,6},{8,9},{10,11},{12,... | collective-permute-start | bytes 1572872 | tf_op jit(solution)/shard_map/swap/ppermute | solution.py:72
  6.8 26.2 %copy-start.3 = (bf16[3,3,256,256]{3,2,1,0:T(8,128)(2,1)S(1)}, bf16[3,3,256,256]{3,2,1,0:T(8,128)(2,1)}, u32[]{:S(2)}) copy-start(bf16[3,3,256,256]{3,2,1,0:T(8,128)(2,1)} %refs_8_.1) | copy-start | bytes 3538948
  6.9 5.6 %collective-permute-start.3 = (bf16[34,256]{1,0:T(8,128)(2,1)S(1)}, bf16[34,256]{1,0:T(8,128)(2,1)S(1)}, u32[]{:S(2)}, u32[]{:S(2)}) collective-permute-start(bf16[34,256]{1,0:T(8,128)(2,1)S(1)} %get-tuple-element.55), channel_id=1, source_target_pairs={{8,16},{16,8},{9,17},{17,9},{10,18},{18,10},{11,19},{19,11},{12,20... | collective-permute-start | bytes 52232 | tf_op jit(solution)/shard_map/own_band_far/ppermute | solution.py:72
  10.1 3.0 %collective-permute-start.2 = (bf16[34,256]{1,0:T(8,128)(2,1)S(1)}, bf16[34,256]{1,0:T(8,128)(2,1)S(1)}, u32[]{:S(2)}, u32[]{:S(2)}) collective-permute-start(bf16[34,256]{1,0:T(8,128)(2,1)S(1)} %get-tuple-element.56), channel_id=1, source_target_pairs={{0,8},{16,24},{8,0},{24,16},{1,9},{17,25},{9,1},{25,17},{2,10},{18... | collective-permute-start | bytes 52232 | tf_op jit(solution)/shard_map/own_band_near/ppermute | solution.py:72
  13.1 6.5 %collective-permute-start.5 = (bf16[16,32,256]{2,1,0:T(8,128)(2,1)S(1)}, bf16[16,32,256]{2,1,0:T(8,128)(2,1)}, u32[]{:S(2)}, u32[]{:S(2)}) collective-permute-start(bf16[16,32,256]{2,1,0:T(8,128)(2,1)S(1)} %get-tuple-element.23.refs_0_), channel_id=1, source_target_pairs={{2,10},{3,11},{4,4},{5,5},{6,22},{7,23},{8,0},{9,1},{12,28},{13,29... | collective-permute-start | bytes 786440 | tf_op jit(solution)/shard_map/hop0/ppermute | solution.py:52
  14.4 10.6 %collective-permute-start.7 = (bf16[16,32,256]{2,1,0:T(8,128)(2,1)S(1)}, bf16[16,32,256]{2,1,0:T(8,128)(2,1)}, u32[]{:S(2)}, u32[]{:S(2)}) collective-permute-start(bf16[16,32,256]{2,1,0:T(8,128)(2,1)S(1)} %get-tuple-element.24.refs_1_), channel_id=1, source_target_pairs={{2,2},{3,3},{4,20},{5,21},{6,14},{7,15},{8,8},{9,9},{12,4},{13,5},... | collective-permute-start | bytes 786440 | tf_op jit(solution)/shard_map/hop1/ppermute | solution.py:52
  16.4 11.1 %collective-permute-start.9 = (bf16[16,32,256]{2,1,0:T(8,128)(2,1)S(1)}, bf16[16,32,256]{2,1,0:T(8,128)(2,1)}, u32[]{:S(2)}, u32[]{:S(2)}) collective-permute-start(bf16[16,32,256]{2,1,0:T(8,128)(2,1)S(1)} %get-tuple-element.25.refs_2_), channel_id=1, source_target_pairs={{2,10},{3,11},{4,4},{5,5},{6,22},{7,23},{8,0},{9,1},{12,28},{13,29... | collective-permute-start | bytes 786440 | tf_op jit(solution)/shard_map/hop2/ppermute | solution.py:52
  17.7 13.3 %collective-permute-start.11 = (bf16[16,32,256]{2,1,0:T(8,128)(2,1)S(1)}, bf16[16,32,256]{2,1,0:T(8,128)(2,1)}, u32[]{:S(2)}, u32[]{:S(2)}) collective-permute-start(bf16[16,32,256]{2,1,0:T(8,128)(2,1)S(1)} %get-tuple-element.26.refs_3_), channel_id=1, source_target_pairs={{2,2},{3,3},{4,20},{5,21},{6,14},{7,15},{8,8},{9,9},{12,4},{13,5},... | collective-permute-start | bytes 786440 | tf_op jit(solution)/shard_map/hop3/ppermute | solution.py:52
  19.6 25.2 %collective-permute-start.6 = (bf16[16,32,256]{2,1,0:T(8,128)(2,1)}, bf16[16,32,256]{2,1,0:T(8,128)(2,1)S(1)}, u32[]{:S(2)}, u32[]{:S(2)}) collective-permute-start(bf16[16,32,256]{2,1,0:T(8,128)(2,1)} %collective-permute-done.5), channel_id=1, source_target_pairs={{10,8},{11,9},{4,16},{5,17},{22,24},{23,25},{0,2},{1,3},{28,18},{2... | collective-permute-start | bytes 786440 | tf_op jit(solution)/shard_map/land0/ppermute | solution.py:52
  25.0 19.8 %collective-permute-start.8 = (bf16[16,32,256]{2,1,0:T(8,128)(2,1)}, bf16[16,32,256]{2,1,0:T(8,128)(2,1)S(1)}, u32[]{:S(2)}, u32[]{:S(2)}) collective-permute-start(bf16[16,32,256]{2,1,0:T(8,128)(2,1)} %collective-permute-done.7), channel_id=1, source_target_pairs={{2,8},{3,9},{20,16},{21,17},{14,24},{15,25},{8,2},{9,3},{4,18},{5,... | collective-permute-start | bytes 786440 | tf_op jit(solution)/shard_map/land1/ppermute | solution.py:52
  27.5 17.4 %collective-permute-start.10 = (bf16[16,32,256]{2,1,0:T(8,128)(2,1)}, bf16[16,32,256]{2,1,0:T(8,128)(2,1)S(1)}, u32[]{:S(2)}, u32[]{:S(2)}) collective-permute-start(bf16[16,32,256]{2,1,0:T(8,128)(2,1)} %collective-permute-done.9), channel_id=1, source_target_pairs={{10,8},{11,9},{4,16},{5,17},{22,24},{23,25},{0,2},{1,3},{28,18},{2... | collective-permute-start | bytes 786440 | tf_op jit(solution)/shard_map/land2/ppermute | solution.py:52
  31.0 20.0 %collective-permute-start.12 = (bf16[16,32,256]{2,1,0:T(8,128)(2,1)}, bf16[16,32,256]{2,1,0:T(8,128)(2,1)S(1)}, u32[]{:S(2)}, u32[]{:S(2)}) collective-permute-start(bf16[16,32,256]{2,1,0:T(8,128)(2,1)} %collective-permute-done.11), channel_id=1, source_target_pairs={{2,8},{3,9},{20,16},{21,17},{14,24},{15,25},{8,2},{9,3},{4,18},{5,... | collective-permute-start | bytes 786440 | tf_op jit(solution)/shard_map/land3/ppermute | solution.py:52
  35.8 3.6 %collective-permute-start.13 = (bf16[96,256]{1,0:T(8,128)(2,1)S(1)}, bf16[96,256]{1,0:T(8,128)(2,1)S(1)}, u32[]{:S(2)}, u32[]{:S(2)}) collective-permute-start(bf16[96,256]{1,0:T(8,128)(2,1)S(1)} %get-tuple-element.28), channel_id=1, source_target_pairs={{0,1},{2,3},{4,5},{6,7},{1,0},{3,2},{5,4},{7,6},{8,9},{10,11},{12,... | collective-permute-start | bytes 147464 | tf_op jit(solution)/shard_map/ring_swap/ppermute | solution.py:72
  39.4 14.3 %collective-permute-start.14 = (bf16[192,256]{1,0:T(8,128)(2,1)S(1)}, bf16[192,256]{1,0:T(8,128)(2,1)S(1)}, u32[]{:S(2)}, u32[]{:S(2)}) collective-permute-start(bf16[192,256]{1,0:T(8,128)(2,1)S(1)} %constant_dynamic-update-slice_fusion.kept), channel_id=1, source_target_pairs={{2,8},{3,9},{4,16},{5,17},{6,24},{7,25},{8,2},{9,3},{12,18},{13,19... | collective-permute-start | bytes 294920 | tf_op jit(solution)/shard_map/ring/ppermute | solution.py:52
  53.7 6.8 %copy-start.1 = (bf16[3,3,256,256]{3,2,1,0:T(8,128)(2,1)S(1)}, bf16[3,3,256,256]{3,2,1,0:T(8,128)(2,1)}, u32[]{:S(2)}) copy-start(bf16[3,3,256,256]{3,2,1,0:T(8,128)(2,1)} %w_second.1) | copy-start | bytes 3538948
  54.6 10.5 %collective-permute-start.15 = (bf16[64,8,256]{2,1,0:T(8,128)(2,1)S(1)}, bf16[64,8,256]{2,1,0:T(8,128)(2,1)S(1)}, u32[]{:S(2)}, u32[]{:S(2)}) collective-permute-start(bf16[64,8,256]{2,1,0:T(8,128)(2,1)S(1)} %get-tuple-element.30), channel_id=1, source_target_pairs={{0,1},{2,3},{4,5},{6,7},{1,0},{3,2},{5,4},{7,6},{8,9},{10,11},{12,... | collective-permute-start | bytes 786440 | tf_op jit(solution)/shard_map/sym_near/ppermute | solution.py:72
  56.0 9.1 %collective-permute-start.16 = (bf16[64,8,256]{2,1,0:T(8,128)(2,1)S(1)}, bf16[64,8,256]{2,1,0:T(8,128)(2,1)S(1)}, u32[]{:S(2)}, u32[]{:S(2)}) collective-permute-start(bf16[64,8,256]{2,1,0:T(8,128)(2,1)S(1)} %get-tuple-element.31), channel_id=1, source_target_pairs={{1,2},{3,4},{5,6},{2,1},{4,3},{6,5},{9,10},{11,12},{13,14},{10,9},... | collective-permute-start | bytes 786440 | tf_op jit(solution)/shard_map/sym_far/ppermute | solution.py:72
  65.1 5.6 %copy-start.2 = (bf16[3,3,256,256]{3,2,1,0:T(8,128)(2,1)S(1)}, bf16[3,3,256,256]{3,2,1,0:T(8,128)(2,1)}, u32[]{:S(2)}) copy-start(bf16[3,3,256,256]{3,2,1,0:T(8,128)(2,1)} %w_third.1) | copy-start | bytes 3538948
  65.2 10.9 %collective-permute-start.17 = (bf16[6,48,256]{2,1,0:T(8,128)(2,1)S(1)}, bf16[6,48,256]{2,1,0:T(8,128)(2,1)S(1)}, u32[]{:S(2)}, u32[]{:S(2)}) collective-permute-start(bf16[6,48,256]{2,1,0:T(8,128)(2,1)S(1)} %pad_maximum_fusion), channel_id=1, source_target_pairs={{0,8},{16,24},{8,0},{24,16},{1,9},{17,25},{9,1},{25,17},{2,10},{18... | collective-permute-start | bytes 442376 | tf_op jit(solution)/shard_map/sym_band_near/ppermute | solution.py:72
  65.3 10.8 %collective-permute-start.18 = (bf16[6,48,256]{2,1,0:T(8,128)(2,1)S(1)}, bf16[6,48,256]{2,1,0:T(8,128)(2,1)S(1)}, u32[]{:S(2)}, u32[]{:S(2)}) collective-permute-start(bf16[6,48,256]{2,1,0:T(8,128)(2,1)S(1)} %pad_maximum_fusion.1), channel_id=1, source_target_pairs={{8,16},{16,8},{9,17},{17,9},{10,18},{18,10},{11,19},{19,11},{12,20... | collective-permute-start | bytes 442376 | tf_op jit(solution)/shard_map/sym_band_far/ppermute | solution.py:72

commit v6 on v5

--- a/solution.py
+++ b/solution.py
@@ -354,10 +354,10 @@
     band_near, band_far, *pieces = lax.optimization_barrier((band_near, band_far, *pieces))
     for i, piece in enumerate(pieces):
         with jax.named_scope(f"hop{i}"):
-            hops.append(place.hop(piece, i % 2))
+            hops.append(place.hop(piece, (0, 1, 1, 0)[i]))
     for i, hop in enumerate(hops):
         with jax.named_scope(f"land{i}"):
-            got.append(place.land(hop, i % 2))
+            got.append(place.land(hop, (0, 1, 1, 0)[i]))
     first, ring, other_ring = call(
         "first",
         lambda *refs: first_kernel(*refs, step=divisor(tile_rows, 16)),

time: 79.4 us -> 78.4 us (0.987)
  starting transfers between devices: 46.7 us -> 45.7 us
    ppermute x9, starting transfers between devices: 25.1 us -> 23.6 us  [chips(): return lax.ppermute(array, AXES, pairs)]
  transfers between devices with their start and end apart: 19 -> 19, of which waited for: 4 -> 6; matrix products, arithmetic and copies ran while one was open for 3% -> 3% of each run, Pallas kernels for 20% -> 20%
where the time goes in v6:
time: 78.4 us; the launch traced here: 78 us
  starting transfers between devices  45.7 us (58%)
  Pallas kernels  19.2 us (24%)
  waiting for transfers between devices  8.96 us (11%)
  local copies, waits for them, and re-layouts  3.5 us (4%)
    ppermute x9, starting transfers between devices, chips(): return lax.ppermute(array, AXES, pairs)  23.6 us
    ppermute x10, starting transfers between devices, pairwise(): return lax.ppermute(array, axis, pairs + [(j, i) for i, j in pairs])  22 us
    pallas_call x6, Pallas kernels, call(): pl.pallas_call(kernel, out_shape=outs, in_specs=in_specs or whole(len(ins...  19.2 us
    ppermute x9, waiting for transfers between devices, chips(): return lax.ppermute(array, AXES, pairs)  6.23 us
    ppermute x10, waiting for transfers between devices, pairwise(): return lax.ppermute(array, axis, pairs + [(j, i) for i, j in pairs])  2.73 us
  transfers between devices with their start and end apart: 19, of which 6 were waited for; matrix products, arithmetic and copies ran while one was open for 3% of the time, Pallas kernels for 20%

profile of v6, /device:TPU:5, one launch (start us, length us, event | category | flops | bytes accessed | tf_op | source)
XLA Modules:
  0.0 78.0 jit_solution(5172162125749202983)
XLA Ops:
  0.0 1.2 %fusion = (bf16[64,1,256]{2,1,0:T(2,128)(2,1)S(1)}, bf16[64,1,256]{2,1,0:T(2,128)(2,1)S(1)}) fusion(bf16[64,32,256]{2,1,0:T(8,128)(2,1)} %refs_0_.1), kind=kLoop, calls=%fused_computation.25 | loop fusion | bytes 131072 | tf_op jit(solution)/shard_map/slice | solution.py:345
  1.3 3.8 %collective-permute-start.1 = (bf16[64,256]{1,0:T(8,128)(2,1)S(1)}, bf16[64,256]{1,0:T(8,128)(2,1)S(1)}, u32[]{:S(2)}, u32[]{:S(2)}) collective-permute-start(bf16[64,256]{1,0:T(8,128)(2,1)S(1)} %get-tuple-element.51), channel_id=1, source_target_pairs={{1,2},{3,4},{5,6},{2,1},{4,3},{6,5},{9,10},{11,12},{13,14},{10,9},... | collective-permute-start | bytes 98312 | tf_op jit(solution)/shard_map/own_far/ppermute | solution.py:72
  5.1 1.1 %constant_dynamic-slice_fusion.7 = bf16[32,32,256]{2,1,0:T(8,128)(2,1)S(1)} fusion(bf16[64,32,256]{2,1,0:T(8,128)(2,1)} %refs_0_.1, s32[]{:T(128)S(6)} %select_n.97), kind=kLoop, calls=%fused_computation.23 | loop fusion | bytes 1048580 | tf_op jit(solution)/shard_map/dynamic_slice | solution.py:307
  6.2 0.5 collective-permute-start.4
  6.9 3.2 %collective-permute-start.3 = (bf16[34,256]{1,0:T(8,128)(2,1)S(1)}, bf16[34,256]{1,0:T(8,128)(2,1)S(1)}, u32[]{:S(2)}, u32[]{:S(2)}) collective-permute-start(bf16[34,256]{1,0:T(8,128)(2,1)S(1)} %get-tuple-element.55), channel_id=1, source_target_pairs={{8,16},{16,8},{9,17},{17,9},{10,18},{18,10},{11,19},{19,11},{12,20... | collective-permute-start | bytes 52232 | tf_op jit(solution)/shard_map/own_band_far/ppermute | solution.py:72
  10.2 1.1 %fusion.1 = (bf16[16,32,256]{2,1,0:T(8,128)(2,1)S(1)}, bf16[16,32,256]{2,1,0:T(8,128)(2,1)S(1)}) fusion(bf16[32,32,256]{2,1,0:T(8,128)(2,1)} %collective-permute-done.4), kind=kLoop, calls=%fused_computation.26 | loop fusion | bytes 1048576 | tf_op jit(solution)/shard_map/slice | solution.py:342
  11.3 1.2 %collective-permute-done.3.refs_4_ = bf16[34,256]{1,0:T(8,128)(2,1)S(1)} collective-permute-done((bf16[34,256]{1,0:T(8,128)(2,1)S(1)}, bf16[34,256]{1,0:T(8,128)(2,1)S(1)}, u32[]{:S(2)}, u32[]{:S(2)}) %collective-permute-start.3) | collective-permute-done | bytes 17440 | tf_op jit(solution)/shard_map/own_band_far/ppermute | solution.py:72
  12.5 0.6 collective-permute-done.2.refs_3_
  13.1 1.3 %collective-permute-start.5 = (bf16[16,32,256]{2,1,0:T(8,128)(2,1)S(1)}, bf16[16,32,256]{2,1,0:T(8,128)(2,1)}, u32[]{:S(2)}, u32[]{:S(2)}) collective-permute-start(bf16[16,32,256]{2,1,0:T(8,128)(2,1)S(1)} %get-tuple-element.23.refs_0_), channel_id=1, source_target_pairs={{2,10},{3,11},{4,4},{5,5},{6,22},{7,23},{8,0},{9,1},{12,28},{13,29... | collective-permute-start | bytes 786440 | tf_op jit(solution)/shard_map/hop0/ppermute | solution.py:52
  14.4 1.9 %collective-permute-start.7 = (bf16[16,32,256]{2,1,0:T(8,128)(2,1)S(1)}, bf16[16,32,256]{2,1,0:T(8,128)(2,1)}, u32[]{:S(2)}, u32[]{:S(2)}) collective-permute-start(bf16[16,32,256]{2,1,0:T(8,128)(2,1)S(1)} %get-tuple-element.24.refs_1_), channel_id=1, source_target_pairs={{2,2},{3,3},{4,20},{5,21},{6,14},{7,15},{8,8},{9,9},{12,4},{13,5},... | collective-permute-start | bytes 786440 | tf_op jit(solution)/shard_map/hop1/ppermute | solution.py:52
  16.4 1.9 %collective-permute-start.9 = (bf16[16,32,256]{2,1,0:T(8,128)(2,1)S(1)}, bf16[16,32,256]{2,1,0:T(8,128)(2,1)}, u32[]{:S(2)}, u32[]{:S(2)}) collective-permute-start(bf16[16,32,256]{2,1,0:T(8,128)(2,1)S(1)} %get-tuple-element.25.refs_2_), channel_id=1, source_target_pairs={{2,2},{3,3},{4,20},{5,21},{6,14},{7,15},{8,8},{9,9},{12,4},{13,5},... | collective-permute-start | bytes 786440 | tf_op jit(solution)/shard_map/hop2/ppermute | solution.py:52
  18.3 1.4 %collective-permute-start.11 = (bf16[16,32,256]{2,1,0:T(8,128)(2,1)S(1)}, bf16[16,32,256]{2,1,0:T(8,128)(2,1)}, u32[]{:S(2)}, u32[]{:S(2)}) collective-permute-start(bf16[16,32,256]{2,1,0:T(8,128)(2,1)S(1)} %get-tuple-element.26.refs_3_), channel_id=1, source_target_pairs={{2,10},{3,11},{4,4},{5,5},{6,22},{7,23},{8,0},{9,1},{12,28},{13,29... | collective-permute-start | bytes 786440 | tf_op jit(solution)/shard_map/hop3/ppermute | solution.py:52
  19.6 5.3 %collective-permute-start.6 = (bf16[16,32,256]{2,1,0:T(8,128)(2,1)}, bf16[16,32,256]{2,1,0:T(8,128)(2,1)S(1)}, u32[]{:S(2)}, u32[]{:S(2)}) collective-permute-start(bf16[16,32,256]{2,1,0:T(8,128)(2,1)} %collective-permute-done.5), channel_id=1, source_target_pairs={{10,8},{11,9},{4,16},{5,17},{22,24},{23,25},{0,2},{1,3},{28,18},{2... | collective-permute-start | bytes 786440 | tf_op jit(solution)/shard_map/land0/ppermute | solution.py:52
  25.0 2.4 %collective-permute-start.8 = (bf16[16,32,256]{2,1,0:T(8,128)(2,1)}, bf16[16,32,256]{2,1,0:T(8,128)(2,1)S(1)}, u32[]{:S(2)}, u32[]{:S(2)}) collective-permute-start(bf16[16,32,256]{2,1,0:T(8,128)(2,1)} %collective-permute-done.7), channel_id=1, source_target_pairs={{2,8},{3,9},{20,16},{21,17},{14,24},{15,25},{8,2},{9,3},{4,18},{5,... | collective-permute-start | bytes 786440 | tf_op jit(solution)/shard_map/land1/ppermute | solution.py:52
  27.5 1.9 %collective-permute-done.9 = bf16[16,32,256]{2,1,0:T(8,128)(2,1)} collective-permute-done((bf16[16,32,256]{2,1,0:T(8,128)(2,1)S(1)}, bf16[16,32,256]{2,1,0:T(8,128)(2,1)}, u32[]{:S(2)}, u32[]{:S(2)}) %collective-permute-start.9) | collective-permute-done | bytes 262176 | tf_op jit(solution)/shard_map/hop2/ppermute | solution.py:52
  29.3 1.9 %collective-permute-start.10 = (bf16[16,32,256]{2,1,0:T(8,128)(2,1)}, bf16[16,32,256]{2,1,0:T(8,128)(2,1)S(1)}, u32[]{:S(2)}, u32[]{:S(2)}) collective-permute-start(bf16[16,32,256]{2,1,0:T(8,128)(2,1)} %collective-permute-done.9), channel_id=1, source_target_pairs={{2,8},{3,9},{20,16},{21,17},{14,24},{15,25},{8,2},{9,3},{4,18},{5,... | collective-permute-start | bytes 786440 | tf_op jit(solution)/shard_map/land2/ppermute | solution.py:52
  31.3 3.6 %collective-permute-start.12 = (bf16[16,32,256]{2,1,0:T(8,128)(2,1)}, bf16[16,32,256]{2,1,0:T(8,128)(2,1)S(1)}, u32[]{:S(2)}, u32[]{:S(2)}) collective-permute-start(bf16[16,32,256]{2,1,0:T(8,128)(2,1)} %collective-permute-done.11), channel_id=1, source_target_pairs={{10,8},{11,9},{4,16},{5,17},{22,24},{23,25},{0,2},{1,3},{28,18},{2... | collective-permute-start | bytes 786440 | tf_op jit(solution)/shard_map/land3/ppermute | solution.py:52
  34.9 2.9 %first.1 = (bf16[64,32,256]{2,1,0:T(8,128)(2,1)S(1)}, bf16[96,256]{1,0:T(8,128)(2,1)S(1)}, bf16[96,256]{1,0:T(8,128)(2,1)S(1)}) custom-call(bf16[64,32,256]{2,1,0:T(8,128)(2,1)S(1)} %copy-done, bf16[64,256]{1,0:T(8,128)(2,1)S(1)} %collective-permute-done.refs_1_, bf16[64,256]{1,0:T(8,128)(2,1)S(1)} %collective-permute-done.1.refs_2_, ...), custom_call_target="tpu_custom_call" | custom-call | flops 2415919104 | bytes 1179648 | tf_op jit(solution)/shard_map/first/pallas_call | solution.py:324
  37.8 2.6 %collective-permute-start.13 = (bf16[96,256]{1,0:T(8,128)(2,1)S(1)}, bf16[96,256]{1,0:T(8,128)(2,1)S(1)}, u32[]{:S(2)}, u32[]{:S(2)}) collective-permute-start(bf16[96,256]{1,0:T(8,128)(2,1)S(1)} %get-tuple-element.28), channel_id=1, source_target_pairs={{0,1},{2,3},{4,5},{6,7},{1,0},{3,2},{5,4},{7,6},{8,9},{10,11},{12,... | collective-permute-start | bytes 147464 | tf_op jit(solution)/shard_map/ring_swap/ppermute | solution.py:72
  40.4 0.9 %collective-permute-done.13 = bf16[96,256]{1,0:T(8,128)(2,1)S(1)} collective-permute-done((bf16[96,256]{1,0:T(8,128)(2,1)S(1)}, bf16[96,256]{1,0:T(8,128)(2,1)S(1)}, u32[]{:S(2)}, u32[]{:S(2)}) %collective-permute-start.13) | collective-permute-done | bytes 49184 | tf_op jit(solution)/shard_map/ring_swap/ppermute | solution.py:72
  41.2 3.8 %collective-permute-start.14 = (bf16[192,256]{1,0:T(8,128)(2,1)S(1)}, bf16[192,256]{1,0:T(8,128)(2,1)S(1)}, u32[]{:S(2)}, u32[]{:S(2)}) collective-permute-start(bf16[192,256]{1,0:T(8,128)(2,1)S(1)} %constant_dynamic-update-slice_fusion.kept), channel_id=1, source_target_pairs={{2,8},{3,9},{4,16},{5,17},{6,24},{7,25},{8,2},{9,3},{12,18},{13,19... | collective-permute-start | bytes 294920 | tf_op jit(solution)/shard_map/ring/ppermute | solution.py:52
  45.1 2.5 %collective-permute-done.10.refs_6_ = bf16[16,32,256]{2,1,0:T(8,128)(2,1)S(1)} collective-permute-done((bf16[16,32,256]{2,1,0:T(8,128)(2,1)}, bf16[16,32,256]{2,1,0:T(8,128)(2,1)S(1)}, u32[]{:S(2)}, u32[]{:S(2)}) %collective-permute-start.10) | collective-permute-done | bytes 262176 | tf_op jit(solution)/shard_map/land2/ppermute | solution.py:52
  47.6 1.8 %collective-permute-done.12.refs_7_ = bf16[16,32,256]{2,1,0:T(8,128)(2,1)S(1)} collective-permute-done((bf16[16,32,256]{2,1,0:T(8,128)(2,1)}, bf16[16,32,256]{2,1,0:T(8,128)(2,1)S(1)}, u32[]{:S(2)}, u32[]{:S(2)}) %collective-permute-start.12) | collective-permute-done | bytes 262176 | tf_op jit(solution)/shard_map/land3/ppermute | solution.py:52
  49.4 2.7 %turned.1 = bf16[32,64,256]{2,1,0:T(8,128)(2,1)S(1)} custom-call(bf16[16,32,256]{2,1,0:T(8,128)(2,1)S(1)} %get-tuple-element.23.refs_0_, bf16[16,32,256]{2,1,0:T(8,128)(2,1)S(1)} %get-tuple-element.24.refs_1_, bf16[16,32,256]{2,1,0:T(8,128)(2,1)S(1)} %get-tuple-element.25.refs_2_, bf16[16,32,256]{2,1,0:T(8,128)(2,1)S(1)} %get-tuple-element.26.refs_3_, ...), custom_call_target="tpu_custom_call" | custom-call | flops 2415919104 | bytes 1179648 | tf_op jit(solution)/shard_map/turned/pallas_call | solution.py:324
  52.2 0.9 %mean.1 = (bf16[64,32,256]{2,1,0:T(8,128)(2,1)S(1)}, bf16[64,8,256]{2,1,0:T(8,128)(2,1)S(1)}, bf16[64,8,256]{2,1,0:T(8,128)(2,1)S(1)}) custom-call(bf16[64,32,256]{2,1,0:T(8,128)(2,1)S(1)} %get-tuple-element.22.first, bf16[32,64,256]{2,1,0:T(8,128)(2,1)S(1)} %turned.1, bf16[192,256]{1,0:T(8,128)(2,1)S(1)} %constant_dynamic-update-slice_fusion.kept, ...), custom_call_target="tpu_custom_call" | custom-call | bytes 1179648 | tf_op jit(solution)/shard_map/mean/pallas_call | solution.py:324
  53.1 3.1 %collective-permute-start.15 = (bf16[64,8,256]{2,1,0:T(8,128)(2,1)S(1)}, bf16[64,8,256]{2,1,0:T(8,128)(2,1)S(1)}, u32[]{:S(2)}, u32[]{:S(2)}) collective-permute-start(bf16[64,8,256]{2,1,0:T(8,128)(2,1)S(1)} %get-tuple-element.30), channel_id=1, source_target_pairs={{0,1},{2,3},{4,5},{6,7},{1,0},{3,2},{5,4},{7,6},{8,9},{10,11},{12,... | collective-permute-start | bytes 786440 | tf_op jit(solution)/shard_map/sym_near/ppermute | solution.py:72
  56.2 3.5 %collective-permute-start.16 = (bf16[64,8,256]{2,1,0:T(8,128)(2,1)S(1)}, bf16[64,8,256]{2,1,0:T(8,128)(2,1)S(1)}, u32[]{:S(2)}, u32[]{:S(2)}) collective-permute-start(bf16[64,8,256]{2,1,0:T(8,128)(2,1)S(1)} %get-tuple-element.31), channel_id=1, source_target_pairs={{1,2},{3,4},{5,6},{2,1},{4,3},{6,5},{9,10},{11,12},{13,14},{10,9},... | collective-permute-start | bytes 786440 | tf_op jit(solution)/shard_map/sym_far/ppermute | solution.py:72
  59.7 4.6 %inner_second.1.refs_3_ = bf16[60,32,256]{2,1,0:T(8,128)(2,1)S(1)} custom-call(bf16[64,32,256]{2,1,0:T(8,128)(2,1)S(1)} %get-tuple-element.29.refs_0_.sym, bf16[3,3,256,256]{3,2,1,0:T(8,128)(2,1)S(1)} %copy-done.1), custom_call_target="tpu_custom_call" | custom-call | flops 4529848320 | bytes 1179648 | tf_op jit(solution)/shard_map/inner_second/pallas_call | solution.py:324
  64.5 1.7 %collective-permute-start.17 = (bf16[6,48,256]{2,1,0:T(8,128)(2,1)S(1)}, bf16[6,48,256]{2,1,0:T(8,128)(2,1)S(1)}, u32[]{:S(2)}, u32[]{:S(2)}) collective-permute-start(bf16[6,48,256]{2,1,0:T(8,128)(2,1)S(1)} %pad_maximum_fusion), channel_id=1, source_target_pairs={{0,8},{16,24},{8,0},{24,16},{1,9},{17,25},{9,1},{25,17},{2,10},{18... | collective-permute-start | bytes 442376 | tf_op jit(solution)/shard_map/sym_band_near/ppermute | solution.py:72
  66.2 3.5 %collective-permute-start.18 = (bf16[6,48,256]{2,1,0:T(8,128)(2,1)S(1)}, bf16[6,48,256]{2,1,0:T(8,128)(2,1)S(1)}, u32[]{:S(2)}, u32[]{:S(2)}) collective-permute-start(bf16[6,48,256]{2,1,0:T(8,128)(2,1)S(1)} %pad_maximum_fusion.1), channel_id=1, source_target_pairs={{8,16},{16,8},{9,17},{17,9},{10,18},{18,10},{11,19},{19,11},{12,20... | collective-permute-start | bytes 442376 | tf_op jit(solution)/shard_map/sym_band_far/ppermute | solution.py:72
  69.7 5.4 %middle.1 = (bf16[64,32,256]{2,1,0:T(8,128)(2,1)}, bf16[8,48,256]{2,1,0:T(8,128)(2,1)S(1)}, bf16[8,48,256]{2,1,0:T(8,128)(2,1)S(1)}) custom-call(bf16[64,32,256]{2,1,0:T(8,128)(2,1)S(1)} %get-tuple-element.29.refs_0_.sym, bf16[64,8,256]{2,1,0:T(8,128)(2,1)S(1)} %collective-permute-done.15.refs_1_.near, ...), custom_call_target="tpu_custom_call" | custom-call | flops 4227858432 | bytes 1179648 | tf_op jit(solution)/shard_map/middle/pallas_call | solution.py:324
  75.1 2.7 %edges.1 = bf16[64,32,256]{2,1,0:T(8,128)(2,1)} custom-call(bf16[64,32,256]{2,1,0:T(8,128)(2,1)} %get-tuple-element.32._, bf16[64,32,256]{2,1,0:T(8,128)(2,1)S(1)} %get-tuple-element.29.refs_0_.sym, bf16[64,8,256]{2,1,0:T(8,128)(2,1)S(1)} %collective-permute-done.15.refs_1_.near, ...), custom_call_target="tpu_custom_call", output_to_operand_aliasing={{}: (0, {})} | custom-call | flops 1811939328 | bytes 1179648 | tf_op jit(solution)/shard_map/edges/pallas_call | solution.py:324
  (37 shorter events, 0.4 us)
Async XLA Ops:
  0.0 6.7 %copy-start = (bf16[64,32,256]{2,1,0:T(8,128)(2,1)S(1)}, bf16[64,32,256]{2,1,0:T(8,128)(2,1)}, u32[]{:S(2)}) copy-start(bf16[64,32,256]{2,1,0:T(8,128)(2,1)} %refs_0_.1) | copy-start | bytes 3145732
  1.3 5.6 %collective-permute-start.1 = (bf16[64,256]{1,0:T(8,128)(2,1)S(1)}, bf16[64,256]{1,0:T(8,128)(2,1)S(1)}, u32[]{:S(2)}, u32[]{:S(2)}) collective-permute-start(bf16[64,256]{1,0:T(8,128)(2,1)S(1)} %get-tuple-element.51), channel_id=1, source_target_pairs={{1,2},{3,4},{5,6},{2,1},{4,3},{6,5},{9,10},{11,12},{13,14},{10,9},... | collective-permute-start | bytes 98312 | tf_op jit(solution)/shard_map/own_far/ppermute | solution.py:72
  5.0 1.8 %collective-permute-start = (bf16[64,256]{1,0:T(8,128)(2,1)S(1)}, bf16[64,256]{1,0:T(8,128)(2,1)S(1)}, u32[]{:S(2)}, u32[]{:S(2)}) collective-permute-start(bf16[64,256]{1,0:T(8,128)(2,1)S(1)} %get-tuple-element.52), channel_id=1, source_target_pairs={{0,1},{2,3},{4,5},{6,7},{1,0},{3,2},{5,4},{7,6},{8,9},{10,11},{12,... | collective-permute-start | bytes 98312 | tf_op jit(solution)/shard_map/own_near/ppermute | solution.py:72
  6.2 4.0 %collective-permute-start.4 = (bf16[32,32,256]{2,1,0:T(8,128)(2,1)S(1)}, bf16[32,32,256]{2,1,0:T(8,128)(2,1)}, u32[]{:S(2)}, u32[]{:S(2)}) collective-permute-start(bf16[32,32,256]{2,1,0:T(8,128)(2,1)S(1)} %constant_dynamic-slice_fusion.7), channel_id=1, source_target_pairs={{0,1},{2,3},{4,5},{6,7},{1,0},{3,2},{5,4},{7,6},{8,9},{10,11},{12,... | collective-permute-start | bytes 1572872 | tf_op jit(solution)/shard_map/swap/ppermute | solution.py:72
  6.8 28.1 %copy-start.3 = (bf16[3,3,256,256]{3,2,1,0:T(8,128)(2,1)S(1)}, bf16[3,3,256,256]{3,2,1,0:T(8,128)(2,1)}, u32[]{:S(2)}) copy-start(bf16[3,3,256,256]{3,2,1,0:T(8,128)(2,1)} %refs_8_.1) | copy-start | bytes 3538948
  6.9 5.6 %collective-permute-start.3 = (bf16[34,256]{1,0:T(8,128)(2,1)S(1)}, bf16[34,256]{1,0:T(8,128)(2,1)S(1)}, u32[]{:S(2)}, u32[]{:S(2)}) collective-permute-start(bf16[34,256]{1,0:T(8,128)(2,1)S(1)} %get-tuple-element.55), channel_id=1, source_target_pairs={{8,16},{16,8},{9,17},{17,9},{10,18},{18,10},{11,19},{19,11},{12,20... | collective-permute-start | bytes 52232 | tf_op jit(solution)/shard_map/own_band_far/ppermute | solution.py:72
  10.1 3.0 %collective-permute-start.2 = (bf16[34,256]{1,0:T(8,128)(2,1)S(1)}, bf16[34,256]{1,0:T(8,128)(2,1)S(1)}, u32[]{:S(2)}, u32[]{:S(2)}) collective-permute-start(bf16[34,256]{1,0:T(8,128)(2,1)S(1)} %get-tuple-element.56), channel_id=1, source_target_pairs={{0,8},{16,24},{8,0},{24,16},{1,9},{17,25},{9,1},{25,17},{2,10},{18... | collective-permute-start | bytes 52232 | tf_op jit(solution)/shard_map/own_band_near/ppermute | solution.py:72
  13.1 6.5 %collective-permute-start.5 = (bf16[16,32,256]{2,1,0:T(8,128)(2,1)S(1)}, bf16[16,32,256]{2,1,0:T(8,128)(2,1)}, u32[]{:S(2)}, u32[]{:S(2)}) collective-permute-start(bf16[16,32,256]{2,1,0:T(8,128)(2,1)S(1)} %get-tuple-element.23.refs_0_), channel_id=1, source_target_pairs={{2,10},{3,11},{4,4},{5,5},{6,22},{7,23},{8,0},{9,1},{12,28},{13,29... | collective-permute-start | bytes 786440 | tf_op jit(solution)/shard_map/hop0/ppermute | solution.py:52
  14.4 10.6 %collective-permute-start.7 = (bf16[16,32,256]{2,1,0:T(8,128)(2,1)S(1)}, bf16[16,32,256]{2,1,0:T(8,128)(2,1)}, u32[]{:S(2)}, u32[]{:S(2)}) collective-permute-start(bf16[16,32,256]{2,1,0:T(8,128)(2,1)S(1)} %get-tuple-element.24.refs_1_), channel_id=1, source_target_pairs={{2,2},{3,3},{4,20},{5,21},{6,14},{7,15},{8,8},{9,9},{12,4},{13,5},... | collective-permute-start | bytes 786440 | tf_op jit(solution)/shard_map/hop1/ppermute | solution.py:52
  16.4 13.0 %collective-permute-start.9 = (bf16[16,32,256]{2,1,0:T(8,128)(2,1)S(1)}, bf16[16,32,256]{2,1,0:T(8,128)(2,1)}, u32[]{:S(2)}, u32[]{:S(2)}) collective-permute-start(bf16[16,32,256]{2,1,0:T(8,128)(2,1)S(1)} %get-tuple-element.25.refs_2_), channel_id=1, source_target_pairs={{2,2},{3,3},{4,20},{5,21},{6,14},{7,15},{8,8},{9,9},{12,4},{13,5},... | collective-permute-start | bytes 786440 | tf_op jit(solution)/shard_map/hop2/ppermute | solution.py:52
  18.3 13.0 %collective-permute-start.11 = (bf16[16,32,256]{2,1,0:T(8,128)(2,1)S(1)}, bf16[16,32,256]{2,1,0:T(8,128)(2,1)}, u32[]{:S(2)}, u32[]{:S(2)}) collective-permute-start(bf16[16,32,256]{2,1,0:T(8,128)(2,1)S(1)} %get-tuple-element.26.refs_3_), channel_id=1, source_target_pairs={{2,10},{3,11},{4,4},{5,5},{6,22},{7,23},{8,0},{9,1},{12,28},{13,29... | collective-permute-start | bytes 786440 | tf_op jit(solution)/shard_map/hop3/ppermute | solution.py:52
  19.6 25.4 %collective-permute-start.6 = (bf16[16,32,256]{2,1,0:T(8,128)(2,1)}, bf16[16,32,256]{2,1,0:T(8,128)(2,1)S(1)}, u32[]{:S(2)}, u32[]{:S(2)}) collective-permute-start(bf16[16,32,256]{2,1,0:T(8,128)(2,1)} %collective-permute-done.5), channel_id=1, source_target_pairs={{10,8},{11,9},{4,16},{5,17},{22,24},{23,25},{0,2},{1,3},{28,18},{2... | collective-permute-start | bytes 786440 | tf_op jit(solution)/shard_map/land0/ppermute | solution.py:52
  25.0 20.1 %collective-permute-start.8 = (bf16[16,32,256]{2,1,0:T(8,128)(2,1)}, bf16[16,32,256]{2,1,0:T(8,128)(2,1)S(1)}, u32[]{:S(2)}, u32[]{:S(2)}) collective-permute-start(bf16[16,32,256]{2,1,0:T(8,128)(2,1)} %collective-permute-done.7), channel_id=1, source_target_pairs={{2,8},{3,9},{20,16},{21,17},{14,24},{15,25},{8,2},{9,3},{4,18},{5,... | collective-permute-start | bytes 786440 | tf_op jit(solution)/shard_map/land1/ppermute | solution.py:52
  29.3 18.3 %collective-permute-start.10 = (bf16[16,32,256]{2,1,0:T(8,128)(2,1)}, bf16[16,32,256]{2,1,0:T(8,128)(2,1)S(1)}, u32[]{:S(2)}, u32[]{:S(2)}) collective-permute-start(bf16[16,32,256]{2,1,0:T(8,128)(2,1)} %collective-permute-done.9), channel_id=1, source_target_pairs={{2,8},{3,9},{20,16},{21,17},{14,24},{15,25},{8,2},{9,3},{4,18},{5,... | collective-permute-start | bytes 786440 | tf_op jit(solution)/shard_map/land2/ppermute | solution.py:52
  31.3 18.2 %collective-permute-start.12 = (bf16[16,32,256]{2,1,0:T(8,128)(2,1)}, bf16[16,32,256]{2,1,0:T(8,128)(2,1)S(1)}, u32[]{:S(2)}, u32[]{:S(2)}) collective-permute-start(bf16[16,32,256]{2,1,0:T(8,128)(2,1)} %collective-permute-done.11), channel_id=1, source_target_pairs={{10,8},{11,9},{4,16},{5,17},{22,24},{23,25},{0,2},{1,3},{28,18},{2... | collective-permute-start | bytes 786440 | tf_op jit(solution)/shard_map/land3/ppermute | solution.py:52
  37.8 3.5 %collective-permute-start.13 = (bf16[96,256]{1,0:T(8,128)(2,1)S(1)}, bf16[96,256]{1,0:T(8,128)(2,1)S(1)}, u32[]{:S(2)}, u32[]{:S(2)}) collective-permute-start(bf16[96,256]{1,0:T(8,128)(2,1)S(1)} %get-tuple-element.28), channel_id=1, source_target_pairs={{0,1},{2,3},{4,5},{6,7},{1,0},{3,2},{5,4},{7,6},{8,9},{10,11},{12,... | collective-permute-start | bytes 147464 | tf_op jit(solution)/shard_map/ring_swap/ppermute | solution.py:72
  41.2 10.9 %collective-permute-start.14 = (bf16[192,256]{1,0:T(8,128)(2,1)S(1)}, bf16[192,256]{1,0:T(8,128)(2,1)S(1)}, u32[]{:S(2)}, u32[]{:S(2)}) collective-permute-start(bf16[192,256]{1,0:T(8,128)(2,1)S(1)} %constant_dynamic-update-slice_fusion.kept), channel_id=1, source_target_pairs={{2,8},{3,9},{4,16},{5,17},{6,24},{7,25},{8,2},{9,3},{12,18},{13,19... | collective-permute-start | bytes 294920 | tf_op jit(solution)/shard_map/ring/ppermute | solution.py:52
  52.1 7.6 %copy-start.1 = (bf16[3,3,256,256]{3,2,1,0:T(8,128)(2,1)S(1)}, bf16[3,3,256,256]{3,2,1,0:T(8,128)(2,1)}, u32[]{:S(2)}) copy-start(bf16[3,3,256,256]{3,2,1,0:T(8,128)(2,1)} %w_second.1) | copy-start | bytes 3538948
  53.1 11.3 %collective-permute-start.15 = (bf16[64,8,256]{2,1,0:T(8,128)(2,1)S(1)}, bf16[64,8,256]{2,1,0:T(8,128)(2,1)S(1)}, u32[]{:S(2)}, u32[]{:S(2)}) collective-permute-start(bf16[64,8,256]{2,1,0:T(8,128)(2,1)S(1)} %get-tuple-element.30), channel_id=1, source_target_pairs={{0,1},{2,3},{4,5},{6,7},{1,0},{3,2},{5,4},{7,6},{8,9},{10,11},{12,... | collective-permute-start | bytes 786440 | tf_op jit(solution)/shard_map/sym_near/ppermute | solution.py:72
  56.2 8.2 %collective-permute-start.16 = (bf16[64,8,256]{2,1,0:T(8,128)(2,1)S(1)}, bf16[64,8,256]{2,1,0:T(8,128)(2,1)S(1)}, u32[]{:S(2)}, u32[]{:S(2)}) collective-permute-start(bf16[64,8,256]{2,1,0:T(8,128)(2,1)S(1)} %get-tuple-element.31), channel_id=1, source_target_pairs={{1,2},{3,4},{5,6},{2,1},{4,3},{6,5},{9,10},{11,12},{13,14},{10,9},... | collective-permute-start | bytes 786440 | tf_op jit(solution)/shard_map/sym_far/ppermute | solution.py:72
  64.3 5.4 %copy-start.2 = (bf16[3,3,256,256]{3,2,1,0:T(8,128)(2,1)S(1)}, bf16[3,3,256,256]{3,2,1,0:T(8,128)(2,1)}, u32[]{:S(2)}) copy-start(bf16[3,3,256,256]{3,2,1,0:T(8,128)(2,1)} %w_third.1) | copy-start | bytes 3538948
  64.5 10.6 %collective-permute-start.17 = (bf16[6,48,256]{2,1,0:T(8,128)(2,1)S(1)}, bf16[6,48,256]{2,1,0:T(8,128)(2,1)S(1)}, u32[]{:S(2)}, u32[]{:S(2)}) collective-permute-start(bf16[6,48,256]{2,1,0:T(8,128)(2,1)S(1)} %pad_maximum_fusion), channel_id=1, source_target_pairs={{0,8},{16,24},{8,0},{24,16},{1,9},{17,25},{9,1},{25,17},{2,10},{18... | collective-permute-start | bytes 442376 | tf_op jit(solution)/shard_map/sym_band_near/ppermute | solution.py:72
  66.2 8.9 %collective-permute-start.18 = (bf16[6,48,256]{2,1,0:T(8,128)(2,1)S(1)}, bf16[6,48,256]{2,1,0:T(8,128)(2,1)S(1)}, u32[]{:S(2)}, u32[]{:S(2)}) collective-permute-start(bf16[6,48,256]{2,1,0:T(8,128)(2,1)S(1)} %pad_maximum_fusion.1), channel_id=1, source_target_pairs={{8,16},{16,8},{9,17},{17,9},{10,18},{18,10},{11,19},{19,11},{12,20... | collective-permute-start | bytes 442376 | tf_op jit(solution)/shard_map/sym_band_far/ppermute | solution.py:72

commit v7 on v6

--- a/solution.py
+++ b/solution.py
@@ -374,7 +374,7 @@
         got_ring = place.direct(ring)
     (turned,) = call(
         "turned",
-        lambda *refs: turned_kernel(*refs, step=divisor(tile_cols, 8)),
+        lambda *refs: turned_kernel(*refs, step=divisor(tile_cols, 32)),
         (shape(tile_cols, tile_rows),),
         (*pieces, *got, w_first),
         [
@@ -396,7 +396,7 @@
     rows2, rows3 = tile_rows - 4, tile_rows - 2 * EDGE
     (inner,) = call(
         "inner_second",
-        lambda *refs: inner_second_kernel(*refs, step=divisor(rows2, 20)),
+        lambda *refs: inner_second_kernel(*refs, step=divisor(rows2, 30)),
         (shape(rows2, tile_cols),),
         (sym, w_second),
         [scratch(tile_rows, tile_cols, 3 * channels)],
@@ -411,7 +411,7 @@
     band_near = pairwise(band((1 - up) * last), "row", 0, "sym_band_near")
     band_far = pairwise(band(up * last), "row", 1, "sym_band_far")
     width = tile_cols + 2 * STRIP
-    step = divisor(rows3, 26)
+    step = divisor(rows3, 13)
     features, tops, bottoms = call(
         "middle",
         lambda *refs: middle_kernel(*refs, steps=(divisor(rows2, 30), step)),

time: 78.4 us -> 78.3 us (level)
  no operation moved by 1% of the time
where the time goes in v7:
time: 78.3 us; the launch traced here: 77.8 us
  starting transfers between devices  45.7 us (58%)
  Pallas kernels  19 us (24%)
  waiting for transfers between devices  8.96 us (11%)
  local copies, waits for them, and re-layouts  3.5 us (4%)
    ppermute x9, starting transfers between devices, chips(): return lax.ppermute(array, AXES, pairs)  23.6 us
    ppermute x10, starting transfers between devices, pairwise(): return lax.ppermute(array, axis, pairs + [(j, i) for i, j in pairs])  22.1 us
    pallas_call x6, Pallas kernels, call(): pl.pallas_call(kernel, out_shape=outs, in_specs=in_specs or whole(len(ins...  19 us
    ppermute x9, waiting for transfers between devices, chips(): return lax.ppermute(array, AXES, pairs)  6.23 us
    ppermute x10, waiting for transfers between devices, pairwise(): return lax.ppermute(array, axis, pairs + [(j, i) for i, j in pairs])  2.73 us
  transfers between devices with their start and end apart: 19, of which 6 were waited for; matrix products, arithmetic and copies ran while one was open for 3% of the time, Pallas kernels for 20%

profile of v7, /device:TPU:5, one launch (start us, length us, event | category | flops | bytes accessed | tf_op | source)
XLA Modules:
  0.0 77.8 jit_solution(2281947555507527617)
XLA Ops:
  0.0 1.2 %fusion = (bf16[64,1,256]{2,1,0:T(2,128)(2,1)S(1)}, bf16[64,1,256]{2,1,0:T(2,128)(2,1)S(1)}) fusion(bf16[64,32,256]{2,1,0:T(8,128)(2,1)} %refs_0_.1), kind=kLoop, calls=%fused_computation.25 | loop fusion | bytes 131072 | tf_op jit(solution)/shard_map/slice | solution.py:345
  1.3 3.8 %collective-permute-start.1 = (bf16[64,256]{1,0:T(8,128)(2,1)S(1)}, bf16[64,256]{1,0:T(8,128)(2,1)S(1)}, u32[]{:S(2)}, u32[]{:S(2)}) collective-permute-start(bf16[64,256]{1,0:T(8,128)(2,1)S(1)} %get-tuple-element.51), channel_id=1, source_target_pairs={{1,2},{3,4},{5,6},{2,1},{4,3},{6,5},{9,10},{11,12},{13,14},{10,9},... | collective-permute-start | bytes 98312 | tf_op jit(solution)/shard_map/own_far/ppermute | solution.py:72
  5.1 1.1 %constant_dynamic-slice_fusion.7 = bf16[32,32,256]{2,1,0:T(8,128)(2,1)S(1)} fusion(bf16[64,32,256]{2,1,0:T(8,128)(2,1)} %refs_0_.1, s32[]{:T(128)S(6)} %select_n.97), kind=kLoop, calls=%fused_computation.23 | loop fusion | bytes 1048580 | tf_op jit(solution)/shard_map/dynamic_slice | solution.py:307
  6.2 0.5 collective-permute-start.4
  6.9 3.2 %collective-permute-start.3 = (bf16[34,256]{1,0:T(8,128)(2,1)S(1)}, bf16[34,256]{1,0:T(8,128)(2,1)S(1)}, u32[]{:S(2)}, u32[]{:S(2)}) collective-permute-start(bf16[34,256]{1,0:T(8,128)(2,1)S(1)} %get-tuple-element.55), channel_id=1, source_target_pairs={{8,16},{16,8},{9,17},{17,9},{10,18},{18,10},{11,19},{19,11},{12,20... | collective-permute-start | bytes 52232 | tf_op jit(solution)/shard_map/own_band_far/ppermute | solution.py:72
  10.2 1.1 %fusion.1 = (bf16[16,32,256]{2,1,0:T(8,128)(2,1)S(1)}, bf16[16,32,256]{2,1,0:T(8,128)(2,1)S(1)}) fusion(bf16[32,32,256]{2,1,0:T(8,128)(2,1)} %collective-permute-done.4), kind=kLoop, calls=%fused_computation.26 | loop fusion | bytes 1048576 | tf_op jit(solution)/shard_map/slice | solution.py:342
  11.3 1.2 %collective-permute-done.3.refs_4_ = bf16[34,256]{1,0:T(8,128)(2,1)S(1)} collective-permute-done((bf16[34,256]{1,0:T(8,128)(2,1)S(1)}, bf16[34,256]{1,0:T(8,128)(2,1)S(1)}, u32[]{:S(2)}, u32[]{:S(2)}) %collective-permute-start.3) | collective-permute-done | bytes 17440 | tf_op jit(solution)/shard_map/own_band_far/ppermute | solution.py:72
  12.5 0.6 collective-permute-done.2.refs_3_
  13.1 1.3 %collective-permute-start.5 = (bf16[16,32,256]{2,1,0:T(8,128)(2,1)S(1)}, bf16[16,32,256]{2,1,0:T(8,128)(2,1)}, u32[]{:S(2)}, u32[]{:S(2)}) collective-permute-start(bf16[16,32,256]{2,1,0:T(8,128)(2,1)S(1)} %get-tuple-element.23.refs_0_), channel_id=1, source_target_pairs={{2,10},{3,11},{4,4},{5,5},{6,22},{7,23},{8,0},{9,1},{12,28},{13,29... | collective-permute-start | bytes 786440 | tf_op jit(solution)/shard_map/hop0/ppermute | solution.py:52
  14.4 1.9 %collective-permute-start.7 = (bf16[16,32,256]{2,1,0:T(8,128)(2,1)S(1)}, bf16[16,32,256]{2,1,0:T(8,128)(2,1)}, u32[]{:S(2)}, u32[]{:S(2)}) collective-permute-start(bf16[16,32,256]{2,1,0:T(8,128)(2,1)S(1)} %get-tuple-element.24.refs_1_), channel_id=1, source_target_pairs={{2,2},{3,3},{4,20},{5,21},{6,14},{7,15},{8,8},{9,9},{12,4},{13,5},... | collective-permute-start | bytes 786440 | tf_op jit(solution)/shard_map/hop1/ppermute | solution.py:52
  16.4 1.9 %collective-permute-start.9 = (bf16[16,32,256]{2,1,0:T(8,128)(2,1)S(1)}, bf16[16,32,256]{2,1,0:T(8,128)(2,1)}, u32[]{:S(2)}, u32[]{:S(2)}) collective-permute-start(bf16[16,32,256]{2,1,0:T(8,128)(2,1)S(1)} %get-tuple-element.25.refs_2_), channel_id=1, source_target_pairs={{2,2},{3,3},{4,20},{5,21},{6,14},{7,15},{8,8},{9,9},{12,4},{13,5},... | collective-permute-start | bytes 786440 | tf_op jit(solution)/shard_map/hop2/ppermute | solution.py:52
  18.3 1.4 %collective-permute-start.11 = (bf16[16,32,256]{2,1,0:T(8,128)(2,1)S(1)}, bf16[16,32,256]{2,1,0:T(8,128)(2,1)}, u32[]{:S(2)}, u32[]{:S(2)}) collective-permute-start(bf16[16,32,256]{2,1,0:T(8,128)(2,1)S(1)} %get-tuple-element.26.refs_3_), channel_id=1, source_target_pairs={{2,10},{3,11},{4,4},{5,5},{6,22},{7,23},{8,0},{9,1},{12,28},{13,29... | collective-permute-start | bytes 786440 | tf_op jit(solution)/shard_map/hop3/ppermute | solution.py:52
  19.6 5.3 %collective-permute-start.6 = (bf16[16,32,256]{2,1,0:T(8,128)(2,1)}, bf16[16,32,256]{2,1,0:T(8,128)(2,1)S(1)}, u32[]{:S(2)}, u32[]{:S(2)}) collective-permute-start(bf16[16,32,256]{2,1,0:T(8,128)(2,1)} %collective-permute-done.5), channel_id=1, source_target_pairs={{10,8},{11,9},{4,16},{5,17},{22,24},{23,25},{0,2},{1,3},{28,18},{2... | collective-permute-start | bytes 786440 | tf_op jit(solution)/shard_map/land0/ppermute | solution.py:52
  25.0 2.4 %collective-permute-start.8 = (bf16[16,32,256]{2,1,0:T(8,128)(2,1)}, bf16[16,32,256]{2,1,0:T(8,128)(2,1)S(1)}, u32[]{:S(2)}, u32[]{:S(2)}) collective-permute-start(bf16[16,32,256]{2,1,0:T(8,128)(2,1)} %collective-permute-done.7), channel_id=1, source_target_pairs={{2,8},{3,9},{20,16},{21,17},{14,24},{15,25},{8,2},{9,3},{4,18},{5,... | collective-permute-start | bytes 786440 | tf_op jit(solution)/shard_map/land1/ppermute | solution.py:52
  27.5 1.9 %collective-permute-done.9 = bf16[16,32,256]{2,1,0:T(8,128)(2,1)} collective-permute-done((bf16[16,32,256]{2,1,0:T(8,128)(2,1)S(1)}, bf16[16,32,256]{2,1,0:T(8,128)(2,1)}, u32[]{:S(2)}, u32[]{:S(2)}) %collective-permute-start.9) | collective-permute-done | bytes 262176 | tf_op jit(solution)/shard_map/hop2/ppermute | solution.py:52
  29.3 1.9 %collective-permute-start.10 = (bf16[16,32,256]{2,1,0:T(8,128)(2,1)}, bf16[16,32,256]{2,1,0:T(8,128)(2,1)S(1)}, u32[]{:S(2)}, u32[]{:S(2)}) collective-permute-start(bf16[16,32,256]{2,1,0:T(8,128)(2,1)} %collective-permute-done.9), channel_id=1, source_target_pairs={{2,8},{3,9},{20,16},{21,17},{14,24},{15,25},{8,2},{9,3},{4,18},{5,... | collective-permute-start | bytes 786440 | tf_op jit(solution)/shard_map/land2/ppermute | solution.py:52
  31.3 3.6 %collective-permute-start.12 = (bf16[16,32,256]{2,1,0:T(8,128)(2,1)}, bf16[16,32,256]{2,1,0:T(8,128)(2,1)S(1)}, u32[]{:S(2)}, u32[]{:S(2)}) collective-permute-start(bf16[16,32,256]{2,1,0:T(8,128)(2,1)} %collective-permute-done.11), channel_id=1, source_target_pairs={{10,8},{11,9},{4,16},{5,17},{22,24},{23,25},{0,2},{1,3},{28,18},{2... | collective-permute-start | bytes 786440 | tf_op jit(solution)/shard_map/land3/ppermute | solution.py:52
  34.9 2.9 %first.1 = (bf16[64,32,256]{2,1,0:T(8,128)(2,1)S(1)}, bf16[96,256]{1,0:T(8,128)(2,1)S(1)}, bf16[96,256]{1,0:T(8,128)(2,1)S(1)}) custom-call(bf16[64,32,256]{2,1,0:T(8,128)(2,1)S(1)} %copy-done, bf16[64,256]{1,0:T(8,128)(2,1)S(1)} %collective-permute-done.refs_1_, bf16[64,256]{1,0:T(8,128)(2,1)S(1)} %collective-permute-done.1.refs_2_, ...), custom_call_target="tpu_custom_call" | custom-call | flops 2415919104 | bytes 1179648 | tf_op jit(solution)/shard_map/first/pallas_call | solution.py:324
  37.8 2.6 %collective-permute-start.13 = (bf16[96,256]{1,0:T(8,128)(2,1)S(1)}, bf16[96,256]{1,0:T(8,128)(2,1)S(1)}, u32[]{:S(2)}, u32[]{:S(2)}) collective-permute-start(bf16[96,256]{1,0:T(8,128)(2,1)S(1)} %get-tuple-element.28), channel_id=1, source_target_pairs={{0,1},{2,3},{4,5},{6,7},{1,0},{3,2},{5,4},{7,6},{8,9},{10,11},{12,... | collective-permute-start | bytes 147464 | tf_op jit(solution)/shard_map/ring_swap/ppermute | solution.py:72
  40.4 0.9 %collective-permute-done.13 = bf16[96,256]{1,0:T(8,128)(2,1)S(1)} collective-permute-done((bf16[96,256]{1,0:T(8,128)(2,1)S(1)}, bf16[96,256]{1,0:T(8,128)(2,1)S(1)}, u32[]{:S(2)}, u32[]{:S(2)}) %collective-permute-start.13) | collective-permute-done | bytes 49184 | tf_op jit(solution)/shard_map/ring_swap/ppermute | solution.py:72
  41.2 3.8 %collective-permute-start.14 = (bf16[192,256]{1,0:T(8,128)(2,1)S(1)}, bf16[192,256]{1,0:T(8,128)(2,1)S(1)}, u32[]{:S(2)}, u32[]{:S(2)}) collective-permute-start(bf16[192,256]{1,0:T(8,128)(2,1)S(1)} %constant_dynamic-update-slice_fusion.kept), channel_id=1, source_target_pairs={{2,8},{3,9},{4,16},{5,17},{6,24},{7,25},{8,2},{9,3},{12,18},{13,19... | collective-permute-start | bytes 294920 | tf_op jit(solution)/shard_map/ring/ppermute | solution.py:52
  45.1 2.5 %collective-permute-done.10.refs_6_ = bf16[16,32,256]{2,1,0:T(8,128)(2,1)S(1)} collective-permute-done((bf16[16,32,256]{2,1,0:T(8,128)(2,1)}, bf16[16,32,256]{2,1,0:T(8,128)(2,1)S(1)}, u32[]{:S(2)}, u32[]{:S(2)}) %collective-permute-start.10) | collective-permute-done | bytes 262176 | tf_op jit(solution)/shard_map/land2/ppermute | solution.py:52
  47.6 1.8 %collective-permute-done.12.refs_7_ = bf16[16,32,256]{2,1,0:T(8,128)(2,1)S(1)} collective-permute-done((bf16[16,32,256]{2,1,0:T(8,128)(2,1)}, bf16[16,32,256]{2,1,0:T(8,128)(2,1)S(1)}, u32[]{:S(2)}, u32[]{:S(2)}) %collective-permute-start.12) | collective-permute-done | bytes 262176 | tf_op jit(solution)/shard_map/land3/ppermute | solution.py:52
  49.4 2.7 %turned.1 = bf16[32,64,256]{2,1,0:T(8,128)(2,1)S(1)} custom-call(bf16[16,32,256]{2,1,0:T(8,128)(2,1)S(1)} %get-tuple-element.23.refs_0_, bf16[16,32,256]{2,1,0:T(8,128)(2,1)S(1)} %get-tuple-element.24.refs_1_, bf16[16,32,256]{2,1,0:T(8,128)(2,1)S(1)} %get-tuple-element.25.refs_2_, bf16[16,32,256]{2,1,0:T(8,128)(2,1)S(1)} %get-tuple-element.26.refs_3_, ...), custom_call_target="tpu_custom_call" | custom-call | flops 2415919104 | bytes 1179648 | tf_op jit(solution)/shard_map/turned/pallas_call | solution.py:324
  52.2 0.9 %mean.1 = (bf16[64,32,256]{2,1,0:T(8,128)(2,1)S(1)}, bf16[64,8,256]{2,1,0:T(8,128)(2,1)S(1)}, bf16[64,8,256]{2,1,0:T(8,128)(2,1)S(1)}) custom-call(bf16[64,32,256]{2,1,0:T(8,128)(2,1)S(1)} %get-tuple-element.22.first, bf16[32,64,256]{2,1,0:T(8,128)(2,1)S(1)} %turned.1, bf16[192,256]{1,0:T(8,128)(2,1)S(1)} %constant_dynamic-update-slice_fusion.kept, ...), custom_call_target="tpu_custom_call" | custom-call | bytes 1179648 | tf_op jit(solution)/shard_map/mean/pallas_call | solution.py:324
  53.1 3.1 %collective-permute-start.15 = (bf16[64,8,256]{2,1,0:T(8,128)(2,1)S(1)}, bf16[64,8,256]{2,1,0:T(8,128)(2,1)S(1)}, u32[]{:S(2)}, u32[]{:S(2)}) collective-permute-start(bf16[64,8,256]{2,1,0:T(8,128)(2,1)S(1)} %get-tuple-element.30), channel_id=1, source_target_pairs={{0,1},{2,3},{4,5},{6,7},{1,0},{3,2},{5,4},{7,6},{8,9},{10,11},{12,... | collective-permute-start | bytes 786440 | tf_op jit(solution)/shard_map/sym_near/ppermute | solution.py:72
  56.2 3.5 %collective-permute-start.16 = (bf16[64,8,256]{2,1,0:T(8,128)(2,1)S(1)}, bf16[64,8,256]{2,1,0:T(8,128)(2,1)S(1)}, u32[]{:S(2)}, u32[]{:S(2)}) collective-permute-start(bf16[64,8,256]{2,1,0:T(8,128)(2,1)S(1)} %get-tuple-element.31), channel_id=1, source_target_pairs={{1,2},{3,4},{5,6},{2,1},{4,3},{6,5},{9,10},{11,12},{13,14},{10,9},... | collective-permute-start | bytes 786440 | tf_op jit(solution)/shard_map/sym_far/ppermute | solution.py:72
  59.7 4.6 %inner_second.1.refs_3_ = bf16[60,32,256]{2,1,0:T(8,128)(2,1)S(1)} custom-call(bf16[64,32,256]{2,1,0:T(8,128)(2,1)S(1)} %get-tuple-element.29.refs_0_.sym, bf16[3,3,256,256]{3,2,1,0:T(8,128)(2,1)S(1)} %copy-done.1), custom_call_target="tpu_custom_call" | custom-call | flops 4529848320 | bytes 1179648 | tf_op jit(solution)/shard_map/inner_second/pallas_call | solution.py:324
  64.4 1.8 %collective-permute-start.17 = (bf16[6,48,256]{2,1,0:T(8,128)(2,1)S(1)}, bf16[6,48,256]{2,1,0:T(8,128)(2,1)S(1)}, u32[]{:S(2)}, u32[]{:S(2)}) collective-permute-start(bf16[6,48,256]{2,1,0:T(8,128)(2,1)S(1)} %pad_maximum_fusion), channel_id=1, source_target_pairs={{0,8},{16,24},{8,0},{24,16},{1,9},{17,25},{9,1},{25,17},{2,10},{18... | collective-permute-start | bytes 442376 | tf_op jit(solution)/shard_map/sym_band_near/ppermute | solution.py:72
  66.2 3.5 %collective-permute-start.18 = (bf16[6,48,256]{2,1,0:T(8,128)(2,1)S(1)}, bf16[6,48,256]{2,1,0:T(8,128)(2,1)S(1)}, u32[]{:S(2)}, u32[]{:S(2)}) collective-permute-start(bf16[6,48,256]{2,1,0:T(8,128)(2,1)S(1)} %pad_maximum_fusion.1), channel_id=1, source_target_pairs={{8,16},{16,8},{9,17},{17,9},{10,18},{18,10},{11,19},{19,11},{12,20... | collective-permute-start | bytes 442376 | tf_op jit(solution)/shard_map/sym_band_far/ppermute | solution.py:72
  69.7 5.2 %middle.1 = (bf16[64,32,256]{2,1,0:T(8,128)(2,1)}, bf16[8,48,256]{2,1,0:T(8,128)(2,1)S(1)}, bf16[8,48,256]{2,1,0:T(8,128)(2,1)S(1)}) custom-call(bf16[64,32,256]{2,1,0:T(8,128)(2,1)S(1)} %get-tuple-element.29.refs_0_.sym, bf16[64,8,256]{2,1,0:T(8,128)(2,1)S(1)} %collective-permute-done.15.refs_1_.near, ...), custom_call_target="tpu_custom_call" | custom-call | flops 4227858432 | bytes 1179648 | tf_op jit(solution)/shard_map/middle/pallas_call | solution.py:324
  75.0 2.7 %edges.1 = bf16[64,32,256]{2,1,0:T(8,128)(2,1)} custom-call(bf16[64,32,256]{2,1,0:T(8,128)(2,1)} %get-tuple-element.32._, bf16[64,32,256]{2,1,0:T(8,128)(2,1)S(1)} %get-tuple-element.29.refs_0_.sym, bf16[64,8,256]{2,1,0:T(8,128)(2,1)S(1)} %collective-permute-done.15.refs_1_.near, ...), custom_call_target="tpu_custom_call", output_to_operand_aliasing={{}: (0, {})} | custom-call | flops 1811939328 | bytes 1179648 | tf_op jit(solution)/shard_map/edges/pallas_call | solution.py:324
  (37 shorter events, 0.4 us)
Async XLA Ops:
  0.0 6.7 %copy-start = (bf16[64,32,256]{2,1,0:T(8,128)(2,1)S(1)}, bf16[64,32,256]{2,1,0:T(8,128)(2,1)}, u32[]{:S(2)}) copy-start(bf16[64,32,256]{2,1,0:T(8,128)(2,1)} %refs_0_.1) | copy-start | bytes 3145732
  1.3 5.6 %collective-permute-start.1 = (bf16[64,256]{1,0:T(8,128)(2,1)S(1)}, bf16[64,256]{1,0:T(8,128)(2,1)S(1)}, u32[]{:S(2)}, u32[]{:S(2)}) collective-permute-start(bf16[64,256]{1,0:T(8,128)(2,1)S(1)} %get-tuple-element.51), channel_id=1, source_target_pairs={{1,2},{3,4},{5,6},{2,1},{4,3},{6,5},{9,10},{11,12},{13,14},{10,9},... | collective-permute-start | bytes 98312 | tf_op jit(solution)/shard_map/own_far/ppermute | solution.py:72
  5.0 1.8 %collective-permute-start = (bf16[64,256]{1,0:T(8,128)(2,1)S(1)}, bf16[64,256]{1,0:T(8,128)(2,1)S(1)}, u32[]{:S(2)}, u32[]{:S(2)}) collective-permute-start(bf16[64,256]{1,0:T(8,128)(2,1)S(1)} %get-tuple-element.52), channel_id=1, source_target_pairs={{0,1},{2,3},{4,5},{6,7},{1,0},{3,2},{5,4},{7,6},{8,9},{10,11},{12,... | collective-permute-start | bytes 98312 | tf_op jit(solution)/shard_map/own_near/ppermute | solution.py:72
  6.2 4.0 %collective-permute-start.4 = (bf16[32,32,256]{2,1,0:T(8,128)(2,1)S(1)}, bf16[32,32,256]{2,1,0:T(8,128)(2,1)}, u32[]{:S(2)}, u32[]{:S(2)}) collective-permute-start(bf16[32,32,256]{2,1,0:T(8,128)(2,1)S(1)} %constant_dynamic-slice_fusion.7), channel_id=1, source_target_pairs={{0,1},{2,3},{4,5},{6,7},{1,0},{3,2},{5,4},{7,6},{8,9},{10,11},{12,... | collective-permute-start | bytes 1572872 | tf_op jit(solution)/shard_map/swap/ppermute | solution.py:72
  6.8 28.1 %copy-start.3 = (bf16[3,3,256,256]{3,2,1,0:T(8,128)(2,1)S(1)}, bf16[3,3,256,256]{3,2,1,0:T(8,128)(2,1)}, u32[]{:S(2)}) copy-start(bf16[3,3,256,256]{3,2,1,0:T(8,128)(2,1)} %refs_8_.1) | copy-start | bytes 3538948
  6.9 5.6 %collective-permute-start.3 = (bf16[34,256]{1,0:T(8,128)(2,1)S(1)}, bf16[34,256]{1,0:T(8,128)(2,1)S(1)}, u32[]{:S(2)}, u32[]{:S(2)}) collective-permute-start(bf16[34,256]{1,0:T(8,128)(2,1)S(1)} %get-tuple-element.55), channel_id=1, source_target_pairs={{8,16},{16,8},{9,17},{17,9},{10,18},{18,10},{11,19},{19,11},{12,20... | collective-permute-start | bytes 52232 | tf_op jit(solution)/shard_map/own_band_far/ppermute | solution.py:72
  10.1 3.0 %collective-permute-start.2 = (bf16[34,256]{1,0:T(8,128)(2,1)S(1)}, bf16[34,256]{1,0:T(8,128)(2,1)S(1)}, u32[]{:S(2)}, u32[]{:S(2)}) collective-permute-start(bf16[34,256]{1,0:T(8,128)(2,1)S(1)} %get-tuple-element.56), channel_id=1, source_target_pairs={{0,8},{16,24},{8,0},{24,16},{1,9},{17,25},{9,1},{25,17},{2,10},{18... | collective-permute-start | bytes 52232 | tf_op jit(solution)/shard_map/own_band_near/ppermute | solution.py:72
  13.1 6.5 %collective-permute-start.5 = (bf16[16,32,256]{2,1,0:T(8,128)(2,1)S(1)}, bf16[16,32,256]{2,1,0:T(8,128)(2,1)}, u32[]{:S(2)}, u32[]{:S(2)}) collective-permute-start(bf16[16,32,256]{2,1,0:T(8,128)(2,1)S(1)} %get-tuple-element.23.refs_0_), channel_id=1, source_target_pairs={{2,10},{3,11},{4,4},{5,5},{6,22},{7,23},{8,0},{9,1},{12,28},{13,29... | collective-permute-start | bytes 786440 | tf_op jit(solution)/shard_map/hop0/ppermute | solution.py:52
  14.4 10.6 %collective-permute-start.7 = (bf16[16,32,256]{2,1,0:T(8,128)(2,1)S(1)}, bf16[16,32,256]{2,1,0:T(8,128)(2,1)}, u32[]{:S(2)}, u32[]{:S(2)}) collective-permute-start(bf16[16,32,256]{2,1,0:T(8,128)(2,1)S(1)} %get-tuple-element.24.refs_1_), channel_id=1, source_target_pairs={{2,2},{3,3},{4,20},{5,21},{6,14},{7,15},{8,8},{9,9},{12,4},{13,5},... | collective-permute-start | bytes 786440 | tf_op jit(solution)/shard_map/hop1/ppermute | solution.py:52
  16.4 13.0 %collective-permute-start.9 = (bf16[16,32,256]{2,1,0:T(8,128)(2,1)S(1)}, bf16[16,32,256]{2,1,0:T(8,128)(2,1)}, u32[]{:S(2)}, u32[]{:S(2)}) collective-permute-start(bf16[16,32,256]{2,1,0:T(8,128)(2,1)S(1)} %get-tuple-element.25.refs_2_), channel_id=1, source_target_pairs={{2,2},{3,3},{4,20},{5,21},{6,14},{7,15},{8,8},{9,9},{12,4},{13,5},... | collective-permute-start | bytes 786440 | tf_op jit(solution)/shard_map/hop2/ppermute | solution.py:52
  18.3 13.0 %collective-permute-start.11 = (bf16[16,32,256]{2,1,0:T(8,128)(2,1)S(1)}, bf16[16,32,256]{2,1,0:T(8,128)(2,1)}, u32[]{:S(2)}, u32[]{:S(2)}) collective-permute-start(bf16[16,32,256]{2,1,0:T(8,128)(2,1)S(1)} %get-tuple-element.26.refs_3_), channel_id=1, source_target_pairs={{2,10},{3,11},{4,4},{5,5},{6,22},{7,23},{8,0},{9,1},{12,28},{13,29... | collective-permute-start | bytes 786440 | tf_op jit(solution)/shard_map/hop3/ppermute | solution.py:52
  19.6 25.4 %collective-permute-start.6 = (bf16[16,32,256]{2,1,0:T(8,128)(2,1)}, bf16[16,32,256]{2,1,0:T(8,128)(2,1)S(1)}, u32[]{:S(2)}, u32[]{:S(2)}) collective-permute-start(bf16[16,32,256]{2,1,0:T(8,128)(2,1)} %collective-permute-done.5), channel_id=1, source_target_pairs={{10,8},{11,9},{4,16},{5,17},{22,24},{23,25},{0,2},{1,3},{28,18},{2... | collective-permute-start | bytes 786440 | tf_op jit(solution)/shard_map/land0/ppermute | solution.py:52
  25.0 20.1 %collective-permute-start.8 = (bf16[16,32,256]{2,1,0:T(8,128)(2,1)}, bf16[16,32,256]{2,1,0:T(8,128)(2,1)S(1)}, u32[]{:S(2)}, u32[]{:S(2)}) collective-permute-start(bf16[16,32,256]{2,1,0:T(8,128)(2,1)} %collective-permute-done.7), channel_id=1, source_target_pairs={{2,8},{3,9},{20,16},{21,17},{14,24},{15,25},{8,2},{9,3},{4,18},{5,... | collective-permute-start | bytes 786440 | tf_op jit(solution)/shard_map/land1/ppermute | solution.py:52
  29.3 18.3 %collective-permute-start.10 = (bf16[16,32,256]{2,1,0:T(8,128)(2,1)}, bf16[16,32,256]{2,1,0:T(8,128)(2,1)S(1)}, u32[]{:S(2)}, u32[]{:S(2)}) collective-permute-start(bf16[16,32,256]{2,1,0:T(8,128)(2,1)} %collective-permute-done.9), channel_id=1, source_target_pairs={{2,8},{3,9},{20,16},{21,17},{14,24},{15,25},{8,2},{9,3},{4,18},{5,... | collective-permute-start | bytes 786440 | tf_op jit(solution)/shard_map/land2/ppermute | solution.py:52
  31.3 18.2 %collective-permute-start.12 = (bf16[16,32,256]{2,1,0:T(8,128)(2,1)}, bf16[16,32,256]{2,1,0:T(8,128)(2,1)S(1)}, u32[]{:S(2)}, u32[]{:S(2)}) collective-permute-start(bf16[16,32,256]{2,1,0:T(8,128)(2,1)} %collective-permute-done.11), channel_id=1, source_target_pairs={{10,8},{11,9},{4,16},{5,17},{22,24},{23,25},{0,2},{1,3},{28,18},{2... | collective-permute-start | bytes 786440 | tf_op jit(solution)/shard_map/land3/ppermute | solution.py:52
  37.8 3.5 %collective-permute-start.13 = (bf16[96,256]{1,0:T(8,128)(2,1)S(1)}, bf16[96,256]{1,0:T(8,128)(2,1)S(1)}, u32[]{:S(2)}, u32[]{:S(2)}) collective-permute-start(bf16[96,256]{1,0:T(8,128)(2,1)S(1)} %get-tuple-element.28), channel_id=1, source_target_pairs={{0,1},{2,3},{4,5},{6,7},{1,0},{3,2},{5,4},{7,6},{8,9},{10,11},{12,... | collective-permute-start | bytes 147464 | tf_op jit(solution)/shard_map/ring_swap/ppermute | solution.py:72
  41.2 10.9 %collective-permute-start.14 = (bf16[192,256]{1,0:T(8,128)(2,1)S(1)}, bf16[192,256]{1,0:T(8,128)(2,1)S(1)}, u32[]{:S(2)}, u32[]{:S(2)}) collective-permute-start(bf16[192,256]{1,0:T(8,128)(2,1)S(1)} %constant_dynamic-update-slice_fusion.kept), channel_id=1, source_target_pairs={{2,8},{3,9},{4,16},{5,17},{6,24},{7,25},{8,2},{9,3},{12,18},{13,19... | collective-permute-start | bytes 294920 | tf_op jit(solution)/shard_map/ring/ppermute | solution.py:52
  52.2 7.5 %copy-start.1 = (bf16[3,3,256,256]{3,2,1,0:T(8,128)(2,1)S(1)}, bf16[3,3,256,256]{3,2,1,0:T(8,128)(2,1)}, u32[]{:S(2)}) copy-start(bf16[3,3,256,256]{3,2,1,0:T(8,128)(2,1)} %w_second.1) | copy-start | bytes 3538948
  53.1 11.2 %collective-permute-start.15 = (bf16[64,8,256]{2,1,0:T(8,128)(2,1)S(1)}, bf16[64,8,256]{2,1,0:T(8,128)(2,1)S(1)}, u32[]{:S(2)}, u32[]{:S(2)}) collective-permute-start(bf16[64,8,256]{2,1,0:T(8,128)(2,1)S(1)} %get-tuple-element.30), channel_id=1, source_target_pairs={{0,1},{2,3},{4,5},{6,7},{1,0},{3,2},{5,4},{7,6},{8,9},{10,11},{12,... | collective-permute-start | bytes 786440 | tf_op jit(solution)/shard_map/sym_near/ppermute | solution.py:72
  56.2 8.1 %collective-permute-start.16 = (bf16[64,8,256]{2,1,0:T(8,128)(2,1)S(1)}, bf16[64,8,256]{2,1,0:T(8,128)(2,1)S(1)}, u32[]{:S(2)}, u32[]{:S(2)}) collective-permute-start(bf16[64,8,256]{2,1,0:T(8,128)(2,1)S(1)} %get-tuple-element.31), channel_id=1, source_target_pairs={{1,2},{3,4},{5,6},{2,1},{4,3},{6,5},{9,10},{11,12},{13,14},{10,9},... | collective-permute-start | bytes 786440 | tf_op jit(solution)/shard_map/sym_far/ppermute | solution.py:72
  64.3 5.5 %copy-start.2 = (bf16[3,3,256,256]{3,2,1,0:T(8,128)(2,1)S(1)}, bf16[3,3,256,256]{3,2,1,0:T(8,128)(2,1)}, u32[]{:S(2)}) copy-start(bf16[3,3,256,256]{3,2,1,0:T(8,128)(2,1)} %w_third.1) | copy-start | bytes 3538948
  64.4 10.5 %collective-permute-start.17 = (bf16[6,48,256]{2,1,0:T(8,128)(2,1)S(1)}, bf16[6,48,256]{2,1,0:T(8,128)(2,1)S(1)}, u32[]{:S(2)}, u32[]{:S(2)}) collective-permute-start(bf16[6,48,256]{2,1,0:T(8,128)(2,1)S(1)} %pad_maximum_fusion), channel_id=1, source_target_pairs={{0,8},{16,24},{8,0},{24,16},{1,9},{17,25},{9,1},{25,17},{2,10},{18... | collective-permute-start | bytes 442376 | tf_op jit(solution)/shard_map/sym_band_near/ppermute | solution.py:72
  66.2 8.8 %collective-permute-start.18 = (bf16[6,48,256]{2,1,0:T(8,128)(2,1)S(1)}, bf16[6,48,256]{2,1,0:T(8,128)(2,1)S(1)}, u32[]{:S(2)}, u32[]{:S(2)}) collective-permute-start(bf16[6,48,256]{2,1,0:T(8,128)(2,1)S(1)} %pad_maximum_fusion.1), channel_id=1, source_target_pairs={{8,16},{16,8},{9,17},{17,9},{10,18},{18,10},{11,19},{19,11},{12,20... | collective-permute-start | bytes 442376 | tf_op jit(solution)/shard_map/sym_band_far/ppermute | solution.py:72

commit v8 on v7

--- a/solution.py
+++ b/solution.py
@@ -156,30 +156,25 @@
         out[at : at + step] = value.astype(BF16).reshape(step, length, channels)
 
 
-def mean_kernel(first, turned, kept, got, out, to_near, to_far, block, ring):
+def mean_kernel(first, turned, kept, got, out, to_near, to_far):
     row, col = lax.axis_index("row"), lax.axis_index("col")
     core = col % 2
-    diagonal = row == col // 2
     size, length, channels = turned.shape
-    count = 3 * size
-    ring[...] = jnp.where(diagonal, kept[...], got[...])
-    block[...] = turned[...]
-    for side in range(2):
-        left = side * size
-        edge = 0 if side == 0 else length - 1
-
-        def put(at, left=left, edge=edge):
-            block[0, left : left + size, :] = ring[at : at + size]
-            block[size - 1, left : left + size, :] = ring[at + size : at + 2 * size]
-            outer = ring[at + 2 * size : at + count]
-            block[:, edge : edge + 1, :] = outer.reshape(size, 1, channels)
-
-        pl.when(core == side)(lambda put=put: put(0))
-        pl.when(core != side)(lambda put=put: put(count))
+    ring = jnp.where(row == col // 2, kept[...], got[...])
+
+    def mean(own, other):
+        return ((own.astype(F32) + other.astype(F32)) * 0.5).astype(BF16)
+
     for side in range(2):
         rows = slice(side * size, (side + 1) * size)
-        other = jnp.swapaxes(block[:, rows, :], 0, 1).astype(F32)
-        out[rows] = ((first[rows].astype(F32) + other) * 0.5).astype(BF16)
+        out[rows] = mean(first[rows], jnp.swapaxes(turned[:, rows, :], 0, 1))
+        parts = [ring[at : at + size] for at in range(0, 6 * size, size)]
+        upper, lower, outer = [jnp.where(core == side, parts[i], parts[i + 3]) for i in range(3)]
+        for x, part in ((0, upper), (size - 1, lower)):
+            place = slice(x, x + 1)
+            out[rows, place, :] = mean(first[rows, place, :], part.reshape(size, 1, channels))
+        edge = 0 if side == 0 else length - 1
+        out[edge] = mean(first[edge], outer)
     start, end = out[:, :STRIP, :], out[:, size - STRIP :, :]
     to_near[...] = jnp.where(core == 0, end, start)
     to_far[...] = jnp.where(core == 0, start, end)
@@ -388,7 +383,7 @@
         mean_kernel,
         (shape(tile_rows, tile_cols), shape(tile_rows, STRIP), shape(tile_rows, STRIP)),
         (first, turned, ring, got_ring),
-        [scratch(tile_cols, tile_rows, channels), scratch(6 * tile_cols, channels)],
+        [],
     )
 
     near = pairwise(to_near, "col", 0, "sym_near")

time: 78.3 us -> 78.6 us (level)
  no operation moved by 1% of the time
where the time goes in v8:
time: 78.6 us; the launch traced here: 78.1 us
  starting transfers between devices  45.7 us (58%)
  Pallas kernels  19.3 us (25%)
  waiting for transfers between devices  8.96 us (11%)
  local copies, waits for them, and re-layouts  3.5 us (4%)
    ppermute x9, starting transfers between devices, chips(): return lax.ppermute(array, AXES, pairs)  23.6 us
    ppermute x10, starting transfers between devices, pairwise(): return lax.ppermute(array, axis, pairs + [(j, i) for i, j in pairs])  22.1 us
    pallas_call x6, Pallas kernels, call(): pl.pallas_call(kernel, out_shape=outs, in_specs=in_specs or whole(len(ins...  19.3 us
    ppermute x9, waiting for transfers between devices, chips(): return lax.ppermute(array, AXES, pairs)  6.23 us
    ppermute x10, waiting for transfers between devices, pairwise(): return lax.ppermute(array, axis, pairs + [(j, i) for i, j in pairs])  2.73 us
  transfers between devices with their start and end apart: 19, of which 6 were waited for; matrix products, arithmetic and copies ran while one was open for 3% of the time, Pallas kernels for 20%

profile of v8, /device:TPU:5, one launch (start us, length us, event | category | flops | bytes accessed | tf_op | source)
XLA Modules:
  0.0 78.1 jit_solution(7069071641199249447)
XLA Ops:
  0.0 1.2 %fusion = (bf16[64,1,256]{2,1,0:T(2,128)(2,1)S(1)}, bf16[64,1,256]{2,1,0:T(2,128)(2,1)S(1)}) fusion(bf16[64,32,256]{2,1,0:T(8,128)(2,1)} %refs_0_.1), kind=kLoop, calls=%fused_computation.25 | loop fusion | bytes 131072 | tf_op jit(solution)/shard_map/slice | solution.py:340
  1.3 3.8 %collective-permute-start.1 = (bf16[64,256]{1,0:T(8,128)(2,1)S(1)}, bf16[64,256]{1,0:T(8,128)(2,1)S(1)}, u32[]{:S(2)}, u32[]{:S(2)}) collective-permute-start(bf16[64,256]{1,0:T(8,128)(2,1)S(1)} %get-tuple-element.51), channel_id=1, source_target_pairs={{1,2},{3,4},{5,6},{2,1},{4,3},{6,5},{9,10},{11,12},{13,14},{10,9},... | collective-permute-start | bytes 98312 | tf_op jit(solution)/shard_map/own_far/ppermute | solution.py:72
  5.1 1.1 %constant_dynamic-slice_fusion.7 = bf16[32,32,256]{2,1,0:T(8,128)(2,1)S(1)} fusion(bf16[64,32,256]{2,1,0:T(8,128)(2,1)} %refs_0_.1, s32[]{:T(128)S(6)} %select_n.97), kind=kLoop, calls=%fused_computation.23 | loop fusion | bytes 1048580 | tf_op jit(solution)/shard_map/dynamic_slice | solution.py:302
  6.2 0.5 collective-permute-start.4
  6.9 3.2 %collective-permute-start.3 = (bf16[34,256]{1,0:T(8,128)(2,1)S(1)}, bf16[34,256]{1,0:T(8,128)(2,1)S(1)}, u32[]{:S(2)}, u32[]{:S(2)}) collective-permute-start(bf16[34,256]{1,0:T(8,128)(2,1)S(1)} %get-tuple-element.55), channel_id=1, source_target_pairs={{8,16},{16,8},{9,17},{17,9},{10,18},{18,10},{11,19},{19,11},{12,20... | collective-permute-start | bytes 52232 | tf_op jit(solution)/shard_map/own_band_far/ppermute | solution.py:72
  10.2 1.1 %fusion.1 = (bf16[16,32,256]{2,1,0:T(8,128)(2,1)S(1)}, bf16[16,32,256]{2,1,0:T(8,128)(2,1)S(1)}) fusion(bf16[32,32,256]{2,1,0:T(8,128)(2,1)} %collective-permute-done.4), kind=kLoop, calls=%fused_computation.26 | loop fusion | bytes 1048576 | tf_op jit(solution)/shard_map/slice | solution.py:337
  11.3 1.2 %collective-permute-done.3.refs_4_ = bf16[34,256]{1,0:T(8,128)(2,1)S(1)} collective-permute-done((bf16[34,256]{1,0:T(8,128)(2,1)S(1)}, bf16[34,256]{1,0:T(8,128)(2,1)S(1)}, u32[]{:S(2)}, u32[]{:S(2)}) %collective-permute-start.3) | collective-permute-done | bytes 17440 | tf_op jit(solution)/shard_map/own_band_far/ppermute | solution.py:72
  12.5 0.6 collective-permute-done.2.refs_3_
  13.1 1.3 %collective-permute-start.5 = (bf16[16,32,256]{2,1,0:T(8,128)(2,1)S(1)}, bf16[16,32,256]{2,1,0:T(8,128)(2,1)}, u32[]{:S(2)}, u32[]{:S(2)}) collective-permute-start(bf16[16,32,256]{2,1,0:T(8,128)(2,1)S(1)} %get-tuple-element.23.refs_0_), channel_id=1, source_target_pairs={{2,10},{3,11},{4,4},{5,5},{6,22},{7,23},{8,0},{9,1},{12,28},{13,29... | collective-permute-start | bytes 786440 | tf_op jit(solution)/shard_map/hop0/ppermute | solution.py:52
  14.4 1.9 %collective-permute-start.7 = (bf16[16,32,256]{2,1,0:T(8,128)(2,1)S(1)}, bf16[16,32,256]{2,1,0:T(8,128)(2,1)}, u32[]{:S(2)}, u32[]{:S(2)}) collective-permute-start(bf16[16,32,256]{2,1,0:T(8,128)(2,1)S(1)} %get-tuple-element.24.refs_1_), channel_id=1, source_target_pairs={{2,2},{3,3},{4,20},{5,21},{6,14},{7,15},{8,8},{9,9},{12,4},{13,5},... | collective-permute-start | bytes 786440 | tf_op jit(solution)/shard_map/hop1/ppermute | solution.py:52
  16.4 1.9 %collective-permute-start.9 = (bf16[16,32,256]{2,1,0:T(8,128)(2,1)S(1)}, bf16[16,32,256]{2,1,0:T(8,128)(2,1)}, u32[]{:S(2)}, u32[]{:S(2)}) collective-permute-start(bf16[16,32,256]{2,1,0:T(8,128)(2,1)S(1)} %get-tuple-element.25.refs_2_), channel_id=1, source_target_pairs={{2,2},{3,3},{4,20},{5,21},{6,14},{7,15},{8,8},{9,9},{12,4},{13,5},... | collective-permute-start | bytes 786440 | tf_op jit(solution)/shard_map/hop2/ppermute | solution.py:52
  18.3 1.4 %collective-permute-start.11 = (bf16[16,32,256]{2,1,0:T(8,128)(2,1)S(1)}, bf16[16,32,256]{2,1,0:T(8,128)(2,1)}, u32[]{:S(2)}, u32[]{:S(2)}) collective-permute-start(bf16[16,32,256]{2,1,0:T(8,128)(2,1)S(1)} %get-tuple-element.26.refs_3_), channel_id=1, source_target_pairs={{2,10},{3,11},{4,4},{5,5},{6,22},{7,23},{8,0},{9,1},{12,28},{13,29... | collective-permute-start | bytes 786440 | tf_op jit(solution)/shard_map/hop3/ppermute | solution.py:52
  19.6 5.3 %collective-permute-start.6 = (bf16[16,32,256]{2,1,0:T(8,128)(2,1)}, bf16[16,32,256]{2,1,0:T(8,128)(2,1)S(1)}, u32[]{:S(2)}, u32[]{:S(2)}) collective-permute-start(bf16[16,32,256]{2,1,0:T(8,128)(2,1)} %collective-permute-done.5), channel_id=1, source_target_pairs={{10,8},{11,9},{4,16},{5,17},{22,24},{23,25},{0,2},{1,3},{28,18},{2... | collective-permute-start | bytes 786440 | tf_op jit(solution)/shard_map/land0/ppermute | solution.py:52
  25.0 2.4 %collective-permute-start.8 = (bf16[16,32,256]{2,1,0:T(8,128)(2,1)}, bf16[16,32,256]{2,1,0:T(8,128)(2,1)S(1)}, u32[]{:S(2)}, u32[]{:S(2)}) collective-permute-start(bf16[16,32,256]{2,1,0:T(8,128)(2,1)} %collective-permute-done.7), channel_id=1, source_target_pairs={{2,8},{3,9},{20,16},{21,17},{14,24},{15,25},{8,2},{9,3},{4,18},{5,... | collective-permute-start | bytes 786440 | tf_op jit(solution)/shard_map/land1/ppermute | solution.py:52
  27.5 1.9 %collective-permute-done.9 = bf16[16,32,256]{2,1,0:T(8,128)(2,1)} collective-permute-done((bf16[16,32,256]{2,1,0:T(8,128)(2,1)S(1)}, bf16[16,32,256]{2,1,0:T(8,128)(2,1)}, u32[]{:S(2)}, u32[]{:S(2)}) %collective-permute-start.9) | collective-permute-done | bytes 262176 | tf_op jit(solution)/shard_map/hop2/ppermute | solution.py:52
  29.3 1.9 %collective-permute-start.10 = (bf16[16,32,256]{2,1,0:T(8,128)(2,1)}, bf16[16,32,256]{2,1,0:T(8,128)(2,1)S(1)}, u32[]{:S(2)}, u32[]{:S(2)}) collective-permute-start(bf16[16,32,256]{2,1,0:T(8,128)(2,1)} %collective-permute-done.9), channel_id=1, source_target_pairs={{2,8},{3,9},{20,16},{21,17},{14,24},{15,25},{8,2},{9,3},{4,18},{5,... | collective-permute-start | bytes 786440 | tf_op jit(solution)/shard_map/land2/ppermute | solution.py:52
  31.3 3.6 %collective-permute-start.12 = (bf16[16,32,256]{2,1,0:T(8,128)(2,1)}, bf16[16,32,256]{2,1,0:T(8,128)(2,1)S(1)}, u32[]{:S(2)}, u32[]{:S(2)}) collective-permute-start(bf16[16,32,256]{2,1,0:T(8,128)(2,1)} %collective-permute-done.11), channel_id=1, source_target_pairs={{10,8},{11,9},{4,16},{5,17},{22,24},{23,25},{0,2},{1,3},{28,18},{2... | collective-permute-start | bytes 786440 | tf_op jit(solution)/shard_map/land3/ppermute | solution.py:52
  34.9 2.9 %first.1 = (bf16[64,32,256]{2,1,0:T(8,128)(2,1)S(1)}, bf16[96,256]{1,0:T(8,128)(2,1)S(1)}, bf16[96,256]{1,0:T(8,128)(2,1)S(1)}) custom-call(bf16[64,32,256]{2,1,0:T(8,128)(2,1)S(1)} %copy-done, bf16[64,256]{1,0:T(8,128)(2,1)S(1)} %collective-permute-done.refs_1_, bf16[64,256]{1,0:T(8,128)(2,1)S(1)} %collective-permute-done.1.refs_2_, ...), custom_call_target="tpu_custom_call" | custom-call | flops 2415919104 | bytes 1179648 | tf_op jit(solution)/shard_map/first/pallas_call | solution.py:319
  37.8 2.6 %collective-permute-start.13 = (bf16[96,256]{1,0:T(8,128)(2,1)S(1)}, bf16[96,256]{1,0:T(8,128)(2,1)S(1)}, u32[]{:S(2)}, u32[]{:S(2)}) collective-permute-start(bf16[96,256]{1,0:T(8,128)(2,1)S(1)} %get-tuple-element.28), channel_id=1, source_target_pairs={{0,1},{2,3},{4,5},{6,7},{1,0},{3,2},{5,4},{7,6},{8,9},{10,11},{12,... | collective-permute-start | bytes 147464 | tf_op jit(solution)/shard_map/ring_swap/ppermute | solution.py:72
  40.4 0.9 %collective-permute-done.13 = bf16[96,256]{1,0:T(8,128)(2,1)S(1)} collective-permute-done((bf16[96,256]{1,0:T(8,128)(2,1)S(1)}, bf16[96,256]{1,0:T(8,128)(2,1)S(1)}, u32[]{:S(2)}, u32[]{:S(2)}) %collective-permute-start.13) | collective-permute-done | bytes 49184 | tf_op jit(solution)/shard_map/ring_swap/ppermute | solution.py:72
  41.2 3.8 %collective-permute-start.14 = (bf16[192,256]{1,0:T(8,128)(2,1)S(1)}, bf16[192,256]{1,0:T(8,128)(2,1)S(1)}, u32[]{:S(2)}, u32[]{:S(2)}) collective-permute-start(bf16[192,256]{1,0:T(8,128)(2,1)S(1)} %constant_dynamic-update-slice_fusion.kept), channel_id=1, source_target_pairs={{2,8},{3,9},{4,16},{5,17},{6,24},{7,25},{8,2},{9,3},{12,18},{13,19... | collective-permute-start | bytes 294920 | tf_op jit(solution)/shard_map/ring/ppermute | solution.py:52
  45.1 2.5 %collective-permute-done.10.refs_6_ = bf16[16,32,256]{2,1,0:T(8,128)(2,1)S(1)} collective-permute-done((bf16[16,32,256]{2,1,0:T(8,128)(2,1)}, bf16[16,32,256]{2,1,0:T(8,128)(2,1)S(1)}, u32[]{:S(2)}, u32[]{:S(2)}) %collective-permute-start.10) | collective-permute-done | bytes 262176 | tf_op jit(solution)/shard_map/land2/ppermute | solution.py:52
  47.6 1.8 %collective-permute-done.12.refs_7_ = bf16[16,32,256]{2,1,0:T(8,128)(2,1)S(1)} collective-permute-done((bf16[16,32,256]{2,1,0:T(8,128)(2,1)}, bf16[16,32,256]{2,1,0:T(8,128)(2,1)S(1)}, u32[]{:S(2)}, u32[]{:S(2)}) %collective-permute-start.12) | collective-permute-done | bytes 262176 | tf_op jit(solution)/shard_map/land3/ppermute | solution.py:52
  49.4 2.7 %turned.1 = bf16[32,64,256]{2,1,0:T(8,128)(2,1)S(1)} custom-call(bf16[16,32,256]{2,1,0:T(8,128)(2,1)S(1)} %get-tuple-element.23.refs_0_, bf16[16,32,256]{2,1,0:T(8,128)(2,1)S(1)} %get-tuple-element.24.refs_1_, bf16[16,32,256]{2,1,0:T(8,128)(2,1)S(1)} %get-tuple-element.25.refs_2_, bf16[16,32,256]{2,1,0:T(8,128)(2,1)S(1)} %get-tuple-element.26.refs_3_, ...), custom_call_target="tpu_custom_call" | custom-call | flops 2415919104 | bytes 1179648 | tf_op jit(solution)/shard_map/turned/pallas_call | solution.py:319
  52.2 1.2 %mean.1 = (bf16[64,32,256]{2,1,0:T(8,128)(2,1)S(1)}, bf16[64,8,256]{2,1,0:T(8,128)(2,1)S(1)}, bf16[64,8,256]{2,1,0:T(8,128)(2,1)S(1)}) custom-call(bf16[64,32,256]{2,1,0:T(8,128)(2,1)S(1)} %get-tuple-element.22.first, bf16[32,64,256]{2,1,0:T(8,128)(2,1)S(1)} %turned.1, bf16[192,256]{1,0:T(8,128)(2,1)S(1)} %constant_dynamic-update-slice_fusion.kept, ...), custom_call_target="tpu_custom_call" | custom-call | bytes 1179648 | tf_op jit(solution)/shard_map/mean/pallas_call | solution.py:319
  53.4 3.1 %collective-permute-start.15 = (bf16[64,8,256]{2,1,0:T(8,128)(2,1)S(1)}, bf16[64,8,256]{2,1,0:T(8,128)(2,1)S(1)}, u32[]{:S(2)}, u32[]{:S(2)}) collective-permute-start(bf16[64,8,256]{2,1,0:T(8,128)(2,1)S(1)} %get-tuple-element.30), channel_id=1, source_target_pairs={{0,1},{2,3},{4,5},{6,7},{1,0},{3,2},{5,4},{7,6},{8,9},{10,11},{12,... | collective-permute-start | bytes 786440 | tf_op jit(solution)/shard_map/sym_near/ppermute | solution.py:72
  56.5 3.5 %collective-permute-start.16 = (bf16[64,8,256]{2,1,0:T(8,128)(2,1)S(1)}, bf16[64,8,256]{2,1,0:T(8,128)(2,1)S(1)}, u32[]{:S(2)}, u32[]{:S(2)}) collective-permute-start(bf16[64,8,256]{2,1,0:T(8,128)(2,1)S(1)} %get-tuple-element.31), channel_id=1, source_target_pairs={{1,2},{3,4},{5,6},{2,1},{4,3},{6,5},{9,10},{11,12},{13,14},{10,9},... | collective-permute-start | bytes 786440 | tf_op jit(solution)/shard_map/sym_far/ppermute | solution.py:72
  60.0 4.6 %inner_second.1.refs_3_ = bf16[60,32,256]{2,1,0:T(8,128)(2,1)S(1)} custom-call(bf16[64,32,256]{2,1,0:T(8,128)(2,1)S(1)} %get-tuple-element.29.refs_0_.sym, bf16[3,3,256,256]{3,2,1,0:T(8,128)(2,1)S(1)} %copy-done.1), custom_call_target="tpu_custom_call" | custom-call | flops 4529848320 | bytes 1179648 | tf_op jit(solution)/shard_map/inner_second/pallas_call | solution.py:319
  64.7 1.8 %collective-permute-start.17 = (bf16[6,48,256]{2,1,0:T(8,128)(2,1)S(1)}, bf16[6,48,256]{2,1,0:T(8,128)(2,1)S(1)}, u32[]{:S(2)}, u32[]{:S(2)}) collective-permute-start(bf16[6,48,256]{2,1,0:T(8,128)(2,1)S(1)} %pad_maximum_fusion), channel_id=1, source_target_pairs={{0,8},{16,24},{8,0},{24,16},{1,9},{17,25},{9,1},{25,17},{2,10},{18... | collective-permute-start | bytes 442376 | tf_op jit(solution)/shard_map/sym_band_near/ppermute | solution.py:72
  66.5 3.5 %collective-permute-start.18 = (bf16[6,48,256]{2,1,0:T(8,128)(2,1)S(1)}, bf16[6,48,256]{2,1,0:T(8,128)(2,1)S(1)}, u32[]{:S(2)}, u32[]{:S(2)}) collective-permute-start(bf16[6,48,256]{2,1,0:T(8,128)(2,1)S(1)} %pad_maximum_fusion.1), channel_id=1, source_target_pairs={{8,16},{16,8},{9,17},{17,9},{10,18},{18,10},{11,19},{19,11},{12,20... | collective-permute-start | bytes 442376 | tf_op jit(solution)/shard_map/sym_band_far/ppermute | solution.py:72
  70.0 5.2 %middle.1 = (bf16[64,32,256]{2,1,0:T(8,128)(2,1)}, bf16[8,48,256]{2,1,0:T(8,128)(2,1)S(1)}, bf16[8,48,256]{2,1,0:T(8,128)(2,1)S(1)}) custom-call(bf16[64,32,256]{2,1,0:T(8,128)(2,1)S(1)} %get-tuple-element.29.refs_0_.sym, bf16[64,8,256]{2,1,0:T(8,128)(2,1)S(1)} %collective-permute-done.15.refs_1_.near, ...), custom_call_target="tpu_custom_call" | custom-call | flops 4227858432 | bytes 1179648 | tf_op jit(solution)/shard_map/middle/pallas_call | solution.py:319
  75.3 2.7 %edges.1 = bf16[64,32,256]{2,1,0:T(8,128)(2,1)} custom-call(bf16[64,32,256]{2,1,0:T(8,128)(2,1)} %get-tuple-element.32._, bf16[64,32,256]{2,1,0:T(8,128)(2,1)S(1)} %get-tuple-element.29.refs_0_.sym, bf16[64,8,256]{2,1,0:T(8,128)(2,1)S(1)} %collective-permute-done.15.refs_1_.near, ...), custom_call_target="tpu_custom_call", output_to_operand_aliasing={{}: (0, {})} | custom-call | flops 1811939328 | bytes 1179648 | tf_op jit(solution)/shard_map/edges/pallas_call | solution.py:319
  (37 shorter events, 0.4 us)
Async XLA Ops:
  0.0 6.7 %copy-start = (bf16[64,32,256]{2,1,0:T(8,128)(2,1)S(1)}, bf16[64,32,256]{2,1,0:T(8,128)(2,1)}, u32[]{:S(2)}) copy-start(bf16[64,32,256]{2,1,0:T(8,128)(2,1)} %refs_0_.1) | copy-start | bytes 3145732
  1.3 5.6 %collective-permute-start.1 = (bf16[64,256]{1,0:T(8,128)(2,1)S(1)}, bf16[64,256]{1,0:T(8,128)(2,1)S(1)}, u32[]{:S(2)}, u32[]{:S(2)}) collective-permute-start(bf16[64,256]{1,0:T(8,128)(2,1)S(1)} %get-tuple-element.51), channel_id=1, source_target_pairs={{1,2},{3,4},{5,6},{2,1},{4,3},{6,5},{9,10},{11,12},{13,14},{10,9},... | collective-permute-start | bytes 98312 | tf_op jit(solution)/shard_map/own_far/ppermute | solution.py:72
  5.0 1.8 %collective-permute-start = (bf16[64,256]{1,0:T(8,128)(2,1)S(1)}, bf16[64,256]{1,0:T(8,128)(2,1)S(1)}, u32[]{:S(2)}, u32[]{:S(2)}) collective-permute-start(bf16[64,256]{1,0:T(8,128)(2,1)S(1)} %get-tuple-element.52), channel_id=1, source_target_pairs={{0,1},{2,3},{4,5},{6,7},{1,0},{3,2},{5,4},{7,6},{8,9},{10,11},{12,... | collective-permute-start | bytes 98312 | tf_op jit(solution)/shard_map/own_near/ppermute | solution.py:72
  6.2 4.0 %collective-permute-start.4 = (bf16[32,32,256]{2,1,0:T(8,128)(2,1)S(1)}, bf16[32,32,256]{2,1,0:T(8,128)(2,1)}, u32[]{:S(2)}, u32[]{:S(2)}) collective-permute-start(bf16[32,32,256]{2,1,0:T(8,128)(2,1)S(1)} %constant_dynamic-slice_fusion.7), channel_id=1, source_target_pairs={{0,1},{2,3},{4,5},{6,7},{1,0},{3,2},{5,4},{7,6},{8,9},{10,11},{12,... | collective-permute-start | bytes 1572872 | tf_op jit(solution)/shard_map/swap/ppermute | solution.py:72
  6.8 28.1 %copy-start.3 = (bf16[3,3,256,256]{3,2,1,0:T(8,128)(2,1)S(1)}, bf16[3,3,256,256]{3,2,1,0:T(8,128)(2,1)}, u32[]{:S(2)}) copy-start(bf16[3,3,256,256]{3,2,1,0:T(8,128)(2,1)} %refs_8_.1) | copy-start | bytes 3538948
  6.9 5.6 %collective-permute-start.3 = (bf16[34,256]{1,0:T(8,128)(2,1)S(1)}, bf16[34,256]{1,0:T(8,128)(2,1)S(1)}, u32[]{:S(2)}, u32[]{:S(2)}) collective-permute-start(bf16[34,256]{1,0:T(8,128)(2,1)S(1)} %get-tuple-element.55), channel_id=1, source_target_pairs={{8,16},{16,8},{9,17},{17,9},{10,18},{18,10},{11,19},{19,11},{12,20... | collective-permute-start | bytes 52232 | tf_op jit(solution)/shard_map/own_band_far/ppermute | solution.py:72
  10.1 3.0 %collective-permute-start.2 = (bf16[34,256]{1,0:T(8,128)(2,1)S(1)}, bf16[34,256]{1,0:T(8,128)(2,1)S(1)}, u32[]{:S(2)}, u32[]{:S(2)}) collective-permute-start(bf16[34,256]{1,0:T(8,128)(2,1)S(1)} %get-tuple-element.56), channel_id=1, source_target_pairs={{0,8},{16,24},{8,0},{24,16},{1,9},{17,25},{9,1},{25,17},{2,10},{18... | collective-permute-start | bytes 52232 | tf_op jit(solution)/shard_map/own_band_near/ppermute | solution.py:72
  13.1 6.5 %collective-permute-start.5 = (bf16[16,32,256]{2,1,0:T(8,128)(2,1)S(1)}, bf16[16,32,256]{2,1,0:T(8,128)(2,1)}, u32[]{:S(2)}, u32[]{:S(2)}) collective-permute-start(bf16[16,32,256]{2,1,0:T(8,128)(2,1)S(1)} %get-tuple-element.23.refs_0_), channel_id=1, source_target_pairs={{2,10},{3,11},{4,4},{5,5},{6,22},{7,23},{8,0},{9,1},{12,28},{13,29... | collective-permute-start | bytes 786440 | tf_op jit(solution)/shard_map/hop0/ppermute | solution.py:52
  14.4 10.6 %collective-permute-start.7 = (bf16[16,32,256]{2,1,0:T(8,128)(2,1)S(1)}, bf16[16,32,256]{2,1,0:T(8,128)(2,1)}, u32[]{:S(2)}, u32[]{:S(2)}) collective-permute-start(bf16[16,32,256]{2,1,0:T(8,128)(2,1)S(1)} %get-tuple-element.24.refs_1_), channel_id=1, source_target_pairs={{2,2},{3,3},{4,20},{5,21},{6,14},{7,15},{8,8},{9,9},{12,4},{13,5},... | collective-permute-start | bytes 786440 | tf_op jit(solution)/shard_map/hop1/ppermute | solution.py:52
  16.4 13.0 %collective-permute-start.9 = (bf16[16,32,256]{2,1,0:T(8,128)(2,1)S(1)}, bf16[16,32,256]{2,1,0:T(8,128)(2,1)}, u32[]{:S(2)}, u32[]{:S(2)}) collective-permute-start(bf16[16,32,256]{2,1,0:T(8,128)(2,1)S(1)} %get-tuple-element.25.refs_2_), channel_id=1, source_target_pairs={{2,2},{3,3},{4,20},{5,21},{6,14},{7,15},{8,8},{9,9},{12,4},{13,5},... | collective-permute-start | bytes 786440 | tf_op jit(solution)/shard_map/hop2/ppermute | solution.py:52
  18.3 13.0 %collective-permute-start.11 = (bf16[16,32,256]{2,1,0:T(8,128)(2,1)S(1)}, bf16[16,32,256]{2,1,0:T(8,128)(2,1)}, u32[]{:S(2)}, u32[]{:S(2)}) collective-permute-start(bf16[16,32,256]{2,1,0:T(8,128)(2,1)S(1)} %get-tuple-element.26.refs_3_), channel_id=1, source_target_pairs={{2,10},{3,11},{4,4},{5,5},{6,22},{7,23},{8,0},{9,1},{12,28},{13,29... | collective-permute-start | bytes 786440 | tf_op jit(solution)/shard_map/hop3/ppermute | solution.py:52
  19.6 25.4 %collective-permute-start.6 = (bf16[16,32,256]{2,1,0:T(8,128)(2,1)}, bf16[16,32,256]{2,1,0:T(8,128)(2,1)S(1)}, u32[]{:S(2)}, u32[]{:S(2)}) collective-permute-start(bf16[16,32,256]{2,1,0:T(8,128)(2,1)} %collective-permute-done.5), channel_id=1, source_target_pairs={{10,8},{11,9},{4,16},{5,17},{22,24},{23,25},{0,2},{1,3},{28,18},{2... | collective-permute-start | bytes 786440 | tf_op jit(solution)/shard_map/land0/ppermute | solution.py:52
  25.0 20.1 %collective-permute-start.8 = (bf16[16,32,256]{2,1,0:T(8,128)(2,1)}, bf16[16,32,256]{2,1,0:T(8,128)(2,1)S(1)}, u32[]{:S(2)}, u32[]{:S(2)}) collective-permute-start(bf16[16,32,256]{2,1,0:T(8,128)(2,1)} %collective-permute-done.7), channel_id=1, source_target_pairs={{2,8},{3,9},{20,16},{21,17},{14,24},{15,25},{8,2},{9,3},{4,18},{5,... | collective-permute-start | bytes 786440 | tf_op jit(solution)/shard_map/land1/ppermute | solution.py:52
  29.3 18.3 %collective-permute-start.10 = (bf16[16,32,256]{2,1,0:T(8,128)(2,1)}, bf16[16,32,256]{2,1,0:T(8,128)(2,1)S(1)}, u32[]{:S(2)}, u32[]{:S(2)}) collective-permute-start(bf16[16,32,256]{2,1,0:T(8,128)(2,1)} %collective-permute-done.9), channel_id=1, source_target_pairs={{2,8},{3,9},{20,16},{21,17},{14,24},{15,25},{8,2},{9,3},{4,18},{5,... | collective-permute-start | bytes 786440 | tf_op jit(solution)/shard_map/land2/ppermute | solution.py:52
  31.3 18.2 %collective-permute-start.12 = (bf16[16,32,256]{2,1,0:T(8,128)(2,1)}, bf16[16,32,256]{2,1,0:T(8,128)(2,1)S(1)}, u32[]{:S(2)}, u32[]{:S(2)}) collective-permute-start(bf16[16,32,256]{2,1,0:T(8,128)(2,1)} %collective-permute-done.11), channel_id=1, source_target_pairs={{10,8},{11,9},{4,16},{5,17},{22,24},{23,25},{0,2},{1,3},{28,18},{2... | collective-permute-start | bytes 786440 | tf_op jit(solution)/shard_map/land3/ppermute | solution.py:52
  37.8 3.5 %collective-permute-start.13 = (bf16[96,256]{1,0:T(8,128)(2,1)S(1)}, bf16[96,256]{1,0:T(8,128)(2,1)S(1)}, u32[]{:S(2)}, u32[]{:S(2)}) collective-permute-start(bf16[96,256]{1,0:T(8,128)(2,1)S(1)} %get-tuple-element.28), channel_id=1, source_target_pairs={{0,1},{2,3},{4,5},{6,7},{1,0},{3,2},{5,4},{7,6},{8,9},{10,11},{12,... | collective-permute-start | bytes 147464 | tf_op jit(solution)/shard_map/ring_swap/ppermute | solution.py:72
  41.2 10.9 %collective-permute-start.14 = (bf16[192,256]{1,0:T(8,128)(2,1)S(1)}, bf16[192,256]{1,0:T(8,128)(2,1)S(1)}, u32[]{:S(2)}, u32[]{:S(2)}) collective-permute-start(bf16[192,256]{1,0:T(8,128)(2,1)S(1)} %constant_dynamic-update-slice_fusion.kept), channel_id=1, source_target_pairs={{2,8},{3,9},{4,16},{5,17},{6,24},{7,25},{8,2},{9,3},{12,18},{13,19... | collective-permute-start | bytes 294920 | tf_op jit(solution)/shard_map/ring/ppermute | solution.py:52
  52.2 7.8 %copy-start.1 = (bf16[3,3,256,256]{3,2,1,0:T(8,128)(2,1)S(1)}, bf16[3,3,256,256]{3,2,1,0:T(8,128)(2,1)}, u32[]{:S(2)}) copy-start(bf16[3,3,256,256]{3,2,1,0:T(8,128)(2,1)} %w_second.1) | copy-start | bytes 3538948
  53.4 11.2 %collective-permute-start.15 = (bf16[64,8,256]{2,1,0:T(8,128)(2,1)S(1)}, bf16[64,8,256]{2,1,0:T(8,128)(2,1)S(1)}, u32[]{:S(2)}, u32[]{:S(2)}) collective-permute-start(bf16[64,8,256]{2,1,0:T(8,128)(2,1)S(1)} %get-tuple-element.30), channel_id=1, source_target_pairs={{0,1},{2,3},{4,5},{6,7},{1,0},{3,2},{5,4},{7,6},{8,9},{10,11},{12,... | collective-permute-start | bytes 786440 | tf_op jit(solution)/shard_map/sym_near/ppermute | solution.py:72
  56.5 8.1 %collective-permute-start.16 = (bf16[64,8,256]{2,1,0:T(8,128)(2,1)S(1)}, bf16[64,8,256]{2,1,0:T(8,128)(2,1)S(1)}, u32[]{:S(2)}, u32[]{:S(2)}) collective-permute-start(bf16[64,8,256]{2,1,0:T(8,128)(2,1)S(1)} %get-tuple-element.31), channel_id=1, source_target_pairs={{1,2},{3,4},{5,6},{2,1},{4,3},{6,5},{9,10},{11,12},{13,14},{10,9},... | collective-permute-start | bytes 786440 | tf_op jit(solution)/shard_map/sym_far/ppermute | solution.py:72
  64.5 5.5 %copy-start.2 = (bf16[3,3,256,256]{3,2,1,0:T(8,128)(2,1)S(1)}, bf16[3,3,256,256]{3,2,1,0:T(8,128)(2,1)}, u32[]{:S(2)}) copy-start(bf16[3,3,256,256]{3,2,1,0:T(8,128)(2,1)} %w_third.1) | copy-start | bytes 3538948
  64.7 10.6 %collective-permute-start.17 = (bf16[6,48,256]{2,1,0:T(8,128)(2,1)S(1)}, bf16[6,48,256]{2,1,0:T(8,128)(2,1)S(1)}, u32[]{:S(2)}, u32[]{:S(2)}) collective-permute-start(bf16[6,48,256]{2,1,0:T(8,128)(2,1)S(1)} %pad_maximum_fusion), channel_id=1, source_target_pairs={{0,8},{16,24},{8,0},{24,16},{1,9},{17,25},{9,1},{25,17},{2,10},{18... | collective-permute-start | bytes 442376 | tf_op jit(solution)/shard_map/sym_band_near/ppermute | solution.py:72
  66.5 8.8 %collective-permute-start.18 = (bf16[6,48,256]{2,1,0:T(8,128)(2,1)S(1)}, bf16[6,48,256]{2,1,0:T(8,128)(2,1)S(1)}, u32[]{:S(2)}, u32[]{:S(2)}) collective-permute-start(bf16[6,48,256]{2,1,0:T(8,128)(2,1)S(1)} %pad_maximum_fusion.1), channel_id=1, source_target_pairs={{8,16},{16,8},{9,17},{17,9},{10,18},{18,10},{11,19},{19,11},{12,20... | collective-permute-start | bytes 442376 | tf_op jit(solution)/shard_map/sym_band_far/ppermute | solution.py:72
